TPU v7x, 32 devices: a whole 2x2x4 slice. The times are simulated.
32 devices in a mesh: dev: 32 (over z, y, x, core).
Axes of the slice: x: 2, y: 2, z: 4, core: 2. Of those that a mesh axis runs over, the one named last changes fastest.
Arguments:
- gaussians: float32 [59, 262144], P(None, 'dev'), may hold values from -6 to 3
- view_angles: float32 [3], replicated, may hold values from -4 to 4
- tile_order: int32 [512], P('dev'), may hold values from 0 to 511, as said below
- tile_owners: int32 [512, 512], P('dev'), may hold values from 0 to 31, as said below
- tile_locals: int32 [512, 512], P('dev'), may hold values from 0 to 8191
- list_counts: int32 [512], P('dev'), may hold values from 1 to 512, as said below
- image_cotangent: float32 [3, 131072], P(None, 'dev'), may hold values from -6 to 6
Outputs:
- rendered: float32 [3, 131072], P(None, 'dev')
- gradients: float32 [59, 262144], P(None, 'dev')
Inputs may be any that keep to these rules, and one draw needn't show every extreme that they name: `tile_order`: each image tile once. `tile_owners`: the 16 x 512 slots of the tiles of one device name every owner exactly 256 times. Slots from list_counts[i] on are padding.
All inputs are finite; a program needn't handle non-finite values.
Results may differ from a plain program's by a relative error of at most 0.0003.
Values sent between devices are 32-bit elements; how exact they have to be, the bound alone decides.
No kernel may reach another device: no remote copies, remote signals or barrier semaphores. Data moves between devices by JAX's collectives and lax.ppermute only.
A program may use at most 64 MiB of HBM per device.

v0:
```python
from functools import partial

import jax
import jax.numpy as jnp
from jax import lax
from jax.sharding import PartitionSpec as P

PIX = 256
TX = 32
SLOTS = 512
BLOCK = 256


highest = lax.Precision.HIGHEST


def rotation_of(view_angles):
    cos_a = jnp.cos(view_angles[0])
    sin_a = jnp.sin(view_angles[0])
    cos_b = jnp.cos(view_angles[1])
    sin_b = jnp.sin(view_angles[1])
    cos_c = jnp.cos(view_angles[2])
    sin_c = jnp.sin(view_angles[2])
    zero_val = jnp.zeros((), jnp.float32)
    one_val = jnp.ones((), jnp.float32)
    turn_x = jnp.stack(
        [
            jnp.stack([one_val, zero_val, zero_val]),
            jnp.stack([zero_val, cos_a, -sin_a]),
            jnp.stack([zero_val, sin_a, cos_a]),
        ]
    )
    turn_y = jnp.stack(
        [
            jnp.stack([cos_b, zero_val, sin_b]),
            jnp.stack([zero_val, one_val, zero_val]),
            jnp.stack([-sin_b, zero_val, cos_b]),
        ]
    )
    turn_z = jnp.stack(
        [
            jnp.stack([cos_c, -sin_c, zero_val]),
            jnp.stack([sin_c, cos_c, zero_val]),
            jnp.stack([zero_val, zero_val, one_val]),
        ]
    )
    return jnp.dot(turn_z, jnp.dot(turn_y, turn_x, precision=highest), precision=highest)


def harmonics(along_x, along_y, along_z):
    sq_x = along_x * along_x
    sq_y = along_y * along_y
    sq_z = along_z * along_z
    return jnp.stack(
        [
            0.28209479177387814 + 0.0 * along_x,
            -0.4886025119029199 * along_y,
            0.4886025119029199 * along_z,
            -0.4886025119029199 * along_x,
            1.0925484305920792 * along_x * along_y,
            -1.0925484305920792 * along_y * along_z,
            0.31539156525252005 * (2.0 * sq_z - sq_x - sq_y),
            -1.0925484305920792 * along_x * along_z,
            0.5462742152960396 * (sq_x - sq_y),
            -0.5900435899266435 * along_y * (3.0 * sq_x - sq_y),
            2.890611442640554 * along_x * along_y * along_z,
            -0.4570457994644658 * along_y * (4.0 * sq_z - sq_x - sq_y),
            0.3731763325901154 * along_z * (2.0 * sq_z - 3.0 * sq_x - 3.0 * sq_y),
            -0.4570457994644658 * along_x * (4.0 * sq_z - sq_x - sq_y),
            1.445305721320277 * along_z * (sq_x - sq_y),
            -0.5900435899266435 * along_x * (sq_x - 3.0 * sq_y),
        ]
    )


def project(columns, view_angles, camera_frame):
    focal_x, focal_y, centre_x, centre_y = camera_frame
    rotation = rotation_of(view_angles)
    positions = columns[0:3]
    cam_first = (
        rotation[0, 0] * positions[0]
        + rotation[0, 1] * positions[1]
        + rotation[0, 2] * positions[2]
    )
    cam_second = (
        rotation[1, 0] * positions[0]
        + rotation[1, 1] * positions[1]
        + rotation[1, 2] * positions[2]
    )
    mean_x = centre_x + focal_x * cam_first
    mean_y = centre_y + focal_y * cam_second
    scales = jnp.exp(columns[3:6])
    quat_w = columns[6]
    quat_x = columns[7]
    quat_y = columns[8]
    quat_z = columns[9]
    norm_sq = jnp.maximum(
        quat_w * quat_w + quat_x * quat_x + quat_y * quat_y + quat_z * quat_z, 1.0
    )
    turned = [
        [
            1.0 - 2.0 * (quat_y * quat_y + quat_z * quat_z) / norm_sq,
            2.0 * (quat_x * quat_y - quat_w * quat_z) / norm_sq,
            2.0 * (quat_x * quat_z + quat_w * quat_y) / norm_sq,
        ],
        [
            2.0 * (quat_x * quat_y + quat_w * quat_z) / norm_sq,
            1.0 - 2.0 * (quat_x * quat_x + quat_z * quat_z) / norm_sq,
            2.0 * (quat_y * quat_z - quat_w * quat_x) / norm_sq,
        ],
        [
            2.0 * (quat_x * quat_z - quat_w * quat_y) / norm_sq,
            2.0 * (quat_y * quat_z + quat_w * quat_x) / norm_sq,
            1.0 - 2.0 * (quat_x * quat_x + quat_y * quat_y) / norm_sq,
        ],
    ]
    first_row = []
    second_row = []
    for column_index in range(3):
        first_row.append(
            focal_x
            * (
                rotation[0, 0] * turned[0][column_index]
                + rotation[0, 1] * turned[1][column_index]
                + rotation[0, 2] * turned[2][column_index]
            )
            * scales[column_index]
        )
        second_row.append(
            focal_y
            * (
                rotation[1, 0] * turned[0][column_index]
                + rotation[1, 1] * turned[1][column_index]
                + rotation[1, 2] * turned[2][column_index]
            )
            * scales[column_index]
        )
    cov_a = (
        first_row[0] * first_row[0]
        + first_row[1] * first_row[1]
        + first_row[2] * first_row[2]
        + 0.3
    )
    cov_b = (
        first_row[0] * second_row[0] + first_row[1] * second_row[1] + first_row[2] * second_row[2]
    )
    cov_c = (
        second_row[0] * second_row[0]
        + second_row[1] * second_row[1]
        + second_row[2] * second_row[2]
        + 0.3
    )
    determinant = cov_a * cov_c - cov_b * cov_b
    opacity = 1.0 / (1.0 + jnp.exp(-columns[10]))
    basis = harmonics(rotation[2, 0], rotation[2, 1], rotation[2, 2])
    coeffs = columns[11:59].reshape(3, 16, columns.shape[1])
    colours = 0.5 + jnp.einsum("k,ckn->cn", basis, coeffs, precision=highest)
    return jnp.stack(
        [
            mean_x,
            mean_y,
            cov_c / determinant,
            -cov_b / determinant,
            cov_a / determinant,
            opacity,
            colours[0],
            colours[1],
            colours[2],
        ]
    )


def render_tile(tile_rows, live_count, tile_id):
    pixels = jnp.arange(PIX, dtype=jnp.int32)
    pixel_x = (tile_id % TX * 16 + pixels % 16).astype(jnp.float32) + 0.5
    pixel_y = (tile_id // TX * 16 + pixels // 16).astype(jnp.float32) + 0.5
    before = (jnp.arange(BLOCK)[:, None] < jnp.arange(BLOCK)[None, :]).astype(jnp.float32)

    def one_block(start, state):
        log_carry, tile_image = state
        segment = tile_rows[:, start : start + BLOCK]
        offset_x = pixel_x[:, None] - segment[0][None, :]
        offset_y = pixel_y[:, None] - segment[1][None, :]
        powers = (
            -0.5
            * (
                segment[2][None, :] * offset_x * offset_x
                + segment[4][None, :] * offset_y * offset_y
            )
            - segment[3][None, :] * offset_x * offset_y
        )
        slot_live = start + jnp.arange(BLOCK, dtype=jnp.int32) < live_count
        alphas = jnp.where(slot_live[None, :], segment[5][None, :] * jnp.exp(powers), 0.0)
        logs = jnp.log1p(-alphas)
        summed = log_carry[:, None] + jnp.dot(logs, before, precision=highest)
        weights = jnp.exp(summed) * alphas
        added = jnp.einsum("ck,pk->cp", segment[6:9], weights, precision=highest)
        return (log_carry + jnp.sum(logs, axis=1), tile_image + added)

    state = (jnp.zeros((PIX,), jnp.float32), jnp.zeros((3, PIX), jnp.float32))
    for block_index in range(SLOTS // BLOCK):
        start = block_index * BLOCK
        step_block = partial(one_block, start)
        if block_index == 0:
            state = step_block(state)
        else:
            state = step_block(state)
    return state[1]


def shards(
    gaussians, view_angles, tile_order, tile_owners, tile_locals, list_counts, image_cotangent
):
    devices = lax.axis_size("dev")
    tile_count = tile_order.shape[0]
    tiles_y = devices * tile_count // TX
    camera_frame = (4.0 * TX, 4.0 * tiles_y, 8.0 * TX, 8.0 * tiles_y)
    owner_flat = tile_owners.reshape(-1)
    local_flat = tile_locals.reshape(-1)
    slot_total = owner_flat.shape[0]
    per_owner = slot_total // devices
    grouping = jnp.argsort(owner_flat, stable=True)
    inverse = (
        jnp.zeros((slot_total,), jnp.int32)
        .at[grouping]
        .set(jnp.arange(slot_total, dtype=jnp.int32))
    )
    wanted = jnp.take(local_flat, grouping).reshape(devices, per_owner)

    def shade_tile(columns, live_count, tile_id):
        return render_tile(project(columns, view_angles, camera_frame), live_count, tile_id)

    asked = lax.all_to_all(wanted, "dev", split_axis=0, concat_axis=0, tiled=True)
    picked = jnp.take(gaussians, asked.reshape(-1), axis=0 + 1).reshape(
        gaussians.shape[0], asked.shape[0], asked.shape[1]
    )
    arrived = lax.all_to_all(picked, "dev", split_axis=1, concat_axis=1, tiled=True)
    asked_ids = asked[None]
    row_width = arrived.shape[0]
    slot_rows = jnp.take(arrived.reshape(row_width, slot_total), inverse, axis=1)
    tile_rows = slot_rows.reshape(row_width, tile_count, SLOTS).transpose(1, 0, 2)
    cotangents = image_cotangent.reshape(3, tile_count, PIX).transpose(1, 0, 2)

    def one_tile(tile_item):
        columns, live_count, tile_id, tile_cot = tile_item
        tile_image, pullback = jax.vjp(
            lambda values: shade_tile(values, live_count, tile_id), columns
        )
        return (tile_image, pullback(tile_cot)[0])

    images, slot_grads = lax.map(one_tile, (tile_rows, list_counts, tile_order, cotangents))
    rendered = images.transpose(1, 0, 2).reshape(3, tile_count * PIX)
    grouped = jnp.take(
        slot_grads.transpose(1, 0, 2).reshape(row_width, slot_total), grouping, axis=1
    )
    received = asked_ids.reshape(slot_total)
    terms = lax.all_to_all(grouped, "dev", split_axis=1, concat_axis=1, tiled=True)
    gradients = jnp.zeros_like(gaussians).at[:, received].add(terms)
    return (rendered, gradients)


def solution(mesh):
    return jax.shard_map(
        shards,
        mesh=mesh,
        in_specs=(
            P(None, "dev"),
            P(),
            P("dev"),
            P("dev", None),
            P("dev", None),
            P("dev"),
            P(None, "dev"),
        ),
        out_specs=(P(None, "dev"), P(None, "dev")),
        check_vma=False,
    )
```

profile of v0, /device:TPU:0, one launch (start us, length us, event | category | flops | bytes accessed | tf_op | source)
XLA Modules:
  0.0 745.2 jit_solution(13782579080511799023)
XLA Ops:
  1.4 6.8 sort.17
  9.0 45.5 %gather_fusion = s32[8192]{0:T(1024)S(1)} fusion(s32[8192]{0:T(1024)S(1)} %bitcast.293, s32[8192]{0:T(1024)S(1)} %get-tuple-element.585), kind=kCustom, calls=%fused_computation.3 | custom fusion | bytes 98304 | tf_op jit(solution)/shard_map/jit(_take)/gather | solution.py:228
  55.2 7.3 all-to-all-start
  62.5 2.8 copy.27
  65.2 4.5 all-to-all-done
  69.7 29.9 %gather_fusion.1 = f32[8192,59]{1,0:T(8,128)} fusion(f32[59,8192]{0,1:T(8,128)} %copy.27, s32[8192]{0:T(1024)S(1)} %fusion.144), kind=kCustom, calls=%fused_computation.clone | custom fusion | bytes 3899392 | tf_op jit(solution)/shard_map/jit(_take)/gather | solution.py:234
  99.7 7.5 broadcast_select_fusion.2
  107.1 3.9 copy.28
  111.1 2.7 all-to-all-start.1
  140.4 30.7 %scatter_custom_fusion = s32[8192]{0:T(1024)S(1)} fusion(s32[8192]{0:T(1024)S(1)} %get-tuple-element.584, s32[8192]{0:T(1024)S(1)} %iota.61, s32[]{:T(128)} %constant.284.clone.1), kind=kCustom, calls=%fused_computation.308 | custom fusion | bytes 32772 | tf_op jit(solution)/shard_map/scatter | solution.py:226
  171.2 2.8 copy.29
  173.9 29.9 %gather_fusion.2 = f32[8192,59]{1,0:T(8,128)} fusion(f32[59,8192]{0,1:T(8,128)} %bitcast.294, s32[8192]{0:T(1024)S(1)} %fusion.145), kind=kCustom, calls=%fused_computation.1.clone | custom fusion | bytes 3899392 | tf_op jit(solution)/shard_map/jit(_take)/gather | solution.py:240
  203.9 7.5 broadcast_select_fusion.1
  211.3 2.9 copy.30
  214.3 375.3 %while.15 = (s32[]{:T(128)}, f32[16,3,256]{2,1,0:T(4,128)S(1)}, f32[16,59,512]{2,1,0:T(8,128)}, f32[16,59,512]{2,1,0:T(8,128)S(1)}, f32[16]{0:T(128)S(1)}, /*ind...) while((s32[]{:T(128)}, f32[16,3,256]{2,1,0:T(4,128)S(1)}, ...), condition=%wide.region_17.19_spmd, body=%wide.region_2.18_spmd.sunk | while | flops 835476480 | bytes 4493020 | solution.py:251
  215.1 3.8 fusion.262
  221.8 3.8 add_bitcast_fusion.3
  232.4 1.1 fusion.275
  238.5 3.8 fusion.262
  245.2 3.8 add_bitcast_fusion.3
  255.9 1.1 fusion.275
  262.0 3.8 fusion.262
  268.7 3.8 add_bitcast_fusion.3
  285.4 3.8 fusion.262
  292.2 3.8 add_bitcast_fusion.3
  299.2 1.1 fusion.276
  308.9 3.8 fusion.262
  315.6 3.8 add_bitcast_fusion.3
  326.2 1.1 fusion.275
  332.4 3.8 fusion.262
  339.1 3.8 add_bitcast_fusion.3
  349.7 1.1 fusion.275
  355.8 3.8 fusion.262
  362.5 3.8 add_bitcast_fusion.3
  379.3 3.8 fusion.262
  386.0 3.8 add_bitcast_fusion.3
  393.0 1.1 fusion.276
  402.7 3.8 fusion.262
  409.5 3.8 add_bitcast_fusion.3
  426.2 3.8 fusion.262
  432.9 3.8 add_bitcast_fusion.3
  449.7 3.8 fusion.262
  456.4 3.8 add_bitcast_fusion.3
  473.1 3.8 fusion.262
  479.8 3.8 add_bitcast_fusion.3
  496.6 3.8 fusion.262
  503.3 3.8 add_bitcast_fusion.3
  520.0 3.8 fusion.262
  526.8 3.8 add_bitcast_fusion.3
  543.5 3.8 fusion.262
  550.2 3.8 add_bitcast_fusion.3
  567.0 3.8 fusion.262
  573.7 3.8 add_bitcast_fusion.3
  589.7 3.9 copy.32
  593.5 29.9 %gather_fusion.3 = f32[8192,59]{1,0:T(8,128)} fusion(f32[59,8192]{0,1:T(8,128)} %bitcast.295, s32[8192]{0:T(1024)S(1)} %get-tuple-element.585), kind=kCustom, calls=%fused_computation.2.clone | custom fusion | bytes 3899392 | tf_op jit(solution)/shard_map/jit(_take)/gather | solution.py:253
  623.4 7.5 %broadcast_select_fusion = f32[8192,59]{1,0:T(8,128)} fusion(f32[8192,59]{1,0:T(8,128)} %gather_fusion.3, pred[8192]{0:T(1024)(128)(4,1)S(1)} %get-tuple-element.530), kind=kLoop, calls=%fused_computation.292 | loop fusion | flops 483328 | bytes 3874816 | tf_op jit(solution)/shard_map/jit(_take)/select_n | solution.py:253
  630.9 3.8 copy.33
  634.7 6.1 all-to-all-start.2
  640.8 48.7 %all-to-all-done.2 = f32[59,32,256]{2,0,1:T(8,128)S(1)} async-done(((f32[59,32,256]{2,0,1:T(8,128)}), f32[59,32,256]{2,0,1:T(8,128)S(1)}, u32[]{:S(2)}, u32[]{:S(2)}) %all-to-all-start.2) | async-done | bytes 1933344 | tf_op jit(solution)/shard_map/all_to_all | solution.py:257
  689.5 1.1 copy.34
  691.0 1.2 copy.40
  692.2 2.8 copy.35
  694.9 46.5 %scatter_custom_fusion.1 = f32[59,8192]{0,1:T(8,128)} fusion(s32[8192]{0:T(1024)S(1)} %bitcast.315, f32[8192,59]{1,0:T(8,128)} %copy.35, f32[]{:T(128)} %constant.285.clone.1), kind=kCustom, calls=%fused_computation.295 | custom fusion | flops 483328 | bytes 1933824 | tf_op jit(solution)/shard_map/scatter-add | solution.py:258
  741.4 3.8 copy.36
  (897 shorter events, 210.7 us)
Async XLA Ops:
  9.0 53.5 %copy-start = (f32[59,8192]{1,0:T(8,128)S(1)}, f32[59,8192]{1,0:T(8,128)}, u32[]{:S(2)}) copy-start(f32[59,8192]{1,0:T(8,128)} %param.11) | copy-start | bytes 5799940
  55.2 14.6 %all-to-all-start = ((s32[32,1,256]{2,1,0:T(1,128)}), s32[32,1,256]{2,1,0:T(1,128)S(1)}, u32[]{:S(2)}, u32[]{:S(2)}) async-start(s32[32,1,256]{2,1,0:T(1,128)} %bitcast.51), calls=%async_computation | async-start | bytes 65536 | tf_op jit(solution)/shard_map/all_to_all | solution.py:233
  107.1 6.7 copy-start.1
  107.1 11.8 %copy-start.6 = (f32[1,3]{1,0:T(1,128)S(1)}, f32[1,3]{1,0:T(1,128)}, u32[]{:S(2)}) copy-start(f32[1,3]{1,0:T(1,128)} %constant.291.clone.1) | copy-start | bytes 40
  107.1 11.8 %copy-start.7 = (f32[1,3]{1,0:T(1,128)S(1)}, f32[1,3]{1,0:T(1,128)}, u32[]{:S(2)}) copy-start(f32[1,3]{1,0:T(1,128)} %constant.292.clone.1) | copy-start | bytes 40
  107.1 11.9 %copy-start.2 = (f32[1,3]{1,0:T(1,128)S(1)}, f32[1,3]{1,0:T(1,128)}, u32[]{:S(2)}) copy-start(f32[1,3]{1,0:T(1,128)} %constant.290.clone.1) | copy-start | bytes 40
  111.1 60.1 %all-to-all-start.1 = ((f32[59,32,256]{2,0,1:T(8,128)}), f32[59,32,256]{2,0,1:T(8,128)S(1)}, u32[]{:S(2)}, u32[]{:S(2)}) async-start(f32[59,32,256]{2,0,1:T(8,128)} %copy.28), calls=%async_computation.1 | async-start | bytes 4194304 | tf_op jit(solution)/shard_map/all_to_all | solution.py:237
  211.3 2.9 copy-start.3
  211.3 3.0 copy-start.4
  589.6 33.8 %copy-start.5 = (f32[16,3,256]{2,1,0:T(4,128)}, f32[16,3,256]{2,1,0:T(4,128)S(1)}, u32[]{:S(2)}) copy-start(f32[16,3,256]{2,1,0:T(4,128)S(1)} %get-tuple-element.419) | copy-start | bytes 147460
  634.7 54.8 %all-to-all-start.2 = ((f32[59,32,256]{2,0,1:T(8,128)}), f32[59,32,256]{2,0,1:T(8,128)S(1)}, u32[]{:S(2)}, u32[]{:S(2)}) async-start(f32[59,32,256]{2,0,1:T(8,128)} %copy.33), calls=%async_computation.2 | async-start | bytes 4194304 | tf_op jit(solution)/shard_map/all_to_all | solution.py:257
where the time goes:
time: 751 us; the launch traced here: 745 us
  other arithmetic  248 us (33%)
  local copies, waits for them, and re-layouts  230 us (31%)
  matrix products  131 us (17%)
  waiting for transfers between devices  53.2 us (7%)
  loops' own time  41.8 us (6%)
  between operations  25.6 us (3%)
  starting transfers between devices  16.1 us (2%)
    dot_general x96, matrix products, one_block(): added = jnp.einsum('ck,pk->cp', segment[6:9], weights, precision=highest)  85.6 us
    div x16, other arithmetic, project(): cov_c / determinant  60.5 us
    add x16, other arithmetic, project(): mean_x = centre_x + focal_x * cam_first  60.1 us
    all_to_all x1, waiting for transfers between devices, shards(): lax.all_to_all(grouped, 'dev', split_axis=1, concat_axis=1, tiled=True)  48.7 us
    scatter-add x1, other arithmetic, shards(): gradients = jnp.zeros_like(gaussians).at[:, received].add(terms)  46.5 us
    gather x1, local copies, waits for them, and re-layouts, shards(): wanted = jnp.take(local_flat, grouping).reshape(devices, per_owner)  45.5 us
    dot_general x64, matrix products, one_block(): summed = log_carry[:, None] + jnp.dot(logs, before, precision=highest)  42.2 us
    another operation x1, loops' own time, shards(): lax.map(one_tile, (tile_rows, list_counts, tile_order, cotangents))  41.8 us
  transfers between devices with their start and end apart: 3, of which 2 were waited for; matrix products, arithmetic and copies ran while one was open for 5% of the time, Pallas kernels for 0%

commit v1 on v0

v1 whole, which is shorter than its diff:
```python
from functools import partial

import jax
import jax.numpy as jnp
from jax import lax
from jax.experimental import pallas as pl
from jax.experimental.pallas import tpu as pltpu
from jax.sharding import PartitionSpec as P

PIX = 256
TX = 32
LANES = 128
PROJ = 9
GROUP = 8
STEP = LANES // GROUP
LOG2E = 1.4426950408889634
VMEM_BYTES = 52 * 1024 * 1024

f32 = jnp.float32
bf16 = jnp.bfloat16
i32 = jnp.int32


def iota(shape, dim):
    return lax.broadcasted_iota(i32, shape, dim)


def lane_pick(row, lanes):
    source = jnp.broadcast_to(row, lanes.shape)
    return jnp.take_along_axis(source, lanes, axis=1, mode="promise_in_bounds")


def split_two(values):
    first = values.astype(bf16).astype(f32)
    return first, values - first


def split_three(values):
    first, rest = split_two(values)
    second, third = split_two(rest)
    return first, second, third


def dot(lhs, rhs):
    return lax.dot_general(lhs, rhs, (((1,), (0,)), ((), ())), preferred_element_type=f32)


def dot_nt(lhs, rhs):
    return lax.dot_general(lhs, rhs, (((1,), (1,)), ((), ())), preferred_element_type=f32)


def dot_tn(lhs, rhs):
    return lax.dot_general(lhs, rhs, (((0,), (0,)), ((), ())), preferred_element_type=f32)


class Rows:
    def __init__(self, devices, per_owner):
        self.halves = per_owner // LANES if per_owner % LANES == 0 else 0
        self.count = devices * per_owner // LANES

    def ids(self, ref, block):
        halves = self.halves
        if halves <= 1:
            return ref[pl.ds(8 * block, 8), :]
        return ref[pl.ds(block // halves * 8 * halves + block % halves, 8, stride=halves), :]

    def natural(self, ref, block):
        halves = self.halves
        if halves <= 1:
            return ref[pl.ds(8 * block, 8), :]
        start = block // halves * 8
        return ref[start : start + 8, block % halves * LANES : (block % halves + 1) * LANES]

    def block(self, channel, block):
        halves = self.halves
        if halves == 0:
            return pl.ds(channel * self.count + 8 * block, 8)
        start = block // halves * 8 * PROJ * halves + channel * halves + block % halves
        return pl.ds(start, 8, stride=PROJ * halves)

    def row(self, channel, major, minor):
        halves = self.halves
        if halves == 0:
            return channel * self.count + major
        return major * (PROJ * halves) + channel * halves + minor

    def minors(self):
        return max(self.halves, 1)


def gather_rows(ref, place, majors, minors, slots):
    rows = slots // LANES
    lanes = slots % LANES

    def step(major, found):
        for minor in range(minors):
            here = rows == major * minors + minor
            found = tuple(
                jnp.where(here, lane_pick(ref[pl.ds(place(channel, major, minor), 1), :], lanes), value)
                for channel, value in enumerate(found)
            )
        return found

    start = tuple(jnp.zeros(slots.shape, f32) for _ in range(PROJ))
    return lax.fori_loop(0, majors, step, start, unroll=4)


def route_kernel(devices, per_owner, own_ref, loc_ref, want_ref, back_ref, pos_ref, own_s, loc_s, rank_s):
    rows = own_s.shape[0]
    blocks = own_ref.shape[1] // LANES
    lane = iota((8, LANES), 1)
    from_slot = iota((8, LANES), 0) * STEP + lane // GROUP
    tile_of = lane % GROUP
    for group in range(own_ref.shape[0] // GROUP):
        for block in range(blocks):
            for source, target in ((own_ref, own_s), (loc_ref, loc_s)):
                part = source[group * GROUP : (group + 1) * GROUP, block * LANES : (block + 1) * LANES]
                out = jnp.zeros((8, LANES), i32)
                for tile in range(GROUP):
                    out = jnp.where(tile_of == tile, lane_pick(part[tile : tile + 1], from_slot), out)
                start = (group * blocks + block) * 8
                target[start : start + 8, :] = out
    owner = own_s[...]
    left = (iota((LANES, 2 * LANES), 0) < iota((LANES, 2 * LANES), 1)) | (iota((LANES, 2 * LANES), 1) >= LANES)
    above = iota((rows, rows), 1) < iota((rows, rows), 0)
    hits = jnp.concatenate([jnp.where(owner == one, 1.0, 0.0).astype(bf16) for one in range(devices)], axis=0)
    sums = dot(hits, jnp.where(left, 1.0, 0.0).astype(bf16))
    totals = jnp.concatenate(
        [sums[one * rows : (one + 1) * rows, LANES:].astype(bf16) for one in range(devices)], axis=1
    )
    base = dot(jnp.where(above, 1.0, 0.0).astype(bf16), totals)
    rank = jnp.zeros((rows, LANES), f32)
    for one in range(devices):
        here = sums[one * rows : (one + 1) * rows, :LANES] + base[:, one * LANES : (one + 1) * LANES]
        rank = jnp.where(owner == one, here, rank)
    rank = rank.astype(i32)
    pos_ref[...] = owner * per_owner + rank
    rank_s[...] = rank

    owner_id = iota((devices, LANES), 0)
    rank_id = iota((per_owner, LANES), 0)
    slot_lane = iota((devices, LANES), 1).astype(f32)

    def place(index, total):
        start = pl.multiple_of(index * 8, 8)
        own_rows = own_s[pl.ds(start, 8), :]
        loc_rows = loc_s[pl.ds(start, 8), :]
        rank_rows = rank_s[pl.ds(start, 8), :]
        high_rows = (loc_rows // LANES).astype(f32)
        low_rows = (loc_rows % LANES).astype(f32)
        lhs = []
        rhs = []
        for row in range(8):
            mine = own_rows[row : row + 1] == owner_id
            number = (start + row).astype(f32)
            lhs.append(
                jnp.concatenate(
                    [
                        jnp.where(mine, high_rows[row : row + 1], 0.0),
                        jnp.where(mine, low_rows[row : row + 1], 0.0),
                        jnp.where(mine, number, 0.0),
                        jnp.where(mine, slot_lane, 0.0),
                    ],
                    axis=0,
                ).astype(bf16)
            )
            rhs.append(jnp.where(rank_rows[row : row + 1] == rank_id, 1.0, 0.0).astype(bf16))
        return total + dot_nt(jnp.concatenate(lhs, axis=1), jnp.concatenate(rhs, axis=1))

    total = lax.fori_loop(0, rows // 8, place, jnp.zeros((4 * devices, per_owner), f32)).astype(i32)
    want = total[:devices] * LANES + total[devices : 2 * devices]
    halves = per_owner // LANES
    if per_owner % LANES == 0 and halves > 1:
        for half in range(halves):
            want_ref[pl.ds(half, devices, stride=halves), :] = want[:, half * LANES : (half + 1) * LANES]
    else:
        want_ref[...] = want
    back_ref[...] = total[2 * devices : 3 * devices] * LANES + total[3 * devices :]


def view(angles_ref):
    angle = [jnp.full((1, LANES), angles_ref[index], f32) for index in range(3)]
    (cos_a, cos_b, cos_c) = [jnp.cos(one) for one in angle]
    (sin_a, sin_b, sin_c) = [jnp.sin(one) for one in angle]
    return [
        [cos_c * cos_b, cos_c * sin_b * sin_a - sin_c * cos_a, cos_c * sin_b * cos_a + sin_c * sin_a],
        [sin_c * cos_b, sin_c * sin_b * sin_a + cos_c * cos_a, sin_c * sin_b * cos_a - cos_c * sin_a],
        [-sin_b, cos_b * sin_a, cos_b * cos_a],
    ]


def harmonics(along_x, along_y, along_z):
    sq_x = along_x * along_x
    sq_y = along_y * along_y
    sq_z = along_z * along_z
    return [
        0.28209479177387814 + 0.0 * along_x,
        -0.4886025119029199 * along_y,
        0.4886025119029199 * along_z,
        -0.4886025119029199 * along_x,
        1.0925484305920792 * along_x * along_y,
        -1.0925484305920792 * along_y * along_z,
        0.31539156525252005 * (2.0 * sq_z - sq_x - sq_y),
        -1.0925484305920792 * along_x * along_z,
        0.5462742152960396 * (sq_x - sq_y),
        -0.5900435899266435 * along_y * (3.0 * sq_x - sq_y),
        2.890611442640554 * along_x * along_y * along_z,
        -0.4570457994644658 * along_y * (4.0 * sq_z - sq_x - sq_y),
        0.3731763325901154 * along_z * (2.0 * sq_z - 3.0 * sq_x - 3.0 * sq_y),
        -0.4570457994644658 * along_x * (4.0 * sq_z - sq_x - sq_y),
        1.445305721320277 * along_z * (sq_x - sq_y),
        -0.5900435899266435 * along_x * (sq_x - 3.0 * sq_y),
    ]


def basis_rows(basis, eighth):
    sub = iota((8, LANES), 0)
    found = []
    for colour in range(3):
        out = None
        for inner in range(8):
            index = 8 * eighth + inner - 11 - 16 * colour
            if 0 <= index < 16:
                out = jnp.zeros((8, LANES), f32) if out is None else out
                out = jnp.where(sub == inner, basis[index], out)
        found.append(out)
    return found


def shape_of(columns, rotation, camera_frame):
    focal_x, focal_y, centre_x, centre_y = camera_frame
    positions = columns[0:3]
    cam_first = rotation[0][0] * positions[0] + rotation[0][1] * positions[1] + rotation[0][2] * positions[2]
    cam_second = rotation[1][0] * positions[0] + rotation[1][1] * positions[1] + rotation[1][2] * positions[2]
    mean_x = centre_x + focal_x * cam_first
    mean_y = centre_y + focal_y * cam_second
    scales = [jnp.exp(one) for one in columns[3:6]]
    quat_w, quat_x, quat_y, quat_z = columns[6:10]
    norm_sq = jnp.maximum(quat_w * quat_w + quat_x * quat_x + quat_y * quat_y + quat_z * quat_z, 1.0)
    twice = 2.0 / norm_sq
    turned = [
        [
            1.0 - twice * (quat_y * quat_y + quat_z * quat_z),
            twice * (quat_x * quat_y - quat_w * quat_z),
            twice * (quat_x * quat_z + quat_w * quat_y),
        ],
        [
            twice * (quat_x * quat_y + quat_w * quat_z),
            1.0 - twice * (quat_x * quat_x + quat_z * quat_z),
            twice * (quat_y * quat_z - quat_w * quat_x),
        ],
        [
            twice * (quat_x * quat_z - quat_w * quat_y),
            twice * (quat_y * quat_z + quat_w * quat_x),
            1.0 - twice * (quat_x * quat_x + quat_y * quat_y),
        ],
    ]
    rows = []
    for focal, turn in ((focal_x, rotation[0]), (focal_y, rotation[1])):
        rows.append(
            [
                focal * (turn[0] * turned[0][k] + turn[1] * turned[1][k] + turn[2] * turned[2][k]) * scales[k]
                for k in range(3)
            ]
        )
    first, second = rows
    cov_a = first[0] * first[0] + first[1] * first[1] + first[2] * first[2] + 0.3
    cov_b = first[0] * second[0] + first[1] * second[1] + first[2] * second[2]
    cov_c = second[0] * second[0] + second[1] * second[1] + second[2] * second[2] + 0.3
    determinant = cov_a * cov_c - cov_b * cov_b
    opacity = 1.0 / (1.0 + jnp.exp(-columns[10]))
    return mean_x, mean_y, cov_c / determinant, -cov_b / determinant, cov_a / determinant, opacity


def spread_columns(gauss_ref, dense_s):
    rows = gauss_ref.shape[1] // LANES
    for row in range(rows):
        for eighth in range(2):
            dense_s[pl.ds(8 * eighth * rows + row, 8, stride=rows), :] = gauss_ref[
                8 * eighth : 8 * eighth + 8, row * LANES : (row + 1) * LANES
            ]


def shade_kernel(camera_frame, angles_ref, gauss_ref, table_ref, dense_s, tint_s):
    rows = gauss_ref.shape[1] // LANES
    spread_columns(gauss_ref, dense_s)
    rotation = view(angles_ref)
    basis = harmonics(*rotation[2])
    patterns = [basis_rows(basis, eighth) for eighth in range(7)]
    for row in range(rows):
        lanes = slice(row * LANES, (row + 1) * LANES)
        tints = [None] * 3
        for eighth in range(1, 7):
            block = gauss_ref[8 * eighth : 8 * eighth + 8, lanes]
            for colour in range(3):
                pattern = patterns[eighth][colour]
                if pattern is not None:
                    term = block * pattern
                    tints[colour] = term if tints[colour] is None else tints[colour] + term
        for colour in range(3):
            tint_s[pl.ds(8 * colour * rows + row, 8, stride=rows), :] = tints[colour]
        tint_s[pl.ds(24 * rows + row, 3, stride=rows), :] = gauss_ref[56:59, lanes]
    columns = [dense_s[index * rows : (index + 1) * rows, :] for index in range(11)]
    shaped = shape_of(columns, rotation, camera_frame)
    for index, value in enumerate(shaped):
        table_ref[index * rows : (index + 1) * rows, :] = value
    for colour in range(3):
        total = 0.5
        for inner in range(8):
            start = (8 * colour + inner) * rows
            total = total + tint_s[start : start + rows, :]
        if colour == 2:
            for inner in range(3):
                start = (24 + inner) * rows
                total = total + basis[13 + inner] * tint_s[start : start + rows, :]
        table_ref[(6 + colour) * rows : (7 + colour) * rows, :] = total


def pick_kernel(layout, table_ref, asked_ref, out_ref):
    rows = table_ref.shape[0] // PROJ
    for block in range(layout.count // 8):
        slots = layout.ids(asked_ref, block)
        found = gather_rows(table_ref, lambda channel, major, minor: channel * rows + major, rows, 1, slots)
        for channel in range(PROJ):
            out_ref[layout.block(channel, block), :] = found[channel]


def render_kernel(
    layout,
    count_ref,
    order_ref,
    rows_ref,
    pos_ref,
    back_ref,
    cot_ref,
    image_ref,
    out_ref,
    raw_s,
    coef_s,
    cot_s,
    rhs_s,
    tint_s,
    alpha_s,
    shade_s,
    weight_s,
    delta_s,
    sums_s,
):
    slot_rows = pos_ref.shape[0]
    groups = cot_ref.shape[1] // (GROUP * PIX)
    chunks = slot_rows // groups
    sub = iota((8, LANES), 0)
    lane = iota((8, LANES), 1)
    tile_of = lane % GROUP
    blocks = slot_rows // 8
    middles = []
    for group in range(groups):
        middle_x = jnp.zeros((8, LANES), f32)
        middle_y = jnp.zeros((8, LANES), f32)
        live = jnp.zeros((8, LANES), i32)
        for tile in range(GROUP):
            shown = order_ref[group * GROUP + tile]
            here = tile_of == tile
            middle_x = jnp.where(here, (shown % TX * 16 + 8).astype(f32), middle_x)
            middle_y = jnp.where(here, (shown // TX * 16 + 8).astype(f32), middle_y)
            live = jnp.where(here, count_ref[group * GROUP + tile], live)
        middles.append((middle_x, middle_y, live))

    for block in range(blocks):
        group = block * 8 // chunks
        middle_x, middle_y, live = middles[group]
        found = gather_rows(
            rows_ref, layout.row, layout.count // layout.minors(), layout.minors(), pos_ref[8 * block : 8 * block + 8, :]
        )
        for channel in range(PROJ):
            raw_s[channel * slot_rows + 8 * block : channel * slot_rows + 8 * block + 8, :] = found[channel]
        at_x = found[0] - middle_x
        at_y = found[1] - middle_y
        quad_a = -0.5 * found[2]
        quad_b = -found[3]
        quad_c = -0.5 * found[4]
        flat = quad_a * at_x * at_x + quad_c * at_y * at_y + quad_b * at_x * at_y + jnp.log(found[5])
        place = (8 * block - group * chunks + sub) * STEP + lane // GROUP
        terms = (
            quad_a * LOG2E,
            quad_b * LOG2E,
            quad_c * LOG2E,
            (-2.0 * quad_a * at_x - quad_b * at_y) * LOG2E,
            (-2.0 * quad_c * at_y - quad_b * at_x) * LOG2E,
            jnp.where(place < live, flat * LOG2E, -1e30),
        )
        for index, term in enumerate(terms):
            for part, value in enumerate(split_three(term)):
                coef_s[pl.ds(8 * block * 24 + 6 * part + index, 8, stride=24), :] = value
        for colour in range(3):
            for part, value in enumerate(split_two(found[6 + colour])):
                coef_s[pl.ds(8 * block * 24 + 18 + 3 * part + colour, 8, stride=24), :] = value

    pixel = iota((24, PIX), 1)
    row = iota((24, PIX), 0)
    pix_x = (pixel % 16).astype(f32) - 7.5
    pix_y = (pixel // 16).astype(f32) - 7.5
    kind = row % 6
    monomials = jnp.where(kind == 0, pix_x * pix_x, jnp.where(kind == 1, pix_x * pix_y, 1.0))
    monomials = jnp.where(kind == 2, pix_y * pix_y, monomials)
    monomials = jnp.where(kind == 3, pix_x, jnp.where(kind == 4, pix_y, monomials))
    moments = jnp.where(iota((8, PIX), 0) < 6, monomials[0:8], 0.0).astype(bf16)
    monomials = jnp.where(row < 18, monomials, 0.0)
    nothing = jnp.zeros((24, PIX), f32)
    for group in range(groups):
        for colour in range(3):
            for tile in range(GROUP):
                start = (group * GROUP + tile) * PIX
                cot_s[group * 24 + colour * GROUP + tile, :] = cot_ref[colour, start : start + PIX]
    cots = []
    for group in range(groups):
        first, second = split_two(cot_s[group * 24 : (group + 1) * 24, :])
        cots.append((jnp.concatenate([first, second], axis=0).astype(bf16), first.astype(bf16)))
        rhs_s[group] = jnp.concatenate(
            [
                jnp.concatenate([monomials, nothing], axis=1),
                jnp.concatenate([nothing, first], axis=1),
                jnp.concatenate([nothing, first], axis=1),
                jnp.concatenate([nothing, second], axis=1),
            ],
            axis=0,
        ).astype(bf16)

    own_tile = sub == tile_of

    def evaluate(index, _):
        for group in range(groups):
            chunk = group * chunks + index
            coefs = coef_s[pl.ds(pl.multiple_of(chunk * 24, 8), 24), :]
            tints = [jnp.where(own_tile, coefs[18 + one : 19 + one], 0.0) for one in range(6)]
            lhs = jnp.concatenate([coefs] + tints + tints[:3], axis=0).astype(bf16)
            tint_s[chunk] = lhs[24:72]
            both = dot_tn(lhs, rhs_s[group])
            start = pl.multiple_of(chunk * LANES, LANES)
            alpha_s[pl.ds(start, LANES), :] = jnp.exp2(both[:, :PIX])
            shade_s[pl.ds(start, LANES), :] = both[:, PIX:]
        return 0

    lax.fori_loop(0, chunks, evaluate, 0)

    def forward(index, state):
        out = []
        for group in range(groups):
            trans, image = state[group]
            chunk = group * chunks + index
            start = pl.multiple_of(chunk * LANES, LANES)
            for step in range(STEP):
                alpha = alpha_s[pl.ds(start + step * GROUP, GROUP), :]
                weight = trans * alpha
                trans = trans - weight
                weight_s[pl.ds(start + step * GROUP, GROUP), :] = weight
            first, second = split_two(weight_s[pl.ds(start, LANES), :])
            first = first.astype(bf16)
            second = second.astype(bf16)
            tints = tint_s[chunk]
            by_first = dot(tints, first)
            image = image + by_first[:24] + by_first[24:] + dot(tints[:24], second)
            both, leading = cots[group]
            by_first = dot_nt(both, first)
            tint_grad = by_first[:24] + by_first[24:] + dot_nt(leading, second)
            for colour in range(3):
                own = jnp.where(own_tile, tint_grad[colour * GROUP : (colour + 1) * GROUP], 0.0)
                sums_s[pl.ds(chunk * 16 + 8 + colour, 1), :] = jnp.sum(own, axis=0, keepdims=True)
            out.append((trans, image))
        return tuple(out)

    start = tuple((jnp.ones((GROUP, PIX), f32), jnp.zeros((24, PIX), f32)) for _ in range(groups))
    state = lax.fori_loop(0, chunks, forward, start)
    for group in range(groups):
        for colour in range(3):
            for tile in range(GROUP):
                at = (group * GROUP + tile) * PIX
                image_ref[colour, at : at + PIX] = state[group][1][colour * GROUP + tile]

    def backward(index, state):
        out = []
        for group in range(groups):
            behind = state[group]
            chunk = group * chunks + chunks - 1 - index
            start = pl.multiple_of(chunk * LANES, LANES)
            for step in reversed(range(STEP)):
                at = pl.ds(start + step * GROUP, GROUP)
                ahead = shade_s[at, :] - behind
                delta_s[group, step * GROUP : (step + 1) * GROUP, :] = weight_s[at, :] * ahead
                behind = behind + alpha_s[at, :] * ahead
            first, second = split_two(delta_s[group])
            found = dot_nt(moments, first.astype(bf16)) + dot_nt(moments, second.astype(bf16))
            sums_s[pl.ds(pl.multiple_of(chunk * 16, 8), 8), :] = found
            out.append(behind)
        return tuple(out)

    lax.fori_loop(0, chunks, backward, tuple(jnp.zeros((GROUP, PIX), f32) for _ in range(groups)))

    slot_s = coef_s
    for block in range(blocks):
        middle_x, middle_y, _ = middles[block * 8 // chunks]
        at = slice(8 * block, 8 * block + 8)
        raw = [raw_s[channel * slot_rows + 8 * block : channel * slot_rows + 8 * block + 8, :] for channel in range(6)]
        (sum_xx, sum_xy, sum_yy, sum_x, sum_y, sum_one) = [
            sums_s[pl.ds(8 * block * 16 + index, 8, stride=16), :] for index in range(6)
        ]
        at_x = raw[0] - middle_x
        at_y = raw[1] - middle_y
        off_x = sum_x - at_x * sum_one
        off_y = sum_y - at_y * sum_one
        grads = [
            raw[2] * off_x + raw[3] * off_y,
            raw[4] * off_y + raw[3] * off_x,
            -0.5 * (sum_xx - at_x * (sum_x + off_x)),
            -(sum_xy - at_y * sum_x - at_x * off_y),
            -0.5 * (sum_yy - at_y * (sum_y + off_y)),
            sum_one / raw[5],
        ] + [sums_s[pl.ds(8 * block * 16 + 8 + colour, 8, stride=16), :] for colour in range(3)]
        for channel, value in enumerate(grads):
            slot_s[channel * slot_rows + 8 * block : channel * slot_rows + 8 * block + 8, :] = value
    for block in range(layout.count // 8):
        slots = layout.natural(back_ref, block)
        found = gather_rows(slot_s, lambda channel, major, minor: channel * slot_rows + major, slot_rows, 1, slots)
        for channel in range(PROJ):
            out_ref[layout.block(channel, block), :] = found[channel]


def collect_kernel(layout, camera_frame, angles_ref, gauss_ref, asked_ref, terms_ref, grad_ref, lhs_s, rhs_s, total_s, dense_s, out_s):
    rows = gauss_ref.shape[1] // LANES
    wide = 2 * LANES
    lows = gauss_ref.shape[1] // wide
    low_id = iota((lows, LANES), 0)
    high_id = iota((wide, LANES), 0)
    minors = layout.minors()
    total_s[...] = jnp.zeros(total_s.shape, f32)

    def add(index, _):
        start = pl.multiple_of(index * 8, 8)
        asked = asked_ref[pl.ds(start, 8), :]
        low = asked // wide
        high = asked % wide
        for row in range(8):
            lanes = slice(row * LANES, (row + 1) * LANES)
            mine = low[row : row + 1] == low_id
            rhs_s[:, lanes] = jnp.where(high[row : row + 1] == high_id, 1.0, 0.0).astype(bf16)
            for channel in range(PROJ):
                at = layout.row(channel, index * (8 // minors) + row // minors, row % minors)
                for part, value in enumerate(split_two(terms_ref[pl.ds(at, 1), :])):
                    first = (part * PROJ + channel) * lows
                    lhs_s[first : first + lows, lanes] = jnp.where(mine, value, 0.0).astype(bf16)
        total_s[...] += dot_nt(lhs_s[...], rhs_s[...])
        return 0

    lax.fori_loop(0, layout.count // 8, add, 0)
    spread_columns(gauss_ref, dense_s)
    rotation = view(angles_ref)
    basis = harmonics(*rotation[2])
    for half in range(2):
        lanes = slice(half * LANES, (half + 1) * LANES)
        sums = [
            total_s[channel * lows : (channel + 1) * lows, lanes]
            + total_s[(PROJ + channel) * lows : (PROJ + channel + 1) * lows, lanes]
            for channel in range(PROJ)
        ]
        columns = tuple(dense_s[pl.ds(index * rows + half, lows, stride=2), :] for index in range(11))
        _, pullback = jax.vjp(lambda *values: shape_of(values, rotation, camera_frame), *columns)
        grads = pullback(tuple(sums[:6]))
        for index, value in enumerate(tuple(grads) + tuple(sums[6:])):
            out_s[pl.ds(index * rows + half, lows, stride=2), :] = value
    sub = iota((8, LANES), 0)
    patterns = [basis_rows(basis, eighth) for eighth in range(8)]
    for row in range(rows):
        lanes = slice(row * LANES, (row + 1) * LANES)
        grad_ref[0:8, lanes] = out_s[pl.ds(row, 8, stride=rows), :]
        tints = [out_s[(11 + colour) * rows + row : (11 + colour) * rows + row + 1, :] for colour in range(3)]
        for eighth in range(1, 8):
            value = None
            for colour in range(3):
                pattern = patterns[eighth][colour]
                if pattern is not None:
                    term = pattern * tints[colour]
                    value = term if value is None else value + term
            if eighth == 1:
                value = jnp.where(sub < 3, out_s[pl.ds(8 * rows + row, 8, stride=rows), :], value)
            if eighth == 7:
                grad_ref[56:59, lanes] = value[0:3]
            else:
                grad_ref[8 * eighth : 8 * eighth + 8, lanes] = value


VMEM = pl.BlockSpec(memory_space=pltpu.VMEM)
SMEM = pl.BlockSpec(memory_space=pltpu.SMEM)


def call(kernel, specs, outs, scratch, flops, name):
    return pl.pallas_call(
        kernel,
        in_specs=specs,
        out_specs=[VMEM] * len(outs),
        out_shape=[jax.ShapeDtypeStruct(shape, dtype) for shape, dtype in outs],
        scratch_shapes=[pltpu.VMEM(shape, dtype) for shape, dtype in scratch],
        compiler_params=pltpu.CompilerParams(vmem_limit_bytes=VMEM_BYTES),
        cost_estimate=pl.CostEstimate(flops=flops, bytes_accessed=4 << 20, transcendentals=0),
        name=name,
    )


def route(devices, owners, locals_):
    slots = owners.size
    per_owner = slots // devices
    rows = slots // LANES
    halves = per_owner // LANES if per_owner % LANES == 0 else 0
    asked = (devices * halves, LANES) if halves else (devices, per_owner)
    return call(
        partial(route_kernel, devices, per_owner),
        [VMEM, VMEM],
        [(asked, i32), ((devices, per_owner), i32), ((rows, LANES), i32)],
        [((rows, LANES), i32)] * 3,
        1 << 30,
        "route",
    )(owners, locals_)


def shade(camera_frame, view_angles, gaussians):
    rows = gaussians.shape[1] // LANES
    return call(
        partial(shade_kernel, camera_frame),
        [SMEM, VMEM],
        [((PROJ * rows, LANES), f32)],
        [((16 * rows, LANES), f32), ((27 * rows, LANES), f32)],
        1 << 30,
        "shade",
    )(view_angles, gaussians)[0]


def pick(layout, table, asked):
    return call(
        partial(pick_kernel, layout),
        [VMEM, VMEM],
        [((PROJ * layout.count, LANES), f32)],
        [],
        1 << 30,
        "pick",
    )(table, asked)[0]


def render(layout, list_counts, tile_order, rows, pos, back, cotangent):
    slot_rows = pos.shape[0]
    groups = tile_order.shape[0] // GROUP
    slots = slot_rows * LANES
    return call(
        partial(render_kernel, layout),
        [SMEM, SMEM, VMEM, VMEM, VMEM, VMEM],
        [(cotangent.shape, f32), ((PROJ * layout.count, LANES), f32)],
        [
            ((PROJ * slot_rows, LANES), f32),
            ((24 * slot_rows, LANES), f32),
            ((24 * groups, PIX), f32),
            ((groups, 96, 2 * PIX), bf16),
            ((slot_rows, 48, LANES), bf16),
            ((slots, PIX), f32),
            ((slots, PIX), f32),
            ((slots, PIX), f32),
            ((groups, LANES, PIX), f32),
            ((16 * slot_rows, LANES), f32),
        ],
        1 << 34,
        "render",
    )(list_counts, tile_order, rows, pos, back, cotangent)


def collect(layout, camera_frame, view_angles, gaussians, asked, terms):
    rows = gaussians.shape[1] // LANES
    lows = gaussians.shape[1] // (2 * LANES)
    return call(
        partial(collect_kernel, layout, camera_frame),
        [SMEM, VMEM, VMEM, VMEM],
        [(gaussians.shape, f32)],
        [
            ((2 * PROJ * lows, 8 * LANES), bf16),
            ((2 * LANES, 8 * LANES), bf16),
            ((2 * PROJ * lows, 2 * LANES), f32),
            ((16 * rows, LANES), f32),
            ((16 * rows, LANES), f32),
        ],
        1 << 32,
        "collect",
    )(view_angles, gaussians, asked, terms)[0]


def swap_rows(layout, devices, rows):
    if layout.halves:
        return lax.all_to_all(rows, "dev", split_axis=0, concat_axis=0, tiled=True)
    apart = rows.reshape(PROJ, devices, layout.count * LANES // devices)
    return lax.all_to_all(apart, "dev", split_axis=1, concat_axis=1, tiled=True).reshape(rows.shape)


def shards(gaussians, view_angles, tile_order, tile_owners, tile_locals, list_counts, image_cotangent):
    devices = lax.axis_size("dev")
    tiles_y = devices * tile_order.shape[0] // TX
    camera_frame = (4.0 * TX, 4.0 * tiles_y, 8.0 * TX, 8.0 * tiles_y)
    layout = Rows(devices, tile_owners.size // devices)
    want, back, pos = route(devices, tile_owners, tile_locals)
    asked = lax.all_to_all(want, "dev", split_axis=0, concat_axis=0, tiled=True)
    table = shade(camera_frame, view_angles, gaussians)
    if not layout.halves:
        asked = asked.reshape(layout.count, LANES)
        back = back.reshape(layout.count, LANES)
    arrived = swap_rows(layout, devices, pick(layout, table, asked))
    rendered, slot_grads = render(layout, list_counts, tile_order, arrived, pos, back, image_cotangent)
    terms = swap_rows(layout, devices, slot_grads)
    gradients = collect(layout, camera_frame, view_angles, gaussians, asked, terms)
    return (rendered, gradients)


def solution(mesh):
    return jax.shard_map(
        shards,
        mesh=mesh,
        in_specs=(
            P(None, "dev"),
            P(),
            P("dev"),
            P("dev", None),
            P("dev", None),
            P("dev"),
            P(None, "dev"),
        ),
        out_specs=(P(None, "dev"), P(None, "dev")),
        check_vma=False,
    )
```

time: 751 us -> 126 us (0.17)
  other arithmetic: 248 us -> 0 us
  local copies, waits for them, and re-layouts: 230 us -> 1.63 us
  matrix products: 131 us -> 0 us
  Pallas kernels: 0 us -> 81 us
  waiting for transfers between devices: 53.2 us -> 4.37 us
  loops' own time: 41.8 us -> 0 us
  blocking collectives: 0 us -> 30.4 us
  between operations: 25.6 us -> 0.72 us
  starting transfers between devices: 16.1 us -> 7.29 us
    gather x4 -> x0, local copies, waits for them, and re-layouts: 135 us -> none  [the longest x1 45.5 us: shards(): wanted = jnp.take(local_flat, grouping).reshape(devices, per_owner)]
    dot_general x178 -> x0, matrix products: 131 us -> none  [the longest x96 85.6 us: one_block(): added = jnp.einsum('ck,pk->cp', segment[6:9], weights, precision=highest)]
    pallas_call x0 -> x5, Pallas kernels: none -> 81 us  [the longest x1 50.8 us: render(): call(partial(render_kernel, layout), [SMEM, SMEM, VMEM, VMEM, VMEM, VMEM]...]
    div x48 -> x0, other arithmetic: 61.2 us -> none  [the longest x16 60.5 us: project(): cov_c / determinant]
    add x64 -> x0, other arithmetic: 60.4 us -> none  [the longest x16 60.1 us: project(): mean_x = centre_x + focal_x * cam_first]
    all_to_all x3 -> x1, waiting for transfers between devices: 53.2 us -> 4.37 us  [shards(): asked = lax.all_to_all(want, 'dev', split_axis=0, concat_axis=0, tiled=True)]
    scatter-add x1 -> x0, other arithmetic: 46.5 us -> none  [shards(): gradients = jnp.zeros_like(gaussians).at[:, received].add(terms)]
    another operation x1 -> x0, loops' own time: 41.8 us -> none  [shards(): lax.map(one_tile, (tile_rows, list_counts, tile_order, cotangents))]
  transfers between devices with their start and end apart: 3 -> 1, of which waited for: 2 -> 1; matrix products, arithmetic and copies ran while one was open for 5% -> 0% of each run, Pallas kernels for 0% -> 2%
where the time goes in v1:
time: 126 us; the launch traced here: 125 us
  Pallas kernels  81 us (64%)
  blocking collectives  30.4 us (24%)
  starting transfers between devices  7.29 us (6%)
  waiting for transfers between devices  4.37 us (3%)
  local copies, waits for them, and re-layouts  1.63 us (1%)
    pallas_call x1, Pallas kernels, render(): call(partial(render_kernel, layout), [SMEM, SMEM, VMEM, VMEM, VMEM, VMEM]...  50.8 us
    all_to_all x2, blocking collectives, swap_rows(): return lax.all_to_all(rows, 'dev', split_axis=0, concat_axis=0, tiled=True)  30.4 us
    pallas_call x1, Pallas kernels, pick(): call(partial(pick_kernel, layout), [VMEM, VMEM], [((PROJ * layout.count,...  13.8 us
    pallas_call x1, Pallas kernels, collect(): call(partial(collect_kernel, layout, camera_frame), [SMEM, VMEM, VMEM, VM...  9.39 us
    all_to_all x1, starting transfers between devices, shards(): asked = lax.all_to_all(want, 'dev', split_axis=0, concat_axis=0, tiled=True)  7.29 us
    all_to_all x1, waiting for transfers between devices, shards(): asked = lax.all_to_all(want, 'dev', split_axis=0, concat_axis=0, tiled=True)  4.37 us
    pallas_call x1, Pallas kernels, route(): call(partial(route_kernel, devices, per_owner), [VMEM, VMEM], [(asked, i3...  4.08 us
    pallas_call x1, Pallas kernels, shade(): call(partial(shade_kernel, camera_frame), [SMEM, VMEM], [((PROJ * rows, L...  2.86 us
  transfers between devices with their start and end apart: 1, of which 1 were waited for; matrix products, arithmetic and copies ran while one was open for 0% of the time, Pallas kernels for 2%

profile of v1, /device:TPU:0, one launch (start us, length us, event | category | flops | bytes accessed | tf_op | source)
XLA Modules:
  0.0 125.4 jit_solution(18431527665890537875)
XLA Ops:
  0.6 0.0 copy-start.1
  0.6 0.7 copy-done.1
  1.4 0.0 copy-start.2
  1.4 0.8 copy-done.2
  2.1 0.0 copy-start.5
  2.1 4.1 %route.1 = (s32[64,128]{1,0:T(8,128)}, s32[32,256]{1,0:T(8,128)S(1)}, s32[64,128]{1,0:T(8,128)S(1)}) custom-call(s32[16,512]{1,0:T(8,128)S(1)} %copy-done.1, s32[16,512]{1,0:T(8,128)S(1)} %copy-done.2), custom_call_target="tpu_custom_call" | custom-call | flops 1073741824 | bytes 4194304 | tf_op jit(solution)/shard_map/route/pallas_call | solution.py:614
  6.2 7.3 %all-to-all-start = ((s32[32,2,128]{2,1,0:T(2,128)}), s32[32,2,128]{2,1,0:T(2,128)S(1)}, u32[]{:S(2)}, u32[]{:S(2)}) async-start(s32[32,2,128]{2,1,0:T(2,128)} %bitcast), calls=%async_computation | async-start | bytes 65536 | tf_op jit(solution)/shard_map/all_to_all | solution.py:704
  13.5 0.0 copy-done.5
  13.5 2.9 %shade.1.table_ref = f32[576,128]{1,0:T(8,128)S(1)} custom-call(f32[3]{0:T(128)S(1)} %copy-done.5, f32[59,8192]{1,0:T(8,128)} %gauss_ref.3), custom_call_target="tpu_custom_call" | custom-call | flops 1073741824 | bytes 4194304 | tf_op jit(solution)/shard_map/shade/pallas_call | solution.py:626
  16.4 4.4 %all-to-all-done = s32[32,2,128]{2,1,0:T(2,128)S(1)} async-done(((s32[32,2,128]{2,1,0:T(2,128)}), s32[32,2,128]{2,1,0:T(2,128)S(1)}, u32[]{:S(2)}, u32[]{:S(2)}) %all-to-all-start) | async-done | bytes 32800 | tf_op jit(solution)/shard_map/all_to_all | solution.py:704
  20.8 0.0 copy-start
  20.8 0.0 copy-start.3
  20.8 0.0 copy-start.4
  20.8 13.8 %pick.1 = f32[576,128]{1,0:T(8,128)S(1)} custom-call(f32[576,128]{1,0:T(8,128)S(1)} %shade.1.table_ref, s32[64,128]{1,0:T(8,128)S(1)} %bitcast.2), custom_call_target="tpu_custom_call" | custom-call | flops 1073741824 | bytes 4194304 | tf_op jit(solution)/shard_map/pick/pallas_call | solution.py:637
  34.7 14.9 %all_to_all.33 = f32[32,18,128]{2,1,0:T(8,128)S(1)} all-to-all(f32[32,18,128]{2,1,0:T(8,128)S(1)} %all_to_all.24), channel_id=1, replica_groups=mesh['dev'=32] {'dev'}, dimensions={0} | all-to-all | bytes 589824 | tf_op jit(solution)/shard_map/all_to_all | solution.py:693
  49.6 0.0 copy-done
  49.6 0.0 copy-done.3
  49.6 0.0 copy-done.4
  49.6 50.8 %render.1 = (f32[3,4096]{1,0:T(4,128)}, f32[576,128]{1,0:T(8,128)S(1)}) custom-call(s32[16]{0:T(128)S(1)} %copy-done.3, s32[16]{0:T(128)S(1)} %copy-done.4, f32[576,128]{1,0:T(8,128)S(1)} %all_to_all.26.rows_ref, s32[64,128]{1,0:T(8,128)S(1)} %get-tuple-element.8.pos_ref, s32[32,256]{1,0:T(8,128)S(1)} %get-tuple-element.9.back_ref, f32[3,4096]{1,0:T(4,128)S(1)} %copy-done), custom_call_target="tpu_custom_call" | custom-call | flops 17179869184 | bytes 4194304 | tf_op jit(solution)/shard_map/render/pallas_call | solution.py:651
  100.5 15.5 %all_to_all.34 = f32[32,18,128]{2,1,0:T(8,128)S(1)} all-to-all(f32[32,18,128]{2,1,0:T(8,128)S(1)} %all_to_all.27), channel_id=1, replica_groups=mesh['dev'=32] {'dev'}, dimensions={0} | all-to-all | bytes 589824 | tf_op jit(solution)/shard_map/all_to_all | solution.py:693
  116.0 9.4 %collect.1 = f32[59,8192]{1,0:T(8,128)} custom-call(f32[3]{0:T(128)S(1)} %copy-done.5, f32[59,8192]{1,0:T(8,128)} %gauss_ref.3, s32[64,128]{1,0:T(8,128)S(1)} %bitcast.3, f32[576,128]{1,0:T(8,128)S(1)} %all_to_all.29.terms_ref), custom_call_target="tpu_custom_call" | custom-call | flops 4294967296 | bytes 4194304 | tf_op jit(solution)/shard_map/collect/pallas_call | solution.py:675
  (4 shorter events, 0.1 us)
Async XLA Ops:
  0.6 0.8 copy-start.1
  1.4 0.8 copy-start.2
  2.1 11.4 %copy-start.5 = (f32[3]{0:T(128)S(1)}, f32[3]{0:T(128)}, u32[]{:S(2)}) copy-start(f32[3]{0:T(128)} %angles_ref.3) | copy-start | bytes 40
  6.2 14.5 %all-to-all-start = ((s32[32,2,128]{2,1,0:T(2,128)}), s32[32,2,128]{2,1,0:T(2,128)S(1)}, u32[]{:S(2)}, u32[]{:S(2)}) async-start(s32[32,2,128]{2,1,0:T(2,128)} %bitcast), calls=%async_computation | async-start | bytes 65536 | tf_op jit(solution)/shard_map/all_to_all | solution.py:704
  20.8 28.8 %copy-start = (f32[3,4096]{1,0:T(4,128)S(1)}, f32[3,4096]{1,0:T(4,128)}, u32[]{:S(2)}) copy-start(f32[3,4096]{1,0:T(4,128)} %cot_ref.1) | copy-start | bytes 147460
  20.8 28.8 %copy-start.3 = (s32[16]{0:T(128)S(1)}, s32[16]{0:T(128)}, u32[]{:S(2)}) copy-start(s32[16]{0:T(128)} %count_ref.1) | copy-start | bytes 196
  20.8 28.8 %copy-start.4 = (s32[16]{0:T(128)S(1)}, s32[16]{0:T(128)}, u32[]{:S(2)}) copy-start(s32[16]{0:T(128)} %order_ref.1) | copy-start | bytes 196

commit v2 on v1

--- a/solution.py
+++ b/solution.py
@@ -88,21 +88,33 @@
         return max(self.halves, 1)
 
 
-def gather_rows(ref, place, majors, minors, slots):
-    rows = slots // LANES
-    lanes = slots % LANES
-
-    def step(major, found):
-        for minor in range(minors):
-            here = rows == major * minors + minor
-            found = tuple(
-                jnp.where(here, lane_pick(ref[pl.ds(place(channel, major, minor), 1), :], lanes), value)
-                for channel, value in enumerate(found)
-            )
-        return found
-
-    start = tuple(jnp.zeros(slots.shape, f32) for _ in range(PROJ))
-    return lax.fori_loop(0, majors, step, start, unroll=4)
+def gather_rows(ref, place, majors, minors, slots, put):
+    rows = [one // LANES for one in slots]
+    lanes = [one % LANES for one in slots]
+    batch = 3
+    for first in range(0, PROJ, batch):
+
+        def step(major, found):
+            for minor in range(minors):
+                here = [one == major * minors + minor for one in rows]
+                out = []
+                for channel in range(batch):
+                    row = ref[pl.ds(place(first + channel, major, minor), 1), :]
+                    source = jnp.broadcast_to(row, (8, LANES))
+                    out.append(
+                        tuple(
+                            jnp.where(mask, lane_pick(source, lane), value)
+                            for mask, lane, value in zip(here, lanes, found[channel])
+                        )
+                    )
+                found = tuple(out)
+            return found
+
+        nothing = tuple(jnp.zeros((8, LANES), f32) for _ in slots)
+        found = lax.fori_loop(0, majors, step, (nothing,) * batch, unroll=2)
+        for channel in range(batch):
+            for block, value in enumerate(found[channel]):
+                put(first + channel, block, value)
 
 
 def route_kernel(devices, per_owner, own_ref, loc_ref, want_ref, back_ref, pos_ref, own_s, loc_s, rank_s):
@@ -281,7 +293,7 @@
             ]
 
 
-def shade_kernel(camera_frame, angles_ref, gauss_ref, table_ref, dense_s, tint_s):
+def shade_kernel(camera_frame, angles_ref, gauss_ref, parts_ref, dense_s, tint_s):
     rows = gauss_ref.shape[1] // LANES
     spread_columns(gauss_ref, dense_s)
     rotation = view(angles_ref)
@@ -302,8 +314,13 @@
         tint_s[pl.ds(24 * rows + row, 3, stride=rows), :] = gauss_ref[56:59, lanes]
     columns = [dense_s[index * rows : (index + 1) * rows, :] for index in range(11)]
     shaped = shape_of(columns, rotation, camera_frame)
+
+    def put(channel, value):
+        parts = jnp.concatenate(split_three(value), axis=0)
+        parts_ref[channel * LANES : (channel + 1) * LANES, :] = parts.T.astype(bf16)
+
     for index, value in enumerate(shaped):
-        table_ref[index * rows : (index + 1) * rows, :] = value
+        put(index, value)
     for colour in range(3):
         total = 0.5
         for inner in range(8):
@@ -313,16 +330,33 @@
             for inner in range(3):
                 start = (24 + inner) * rows
                 total = total + basis[13 + inner] * tint_s[start : start + rows, :]
-        table_ref[(6 + colour) * rows : (7 + colour) * rows, :] = total
-
-
-def pick_kernel(layout, table_ref, asked_ref, out_ref):
-    rows = table_ref.shape[0] // PROJ
-    for block in range(layout.count // 8):
-        slots = layout.ids(asked_ref, block)
-        found = gather_rows(table_ref, lambda channel, major, minor: channel * rows + major, rows, 1, slots)
-        for channel in range(PROJ):
-            out_ref[layout.block(channel, block), :] = found[channel]
+        put(6 + colour, total)
+
+
+def pick_kernel(layout, parts_ref, asked_ref, out_ref):
+    rows = parts_ref.shape[1] // 3
+    pair = 2 * LANES
+    row_id = iota((rows, pair), 0)
+    lane_id = iota((LANES, pair), 0)
+    minors = layout.minors()
+
+    def pick_some(index, _):
+        asked = asked_ref[pl.ds(pl.multiple_of(index * 8, 8), 8), :]
+        for two in range(4):
+            slots = jnp.concatenate([asked[2 * two : 2 * two + 1], asked[2 * two + 1 : 2 * two + 2]], axis=1)
+            here = jnp.where(slots // LANES == row_id, 1.0, 0.0).astype(bf16)
+            found = dot(parts_ref[...], jnp.concatenate([here, here, here], axis=0))
+            mine = slots % LANES == lane_id
+            for channel in range(PROJ):
+                value = jnp.where(mine, found[channel * LANES : (channel + 1) * LANES], 0.0)
+                value = jnp.sum(value, axis=0, keepdims=True)
+                for one in range(2):
+                    row = 2 * two + one
+                    at = layout.row(channel, index * (8 // minors) + row // minors, row % minors)
+                    out_ref[pl.ds(at, 1), :] = value[:, one * LANES : (one + 1) * LANES]
+        return 0
+
+    lax.fori_loop(0, layout.count // 8, pick_some, 0)
 
 
 def render_kernel(
@@ -366,14 +400,17 @@
             live = jnp.where(here, count_ref[group * GROUP + tile], live)
         middles.append((middle_x, middle_y, live))
 
+    def put_raw(channel, block, value):
+        raw_s[channel * slot_rows + 8 * block : channel * slot_rows + 8 * block + 8, :] = value
+
+    slots = [pos_ref[8 * block : 8 * block + 8, :] for block in range(blocks)]
+    gather_rows(rows_ref, layout.row, layout.count // layout.minors(), layout.minors(), slots, put_raw)
     for block in range(blocks):
         group = block * 8 // chunks
         middle_x, middle_y, live = middles[group]
-        found = gather_rows(
-            rows_ref, layout.row, layout.count // layout.minors(), layout.minors(), pos_ref[8 * block : 8 * block + 8, :]
-        )
-        for channel in range(PROJ):
-            raw_s[channel * slot_rows + 8 * block : channel * slot_rows + 8 * block + 8, :] = found[channel]
+        found = [
+            raw_s[channel * slot_rows + 8 * block : channel * slot_rows + 8 * block + 8, :] for channel in range(PROJ)
+        ]
         at_x = found[0] - middle_x
         at_y = found[1] - middle_y
         quad_a = -0.5 * found[2]
@@ -518,11 +555,12 @@
         ] + [sums_s[pl.ds(8 * block * 16 + 8 + colour, 8, stride=16), :] for colour in range(3)]
         for channel, value in enumerate(grads):
             slot_s[channel * slot_rows + 8 * block : channel * slot_rows + 8 * block + 8, :] = value
-    for block in range(layout.count // 8):
-        slots = layout.natural(back_ref, block)
-        found = gather_rows(slot_s, lambda channel, major, minor: channel * slot_rows + major, slot_rows, 1, slots)
-        for channel in range(PROJ):
-            out_ref[layout.block(channel, block), :] = found[channel]
+
+    def put_out(channel, block, value):
+        out_ref[layout.block(channel, block), :] = value
+
+    slots = [layout.natural(back_ref, block) for block in range(layout.count // 8)]
+    gather_rows(slot_s, lambda channel, major, minor: channel * slot_rows + major, slot_rows, 1, slots, put_out)
 
 
 def collect_kernel(layout, camera_frame, angles_ref, gauss_ref, asked_ref, terms_ref, grad_ref, lhs_s, rhs_s, total_s, dense_s, out_s):
@@ -626,7 +664,7 @@
     return call(
         partial(shade_kernel, camera_frame),
         [SMEM, VMEM],
-        [((PROJ * rows, LANES), f32)],
+        [((PROJ * LANES, 3 * rows), bf16)],
         [((16 * rows, LANES), f32), ((27 * rows, LANES), f32)],
         1 << 30,
         "shade",

time: 126 us -> 130 us (1.032)
  Pallas kernels: 81 us -> 85.4 us
    pallas_call x1, Pallas kernels: 50.8 us -> 62.4 us  [render(): call(partial(render_kernel, layout), [SMEM, SMEM, VMEM, VMEM, VMEM, VMEM]...]
    pallas_call x1, Pallas kernels: 13.8 us -> 6.6 us  [pick(): call(partial(pick_kernel, layout), [VMEM, VMEM], [((PROJ * layout.count,...]
where the time goes in v2:
time: 130 us
  Pallas kernels  85.4 us (66%)
  blocking collectives  30.4 us (23%)
  starting transfers between devices  7.29 us (6%)
  waiting for transfers between devices  4.35 us (3%)
  local copies, waits for them, and re-layouts  1.63 us (1%)
    pallas_call x1, Pallas kernels, render(): call(partial(render_kernel, layout), [SMEM, SMEM, VMEM, VMEM, VMEM, VMEM]...  62.4 us
    all_to_all x2, blocking collectives, swap_rows(): return lax.all_to_all(rows, 'dev', split_axis=0, concat_axis=0, tiled=True)  30.4 us
    pallas_call x1, Pallas kernels, collect(): call(partial(collect_kernel, layout, camera_frame), [SMEM, VMEM, VMEM, VM...  9.39 us
    all_to_all x1, starting transfers between devices, shards(): asked = lax.all_to_all(want, 'dev', split_axis=0, concat_axis=0, tiled=True)  7.29 us
    pallas_call x1, Pallas kernels, pick(): call(partial(pick_kernel, layout), [VMEM, VMEM], [((PROJ * layout.count,...  6.6 us
    all_to_all x1, waiting for transfers between devices, shards(): asked = lax.all_to_all(want, 'dev', split_axis=0, concat_axis=0, tiled=True)  4.35 us
    pallas_call x1, Pallas kernels, route(): call(partial(route_kernel, devices, per_owner), [VMEM, VMEM], [(asked, i3...  4.08 us
    pallas_call x1, Pallas kernels, shade(): call(partial(shade_kernel, camera_frame), [SMEM, VMEM], [((PROJ * LANES,...  2.88 us
  transfers between devices with their start and end apart: 1, of which 1 were waited for; matrix products, arithmetic and copies ran while one was open for 0% of the time, Pallas kernels for 2%

profile of v2, /device:TPU:0, one launch (start us, length us, event | category | flops | bytes accessed | tf_op | source)
XLA Modules:
  0.0 129.8 jit_solution(16518497210383731586)
XLA Ops:
  0.6 0.0 copy-start.1
  0.6 0.7 copy-done.1
  1.4 0.0 copy-start.2
  1.4 0.8 copy-done.2
  2.1 0.0 copy-start.5
  2.1 4.1 %route.1 = (s32[64,128]{1,0:T(8,128)}, s32[32,256]{1,0:T(8,128)S(1)}, s32[64,128]{1,0:T(8,128)S(1)}) custom-call(s32[16,512]{1,0:T(8,128)S(1)} %copy-done.1, s32[16,512]{1,0:T(8,128)S(1)} %copy-done.2), custom_call_target="tpu_custom_call" | custom-call | flops 1073741824 | bytes 4194304 | tf_op jit(solution)/shard_map/route/pallas_call | solution.py:652
  6.2 7.3 %all-to-all-start = ((s32[32,2,128]{2,1,0:T(2,128)}), s32[32,2,128]{2,1,0:T(2,128)S(1)}, u32[]{:S(2)}, u32[]{:S(2)}) async-start(s32[32,2,128]{2,1,0:T(2,128)} %bitcast), calls=%async_computation | async-start | bytes 65536 | tf_op jit(solution)/shard_map/all_to_all | solution.py:742
  13.5 0.0 copy-done.5
  13.5 2.9 %shade.1.parts_ref = bf16[1152,192]{1,0:T(8,128)(2,1)S(1)} custom-call(f32[3]{0:T(128)S(1)} %copy-done.5, f32[59,8192]{1,0:T(8,128)} %gauss_ref.3), custom_call_target="tpu_custom_call" | custom-call | flops 1073741824 | bytes 4194304 | tf_op jit(solution)/shard_map/shade/pallas_call | solution.py:664
  16.4 4.4 %all-to-all-done = s32[32,2,128]{2,1,0:T(2,128)S(1)} async-done(((s32[32,2,128]{2,1,0:T(2,128)}), s32[32,2,128]{2,1,0:T(2,128)S(1)}, u32[]{:S(2)}, u32[]{:S(2)}) %all-to-all-start) | async-done | bytes 32800 | tf_op jit(solution)/shard_map/all_to_all | solution.py:742
  20.8 0.0 copy-start
  20.8 0.0 copy-start.3
  20.8 0.0 copy-start.4
  20.8 6.6 %pick.1 = f32[576,128]{1,0:T(8,128)S(1)} custom-call(bf16[1152,192]{1,0:T(8,128)(2,1)S(1)} %shade.1.parts_ref, s32[64,128]{1,0:T(8,128)S(1)} %bitcast.2), custom_call_target="tpu_custom_call" | custom-call | flops 1073741824 | bytes 4194304 | tf_op jit(solution)/shard_map/pick/pallas_call | solution.py:675
  27.4 14.9 %all_to_all.33 = f32[32,18,128]{2,1,0:T(8,128)S(1)} all-to-all(f32[32,18,128]{2,1,0:T(8,128)S(1)} %all_to_all.24), channel_id=1, replica_groups=mesh['dev'=32] {'dev'}, dimensions={0} | all-to-all | bytes 589824 | tf_op jit(solution)/shard_map/all_to_all | solution.py:731
  42.4 0.0 copy-done
  42.4 0.0 copy-done.3
  42.4 0.0 copy-done.4
  42.4 62.4 %render.1 = (f32[3,4096]{1,0:T(4,128)}, f32[576,128]{1,0:T(8,128)S(1)}) custom-call(s32[16]{0:T(128)S(1)} %copy-done.3, s32[16]{0:T(128)S(1)} %copy-done.4, f32[576,128]{1,0:T(8,128)S(1)} %all_to_all.26.rows_ref, s32[64,128]{1,0:T(8,128)S(1)} %get-tuple-element.8.pos_ref, s32[32,256]{1,0:T(8,128)S(1)} %get-tuple-element.9.back_ref, f32[3,4096]{1,0:T(4,128)S(1)} %copy-done), custom_call_target="tpu_custom_call" | custom-call | flops 17179869184 | bytes 4194304 | tf_op jit(solution)/shard_map/render/pallas_call | solution.py:689
  104.8 15.5 %all_to_all.34 = f32[32,18,128]{2,1,0:T(8,128)S(1)} all-to-all(f32[32,18,128]{2,1,0:T(8,128)S(1)} %all_to_all.27), channel_id=1, replica_groups=mesh['dev'=32] {'dev'}, dimensions={0} | all-to-all | bytes 589824 | tf_op jit(solution)/shard_map/all_to_all | solution.py:731
  120.4 9.4 %collect.1 = f32[59,8192]{1,0:T(8,128)} custom-call(f32[3]{0:T(128)S(1)} %copy-done.5, f32[59,8192]{1,0:T(8,128)} %gauss_ref.3, s32[64,128]{1,0:T(8,128)S(1)} %bitcast.3, f32[576,128]{1,0:T(8,128)S(1)} %all_to_all.29.terms_ref), custom_call_target="tpu_custom_call" | custom-call | flops 4294967296 | bytes 4194304 | tf_op jit(solution)/shard_map/collect/pallas_call | solution.py:713
  (4 shorter events, 0.1 us)
Async XLA Ops:
  0.6 0.8 copy-start.1
  1.4 0.8 copy-start.2
  2.1 11.4 %copy-start.5 = (f32[3]{0:T(128)S(1)}, f32[3]{0:T(128)}, u32[]{:S(2)}) copy-start(f32[3]{0:T(128)} %angles_ref.3) | copy-start | bytes 40
  6.2 14.5 %all-to-all-start = ((s32[32,2,128]{2,1,0:T(2,128)}), s32[32,2,128]{2,1,0:T(2,128)S(1)}, u32[]{:S(2)}, u32[]{:S(2)}) async-start(s32[32,2,128]{2,1,0:T(2,128)} %bitcast), calls=%async_computation | async-start | bytes 65536 | tf_op jit(solution)/shard_map/all_to_all | solution.py:742
  20.8 21.6 %copy-start = (f32[3,4096]{1,0:T(4,128)S(1)}, f32[3,4096]{1,0:T(4,128)}, u32[]{:S(2)}) copy-start(f32[3,4096]{1,0:T(4,128)} %cot_ref.1) | copy-start | bytes 147460
  20.8 21.6 %copy-start.3 = (s32[16]{0:T(128)S(1)}, s32[16]{0:T(128)}, u32[]{:S(2)}) copy-start(s32[16]{0:T(128)} %count_ref.1) | copy-start | bytes 196
  20.8 21.6 %copy-start.4 = (s32[16]{0:T(128)S(1)}, s32[16]{0:T(128)}, u32[]{:S(2)}) copy-start(s32[16]{0:T(128)} %order_ref.1) | copy-start | bytes 196

commit v3 on v1

--- a/solution.py
+++ b/solution.py
@@ -12,6 +12,8 @@
 LANES = 128
 PROJ = 9
 GROUP = 8
+WIDE = 2 * LANES
+PARTS = (3, 3, 3, 3, 3, 2, 2, 2, 2)
 STEP = LANES // GROUP
 LOG2E = 1.4426950408889634
 VMEM_BYTES = 52 * 1024 * 1024
@@ -57,26 +59,6 @@
     def __init__(self, devices, per_owner):
         self.halves = per_owner // LANES if per_owner % LANES == 0 else 0
         self.count = devices * per_owner // LANES
-
-    def ids(self, ref, block):
-        halves = self.halves
-        if halves <= 1:
-            return ref[pl.ds(8 * block, 8), :]
-        return ref[pl.ds(block // halves * 8 * halves + block % halves, 8, stride=halves), :]
-
-    def natural(self, ref, block):
-        halves = self.halves
-        if halves <= 1:
-            return ref[pl.ds(8 * block, 8), :]
-        start = block // halves * 8
-        return ref[start : start + 8, block % halves * LANES : (block % halves + 1) * LANES]
-
-    def block(self, channel, block):
-        halves = self.halves
-        if halves == 0:
-            return pl.ds(channel * self.count + 8 * block, 8)
-        start = block // halves * 8 * PROJ * halves + channel * halves + block % halves
-        return pl.ds(start, 8, stride=PROJ * halves)
 
     def row(self, channel, major, minor):
         halves = self.halves
@@ -84,28 +66,47 @@
             return channel * self.count + major
         return major * (PROJ * halves) + channel * halves + minor
 
+    def half(self, ref, channel, half):
+        halves = self.halves
+        if halves == 0:
+            return ref[pl.ds(channel * self.count + half, self.count // 2, stride=2), :]
+        return jnp.concatenate(
+            [ref[pl.ds(self.row(channel, one // halves, one % halves), 1), :] for one in range(half, self.count, 2)], axis=0
+        ) if halves != 2 else ref[pl.ds(channel * 2 + half, self.count // 2, stride=2 * PROJ), :]
+
     def minors(self):
         return max(self.halves, 1)
 
 
-def gather_rows(ref, place, majors, minors, slots):
-    rows = slots // LANES
-    lanes = slots % LANES
-
-    def step(major, found):
-        for minor in range(minors):
-            here = rows == major * minors + minor
-            found = tuple(
-                jnp.where(here, lane_pick(ref[pl.ds(place(channel, major, minor), 1), :], lanes), value)
-                for channel, value in enumerate(found)
-            )
-        return found
-
-    start = tuple(jnp.zeros(slots.shape, f32) for _ in range(PROJ))
-    return lax.fori_loop(0, majors, step, start, unroll=4)
-
-
-def route_kernel(devices, per_owner, own_ref, loc_ref, want_ref, back_ref, pos_ref, own_s, loc_s, rank_s):
+def pick_slots(parts, slots, low_id, high_id, put):
+    here = jnp.where(slots % WIDE == high_id, 1.0, 0.0).astype(bf16)
+    found = dot(parts, here)
+    mine = slots // WIDE == low_id
+    lows = low_id.shape[0]
+    first = 0
+    for channel, count in enumerate(PARTS if parts.shape[0] == sum(PARTS) * lows else (2,) * PROJ):
+        value = found[first * lows : (first + 1) * lows]
+        for part in range(1, count):
+            value = value + found[(first + part) * lows : (first + part + 1) * lows]
+        first += count
+        put(channel, jnp.sum(jnp.where(mine, value, 0.0), axis=0, keepdims=True))
+
+
+def put_parts(parts_ref, channel, half, value, counts):
+    lows = value.shape[0]
+    first = sum(counts[:channel])
+    parts = split_three(value) if counts[channel] == 3 else split_two(value)
+    for part, one in enumerate(parts):
+        at = (first + part) * lows
+        parts_ref[at : at + lows, half * LANES : (half + 1) * LANES] = one.astype(bf16)
+
+
+def route_kernel(devices, per_owner, own_hbm, loc_hbm, want_ref, back_ref, pos_ref, own_ref, loc_ref, own_s, loc_s, rank_s, sems):
+    copies = [pltpu.make_async_copy(own_hbm, own_ref, sems.at[0]), pltpu.make_async_copy(loc_hbm, loc_ref, sems.at[1])]
+    for copy in copies:
+        copy.start()
+    for copy in copies:
+        copy.wait()
     rows = own_s.shape[0]
     blocks = own_ref.shape[1] // LANES
     lane = iota((8, LANES), 1)
@@ -281,7 +282,7 @@
             ]
 
 
-def shade_kernel(camera_frame, angles_ref, gauss_ref, table_ref, dense_s, tint_s):
+def shade_kernel(camera_frame, angles_ref, gauss_ref, parts_ref, dense_s, tint_s):
     rows = gauss_ref.shape[1] // LANES
     spread_columns(gauss_ref, dense_s)
     rotation = view(angles_ref)
@@ -300,29 +301,38 @@
         for colour in range(3):
             tint_s[pl.ds(8 * colour * rows + row, 8, stride=rows), :] = tints[colour]
         tint_s[pl.ds(24 * rows + row, 3, stride=rows), :] = gauss_ref[56:59, lanes]
-    columns = [dense_s[index * rows : (index + 1) * rows, :] for index in range(11)]
-    shaped = shape_of(columns, rotation, camera_frame)
-    for index, value in enumerate(shaped):
-        table_ref[index * rows : (index + 1) * rows, :] = value
-    for colour in range(3):
-        total = 0.5
-        for inner in range(8):
-            start = (8 * colour + inner) * rows
-            total = total + tint_s[start : start + rows, :]
-        if colour == 2:
-            for inner in range(3):
-                start = (24 + inner) * rows
-                total = total + basis[13 + inner] * tint_s[start : start + rows, :]
-        table_ref[(6 + colour) * rows : (7 + colour) * rows, :] = total
-
-
-def pick_kernel(layout, table_ref, asked_ref, out_ref):
-    rows = table_ref.shape[0] // PROJ
-    for block in range(layout.count // 8):
-        slots = layout.ids(asked_ref, block)
-        found = gather_rows(table_ref, lambda channel, major, minor: channel * rows + major, rows, 1, slots)
-        for channel in range(PROJ):
-            out_ref[layout.block(channel, block), :] = found[channel]
+    for half in range(2):
+        at = [pl.ds(index * rows + half, rows // 2, stride=2) for index in range(27)]
+        columns = [dense_s[one, :] for one in at[:11]]
+        for index, value in enumerate(shape_of(columns, rotation, camera_frame)):
+            put_parts(parts_ref, index, half, value, PARTS)
+        for colour in range(3):
+            total = 0.5
+            for inner in range(8):
+                total = total + tint_s[at[8 * colour + inner], :]
+            if colour == 2:
+                for inner in range(3):
+                    total = total + basis[13 + inner] * tint_s[at[24 + inner], :]
+            put_parts(parts_ref, 6 + colour, half, total, PARTS)
+
+
+def pick_kernel(layout, parts_ref, asked_ref, out_ref):
+    low_id = iota((parts_ref.shape[0] // sum(PARTS), WIDE), 0)
+    high_id = iota((WIDE, WIDE), 0)
+    minors = layout.minors()
+
+    def pick_some(index, _):
+        slots = jnp.concatenate([asked_ref[pl.ds(2 * index + one, 1), :] for one in range(2)], axis=1)
+
+        def put(channel, value):
+            for one in range(2):
+                at = layout.row(channel, (2 * index + one) // minors, (2 * index + one) % minors)
+                out_ref[pl.ds(at, 1), :] = value[:, one * LANES : (one + 1) * LANES]
+
+        pick_slots(parts_ref[...], slots, low_id, high_id, put)
+        return 0
+
+    lax.fori_loop(0, layout.count // 2, pick_some, 0, unroll=2)
 
 
 def render_kernel(
@@ -335,6 +345,8 @@
     cot_ref,
     image_ref,
     out_ref,
+    in_s,
+    out_s,
     raw_s,
     coef_s,
     cot_s,
@@ -366,14 +378,29 @@
             live = jnp.where(here, count_ref[group * GROUP + tile], live)
         middles.append((middle_x, middle_y, live))
 
+    for half in range(2):
+        for channel in range(PROJ):
+            put_parts(in_s, channel, half, layout.half(rows_ref, channel, half), PARTS)
+    low_id = iota((slot_rows // 2, WIDE), 0)
+    high_id = iota((WIDE, WIDE), 0)
+
+    def pick_in(index, _):
+        slots = jnp.concatenate([pos_ref[pl.ds(2 * index + one, 1), :] for one in range(2)], axis=1)
+
+        def put(channel, value):
+            for one in range(2):
+                raw_s[pl.ds(channel * slot_rows + 2 * index + one, 1), :] = value[:, one * LANES : (one + 1) * LANES]
+
+        pick_slots(in_s[...], slots, low_id, high_id, put)
+        return 0
+
+    lax.fori_loop(0, slot_rows // 2, pick_in, 0, unroll=2)
     for block in range(blocks):
         group = block * 8 // chunks
         middle_x, middle_y, live = middles[group]
-        found = gather_rows(
-            rows_ref, layout.row, layout.count // layout.minors(), layout.minors(), pos_ref[8 * block : 8 * block + 8, :]
-        )
-        for channel in range(PROJ):
-            raw_s[channel * slot_rows + 8 * block : channel * slot_rows + 8 * block + 8, :] = found[channel]
+        found = [
+            raw_s[channel * slot_rows + 8 * block : channel * slot_rows + 8 * block + 8, :] for channel in range(PROJ)
+        ]
         at_x = found[0] - middle_x
         at_y = found[1] - middle_y
         quad_a = -0.5 * found[2]
@@ -413,17 +440,16 @@
                 start = (group * GROUP + tile) * PIX
                 cot_s[group * 24 + colour * GROUP + tile, :] = cot_ref[colour, start : start + PIX]
     cots = []
+    spare = jnp.zeros((8, PIX), f32)
     for group in range(groups):
         first, second = split_two(cot_s[group * 24 : (group + 1) * 24, :])
-        cots.append((jnp.concatenate([first, second], axis=0).astype(bf16), first.astype(bf16)))
+        cots.append(jnp.concatenate([first, spare, second, spare], axis=0).astype(bf16))
         rhs_s[group] = jnp.concatenate(
             [
-                jnp.concatenate([monomials, nothing], axis=1),
-                jnp.concatenate([nothing, first], axis=1),
-                jnp.concatenate([nothing, first], axis=1),
-                jnp.concatenate([nothing, second], axis=1),
+                jnp.concatenate([jnp.concatenate([nothing, monomials[8 * one : 8 * one + 8]], axis=0) for one in range(3)], axis=0),
+                jnp.concatenate([first, spare, first, spare, second, spare], axis=0),
             ],
-            axis=0,
+            axis=1,
         ).astype(bf16)
 
     own_tile = sub == tile_of
@@ -433,68 +459,91 @@
             chunk = group * chunks + index
             coefs = coef_s[pl.ds(pl.multiple_of(chunk * 24, 8), 24), :]
             tints = [jnp.where(own_tile, coefs[18 + one : 19 + one], 0.0) for one in range(6)]
-            lhs = jnp.concatenate([coefs] + tints + tints[:3], axis=0).astype(bf16)
-            tint_s[chunk] = lhs[24:72]
+            lhs = jnp.concatenate(
+                tints[:3] + [coefs[0:8]] + tints[3:] + [coefs[8:16]] + tints[:3] + [coefs[16:24]], axis=0
+            ).astype(bf16)
+            tint_s[chunk] = lhs[0:64]
             both = dot_tn(lhs, rhs_s[group])
             start = pl.multiple_of(chunk * LANES, LANES)
             alpha_s[pl.ds(start, LANES), :] = jnp.exp2(both[:, :PIX])
             shade_s[pl.ds(start, LANES), :] = both[:, PIX:]
         return 0
 
-    lax.fori_loop(0, chunks, evaluate, 0)
-
-    def forward(index, state):
+    lax.fori_loop(0, chunks, evaluate, 0, unroll=2)
+
+    def scan(index, trans):
         out = []
         for group in range(groups):
-            trans, image = state[group]
+            one = trans[group]
+            start = pl.multiple_of((group * chunks + index) * LANES, LANES)
+            for step in range(STEP):
+                alpha = alpha_s[pl.ds(start + step * GROUP, GROUP), :]
+                weight = one * alpha
+                one = one - weight
+                weight_s[pl.ds(start + step * GROUP, GROUP), :] = weight
+            out.append(one)
+        return tuple(out)
+
+    def paint(index, images):
+        out = []
+        for group in range(groups):
             chunk = group * chunks + index
             start = pl.multiple_of(chunk * LANES, LANES)
-            for step in range(STEP):
-                alpha = alpha_s[pl.ds(start + step * GROUP, GROUP), :]
-                weight = trans * alpha
-                trans = trans - weight
-                weight_s[pl.ds(start + step * GROUP, GROUP), :] = weight
             first, second = split_two(weight_s[pl.ds(start, LANES), :])
             first = first.astype(bf16)
             second = second.astype(bf16)
             tints = tint_s[chunk]
             by_first = dot(tints, first)
-            image = image + by_first[:24] + by_first[24:] + dot(tints[:24], second)
-            both, leading = cots[group]
-            by_first = dot_nt(both, first)
-            tint_grad = by_first[:24] + by_first[24:] + dot_nt(leading, second)
+            out.append(images[group] + by_first[0:24] + by_first[32:56] + dot(tints[0:32], second)[0:24])
+            by_first = dot_nt(cots[group], first)
+            tint_grad = by_first[0:24] + by_first[32:56] + dot_nt(cots[group][0:32], second)[0:24]
             for colour in range(3):
                 own = jnp.where(own_tile, tint_grad[colour * GROUP : (colour + 1) * GROUP], 0.0)
                 sums_s[pl.ds(chunk * 16 + 8 + colour, 1), :] = jnp.sum(own, axis=0, keepdims=True)
-            out.append((trans, image))
         return tuple(out)
 
-    start = tuple((jnp.ones((GROUP, PIX), f32), jnp.zeros((24, PIX), f32)) for _ in range(groups))
-    state = lax.fori_loop(0, chunks, forward, start)
+    def forward(index, state):
+        trans, images = state
+        images = paint(index - 1, images)
+        return scan(index, trans), images
+
+    trans = scan(0, tuple(jnp.ones((GROUP, PIX), f32) for _ in range(groups)))
+    images = tuple(jnp.zeros((24, PIX), f32) for _ in range(groups))
+    trans, images = lax.fori_loop(1, chunks, forward, (trans, images))
+    images = paint(chunks - 1, images)
     for group in range(groups):
         for colour in range(3):
             for tile in range(GROUP):
                 at = (group * GROUP + tile) * PIX
-                image_ref[colour, at : at + PIX] = state[group][1][colour * GROUP + tile]
-
-    def backward(index, state):
+                image_ref[colour, at : at + PIX] = images[group][colour * GROUP + tile]
+
+    def moment(index):
+        for group in range(groups):
+            chunk = group * chunks + index
+            first, second = split_two(delta_s[group])
+            found = dot_nt(moments, first.astype(bf16)) + dot_nt(moments, second.astype(bf16))
+            sums_s[pl.ds(pl.multiple_of(chunk * 16, 8), 8), :] = found
+
+    def rescan(index, behinds):
         out = []
         for group in range(groups):
-            behind = state[group]
-            chunk = group * chunks + chunks - 1 - index
-            start = pl.multiple_of(chunk * LANES, LANES)
+            behind = behinds[group]
+            start = pl.multiple_of((group * chunks + index) * LANES, LANES)
             for step in reversed(range(STEP)):
                 at = pl.ds(start + step * GROUP, GROUP)
                 ahead = shade_s[at, :] - behind
                 delta_s[group, step * GROUP : (step + 1) * GROUP, :] = weight_s[at, :] * ahead
                 behind = behind + alpha_s[at, :] * ahead
-            first, second = split_two(delta_s[group])
-            found = dot_nt(moments, first.astype(bf16)) + dot_nt(moments, second.astype(bf16))
-            sums_s[pl.ds(pl.multiple_of(chunk * 16, 8), 8), :] = found
             out.append(behind)
         return tuple(out)
 
-    lax.fori_loop(0, chunks, backward, tuple(jnp.zeros((GROUP, PIX), f32) for _ in range(groups)))
+    def backward(index, behinds):
+        moment(chunks - index)
+        return rescan(chunks - 1 - index, behinds)
+
+    behinds = rescan(chunks - 1, tuple(jnp.zeros((GROUP, PIX), f32) for _ in range(groups)))
+    lax.fori_loop(1, chunks, backward, behinds)
+    moment(0)
 
     slot_s = coef_s
     for block in range(blocks):
@@ -518,11 +567,28 @@
         ] + [sums_s[pl.ds(8 * block * 16 + 8 + colour, 8, stride=16), :] for colour in range(3)]
         for channel, value in enumerate(grads):
             slot_s[channel * slot_rows + 8 * block : channel * slot_rows + 8 * block + 8, :] = value
-    for block in range(layout.count // 8):
-        slots = layout.natural(back_ref, block)
-        found = gather_rows(slot_s, lambda channel, major, minor: channel * slot_rows + major, slot_rows, 1, slots)
+
+    for half in range(2):
         for channel in range(PROJ):
-            out_ref[layout.block(channel, block), :] = found[channel]
+            value = slot_s[pl.ds(channel * slot_rows + half, slot_rows // 2, stride=2), :]
+            put_parts(out_s, channel, half, value, (2,) * PROJ)
+    minors = layout.minors()
+
+    def pick_out(index, _):
+        if layout.halves == 2:
+            slots = back_ref[pl.ds(index, 1), :]
+        else:
+            slots = jnp.concatenate([back_ref[pl.ds(2 * index + one, 1), :] for one in range(2)], axis=1)
+
+        def put(channel, value):
+            for one in range(2):
+                at = layout.row(channel, (2 * index + one) // minors, (2 * index + one) % minors)
+                out_ref[pl.ds(at, 1), :] = value[:, one * LANES : (one + 1) * LANES]
+
+        pick_slots(out_s[...], slots, low_id, high_id, put)
+        return 0
+
+    lax.fori_loop(0, layout.count // 2, pick_out, 0, unroll=2)
 
 
 def collect_kernel(layout, camera_frame, angles_ref, gauss_ref, asked_ref, terms_ref, grad_ref, lhs_s, rhs_s, total_s, dense_s, out_s):
@@ -589,6 +655,7 @@
 
 
 VMEM = pl.BlockSpec(memory_space=pltpu.VMEM)
+ANY = pl.BlockSpec(memory_space=pl.ANY)
 SMEM = pl.BlockSpec(memory_space=pltpu.SMEM)
 
 
@@ -598,7 +665,7 @@
         in_specs=specs,
         out_specs=[VMEM] * len(outs),
         out_shape=[jax.ShapeDtypeStruct(shape, dtype) for shape, dtype in outs],
-        scratch_shapes=[pltpu.VMEM(shape, dtype) for shape, dtype in scratch],
+        scratch_shapes=[pltpu.VMEM(*one) if isinstance(one, tuple) else one for one in scratch],
         compiler_params=pltpu.CompilerParams(vmem_limit_bytes=VMEM_BYTES),
         cost_estimate=pl.CostEstimate(flops=flops, bytes_accessed=4 << 20, transcendentals=0),
         name=name,
@@ -613,9 +680,9 @@
     asked = (devices * halves, LANES) if halves else (devices, per_owner)
     return call(
         partial(route_kernel, devices, per_owner),
-        [VMEM, VMEM],
+        [ANY, ANY],
         [(asked, i32), ((devices, per_owner), i32), ((rows, LANES), i32)],
-        [((rows, LANES), i32)] * 3,
+        [(owners.shape, i32)] * 2 + [((rows, LANES), i32)] * 3 + [pltpu.SemaphoreType.DMA((2,))],
         1 << 30,
         "route",
     )(owners, locals_)
@@ -626,7 +693,7 @@
     return call(
         partial(shade_kernel, camera_frame),
         [SMEM, VMEM],
-        [((PROJ * rows, LANES), f32)],
+        [((sum(PARTS) * rows // 2, WIDE), bf16)],
         [((16 * rows, LANES), f32), ((27 * rows, LANES), f32)],
         1 << 30,
         "shade",
@@ -653,11 +720,13 @@
         [SMEM, SMEM, VMEM, VMEM, VMEM, VMEM],
         [(cotangent.shape, f32), ((PROJ * layout.count, LANES), f32)],
         [
+            ((sum(PARTS) * slot_rows // 2, WIDE), bf16),
+            ((2 * PROJ * slot_rows // 2, WIDE), bf16),
             ((PROJ * slot_rows, LANES), f32),
             ((24 * slot_rows, LANES), f32),
             ((24 * groups, PIX), f32),
             ((groups, 96, 2 * PIX), bf16),
-            ((slot_rows, 48, LANES), bf16),
+            ((slot_rows, 64, LANES), bf16),
             ((slots, PIX), f32),
             ((slots, PIX), f32),
             ((slots, PIX), f32),
@@ -690,7 +759,8 @@
 
 def swap_rows(layout, devices, rows):
     if layout.halves:
-        return lax.all_to_all(rows, "dev", split_axis=0, concat_axis=0, tiled=True)
+        apart = rows.reshape(devices * PROJ, layout.halves, LANES)
+        return lax.all_to_all(apart, "dev", split_axis=0, concat_axis=0, tiled=True).reshape(rows.shape)
     apart = rows.reshape(PROJ, devices, layout.count * LANES // devices)
     return lax.all_to_all(apart, "dev", split_axis=1, concat_axis=1, tiled=True).reshape(rows.shape)
 
@@ -705,6 +775,7 @@
     table = shade(camera_frame, view_angles, gaussians)
     if not layout.halves:
         asked = asked.reshape(layout.count, LANES)
+    if layout.halves != 2:
         back = back.reshape(layout.count, LANES)
     arrived = swap_rows(layout, devices, pick(layout, table, asked))
     rendered, slot_grads = render(layout, list_counts, tile_order, arrived, pos, back, image_cotangent)

time: 126 us -> 96.8 us (0.77)
  Pallas kernels: 81 us -> 56.1 us
  blocking collectives: 30.4 us -> 26.4 us
    pallas_call x1, Pallas kernels: 50.8 us -> 33.3 us  [render(): call(partial(render_kernel, layout), [SMEM, SMEM, VMEM, VMEM, VMEM, VMEM]...]
    pallas_call x1, Pallas kernels: 13.8 us -> 6.33 us  [pick(): call(partial(pick_kernel, layout), [VMEM, VMEM], [((PROJ * layout.count,...]
    all_to_all x2, blocking collectives: 30.4 us -> 26.4 us  [swap_rows(): lax.all_to_all(apart, 'dev', split_axis=0, concat_axis=0, tiled=True)]
  transfers between devices with their start and end apart: 1 -> 1, of which waited for: 1 -> 1; matrix products, arithmetic and copies ran while one was open for 0% -> 0% of each run, Pallas kernels for 2% -> 3%
where the time goes in v3:
time: 96.8 us; the launch traced here: 96.4 us
  Pallas kernels  56.1 us (58%)
  blocking collectives  26.4 us (27%)
  starting transfers between devices  7.3 us (8%)
  waiting for transfers between devices  4.31 us (4%)
  local copies, waits for them, and re-layouts  1.52 us (2%)
    pallas_call x1, Pallas kernels, render(): call(partial(render_kernel, layout), [SMEM, SMEM, VMEM, VMEM, VMEM, VMEM]...  33.3 us
    all_to_all x2, blocking collectives, swap_rows(): lax.all_to_all(apart, 'dev', split_axis=0, concat_axis=0, tiled=True)  26.4 us
    pallas_call x1, Pallas kernels, collect(): call(partial(collect_kernel, layout, camera_frame), [SMEM, VMEM, VMEM, VM...  9.39 us
    all_to_all x1, starting transfers between devices, shards(): asked = lax.all_to_all(want, 'dev', split_axis=0, concat_axis=0, tiled=True)  7.3 us
    pallas_call x1, Pallas kernels, pick(): call(partial(pick_kernel, layout), [VMEM, VMEM], [((PROJ * layout.count,...  6.33 us
    all_to_all x1, waiting for transfers between devices, shards(): asked = lax.all_to_all(want, 'dev', split_axis=0, concat_axis=0, tiled=True)  4.31 us
    pallas_call x1, Pallas kernels, route(): call(partial(route_kernel, devices, per_owner), [ANY, ANY], [(asked, i32)...  4.16 us
    pallas_call x1, Pallas kernels, shade(): call(partial(shade_kernel, camera_frame), [SMEM, VMEM], [((sum(PARTS) * r...  2.92 us
  transfers between devices with their start and end apart: 1, of which 1 were waited for; matrix products, arithmetic and copies ran while one was open for 0% of the time, Pallas kernels for 3%

profile of v3, /device:TPU:0, one launch (start us, length us, event | category | flops | bytes accessed | tf_op | source)
XLA Modules:
  0.0 96.4 jit_solution(3321036393051673727)
XLA Ops:
  0.6 0.0 copy-start.1
  0.6 0.7 copy-done.1
  1.4 0.0 copy-start.2
  1.4 0.8 copy-done.2
  2.1 0.0 copy-start.5
  2.1 4.2 %route.1 = (s32[64,128]{1,0:T(8,128)}, s32[32,256]{1,0:T(8,128)S(1)}, s32[64,128]{1,0:T(8,128)S(1)}) custom-call(s32[16,512]{1,0:T(8,128)S(1)} %copy-done.1, s32[16,512]{1,0:T(8,128)S(1)} %copy-done.2), custom_call_target="tpu_custom_call" | custom-call | flops 1073741824 | bytes 4194304 | tf_op jit(solution)/shard_map/route/pallas_call | solution.py:681
  6.3 7.3 %all-to-all-start = ((s32[32,2,128]{2,1,0:T(2,128)}), s32[32,2,128]{2,1,0:T(2,128)S(1)}, u32[]{:S(2)}, u32[]{:S(2)}) async-start(s32[32,2,128]{2,1,0:T(2,128)} %bitcast), calls=%async_computation | async-start | bytes 65536 | tf_op jit(solution)/shard_map/all_to_all | solution.py:774
  13.6 0.0 copy-done.5
  13.6 2.9 %shade.1.parts_ref = bf16[736,256]{1,0:T(8,128)(2,1)S(1)} custom-call(f32[3]{0:T(128)S(1)} %copy-done.5, f32[59,8192]{1,0:T(8,128)} %gauss_ref.3), custom_call_target="tpu_custom_call" | custom-call | flops 1073741824 | bytes 4194304 | tf_op jit(solution)/shard_map/shade/pallas_call | solution.py:693
  16.6 4.3 %all-to-all-done = s32[32,2,128]{2,1,0:T(2,128)S(1)} async-done(((s32[32,2,128]{2,1,0:T(2,128)}), s32[32,2,128]{2,1,0:T(2,128)S(1)}, u32[]{:S(2)}, u32[]{:S(2)}) %all-to-all-start) | async-done | bytes 32800 | tf_op jit(solution)/shard_map/all_to_all | solution.py:774
  20.9 0.0 copy-start
  20.9 0.0 copy-start.3
  20.9 0.0 copy-start.4
  20.9 6.3 %pick.1 = f32[576,128]{1,0:T(8,128)S(1)} custom-call(bf16[736,256]{1,0:T(8,128)(2,1)S(1)} %shade.1.parts_ref, s32[64,128]{1,0:T(8,128)S(1)} %bitcast.10), custom_call_target="tpu_custom_call" | custom-call | flops 1073741824 | bytes 4194304 | tf_op jit(solution)/shard_map/pick/pallas_call | solution.py:704
  27.2 13.1 %all_to_all.21 = f32[288,2,128]{2,1,0:T(2,128)S(1)} all-to-all(f32[288,2,128]{2,1,0:T(2,128)S(1)} %bitcast.9), channel_id=1, replica_groups=mesh['dev'=32] {'dev'}, dimensions={0} | all-to-all | bytes 589824 | tf_op jit(solution)/shard_map/all_to_all | solution.py:763
  40.3 0.0 copy-done
  40.3 0.0 copy-done.3
  40.3 0.0 copy-done.4
  40.4 33.3 %render.1 = (f32[3,4096]{1,0:T(4,128)}, f32[576,128]{1,0:T(8,128)S(1)}) custom-call(s32[16]{0:T(128)S(1)} %copy-done.3, s32[16]{0:T(128)S(1)} %copy-done.4, f32[576,128]{1,0:T(8,128)S(1)} %bitcast.6, s32[64,128]{1,0:T(8,128)S(1)} %get-tuple-element.8.pos_ref, s32[32,256]{1,0:T(8,128)S(1)} %get-tuple-element.9.back_ref, f32[3,4096]{1,0:T(4,128)S(1)} %copy-done), custom_call_target="tpu_custom_call" | custom-call | flops 17179869184 | bytes 4194304 | tf_op jit(solution)/shard_map/render/pallas_call | solution.py:718
  73.7 13.3 %all_to_all.22 = f32[288,2,128]{2,1,0:T(2,128)S(1)} all-to-all(f32[288,2,128]{2,1,0:T(2,128)S(1)} %bitcast.7), channel_id=1, replica_groups=mesh['dev'=32] {'dev'}, dimensions={0} | all-to-all | bytes 589824 | tf_op jit(solution)/shard_map/all_to_all | solution.py:763
  87.0 9.4 %collect.1 = f32[59,8192]{1,0:T(8,128)} custom-call(f32[3]{0:T(128)S(1)} %copy-done.5, f32[59,8192]{1,0:T(8,128)} %gauss_ref.3, s32[64,128]{1,0:T(8,128)S(1)} %bitcast.11, f32[576,128]{1,0:T(8,128)S(1)} %bitcast.8), custom_call_target="tpu_custom_call" | custom-call | flops 4294967296 | bytes 4194304 | tf_op jit(solution)/shard_map/collect/pallas_call | solution.py:744
Async XLA Ops:
  0.6 0.8 copy-start.1
  1.4 0.8 copy-start.2
  2.1 11.5 %copy-start.5 = (f32[3]{0:T(128)S(1)}, f32[3]{0:T(128)}, u32[]{:S(2)}) copy-start(f32[3]{0:T(128)} %angles_ref.3) | copy-start | bytes 40
  6.3 14.6 %all-to-all-start = ((s32[32,2,128]{2,1,0:T(2,128)}), s32[32,2,128]{2,1,0:T(2,128)S(1)}, u32[]{:S(2)}, u32[]{:S(2)}) async-start(s32[32,2,128]{2,1,0:T(2,128)} %bitcast), calls=%async_computation | async-start | bytes 65536 | tf_op jit(solution)/shard_map/all_to_all | solution.py:774
  20.9 19.5 %copy-start = (f32[3,4096]{1,0:T(4,128)S(1)}, f32[3,4096]{1,0:T(4,128)}, u32[]{:S(2)}) copy-start(f32[3,4096]{1,0:T(4,128)} %cot_ref.1) | copy-start | bytes 147460
  20.9 19.5 %copy-start.3 = (s32[16]{0:T(128)S(1)}, s32[16]{0:T(128)}, u32[]{:S(2)}) copy-start(s32[16]{0:T(128)} %count_ref.1) | copy-start | bytes 196
  20.9 19.5 %copy-start.4 = (s32[16]{0:T(128)S(1)}, s32[16]{0:T(128)}, u32[]{:S(2)}) copy-start(s32[16]{0:T(128)} %order_ref.1) | copy-start | bytes 196

commit v4 on v3

--- a/solution.py
+++ b/solution.py
@@ -16,6 +16,7 @@
 PARTS = (3, 3, 3, 3, 3, 2, 2, 2, 2)
 STEP = LANES // GROUP
 LOG2E = 1.4426950408889634
+BATCH = 4
 VMEM_BYTES = 52 * 1024 * 1024
 
 f32 = jnp.float32
@@ -332,7 +333,7 @@
         pick_slots(parts_ref[...], slots, low_id, high_id, put)
         return 0
 
-    lax.fori_loop(0, layout.count // 2, pick_some, 0, unroll=2)
+    lax.fori_loop(0, layout.count // 2, pick_some, 0, unroll=4)
 
 
 def render_kernel(
@@ -355,7 +356,6 @@
     alpha_s,
     shade_s,
     weight_s,
-    delta_s,
     sums_s,
 ):
     slot_rows = pos_ref.shape[0]
@@ -394,7 +394,7 @@
         pick_slots(in_s[...], slots, low_id, high_id, put)
         return 0
 
-    lax.fori_loop(0, slot_rows // 2, pick_in, 0, unroll=2)
+    lax.fori_loop(0, slot_rows // 2, pick_in, 0, unroll=4)
     for block in range(blocks):
         group = block * 8 // chunks
         middle_x, middle_y, live = middles[group]
@@ -469,7 +469,7 @@
             shade_s[pl.ds(start, LANES), :] = both[:, PIX:]
         return 0
 
-    lax.fori_loop(0, chunks, evaluate, 0, unroll=2)
+    lax.fori_loop(0, chunks, evaluate, 0, unroll=BATCH)
 
     def scan(index, trans):
         out = []
@@ -502,15 +502,26 @@
                 sums_s[pl.ds(chunk * 16 + 8 + colour, 1), :] = jnp.sum(own, axis=0, keepdims=True)
         return tuple(out)
 
-    def forward(index, state):
+    def scan_batch(batch, trans):
+        for one in range(BATCH):
+            trans = scan(batch * BATCH + one, trans)
+        return trans
+
+    def paint_batch(batch, images):
+        for one in range(BATCH):
+            images = paint(batch * BATCH + one, images)
+        return images
+
+    def forward(batch, state):
         trans, images = state
-        images = paint(index - 1, images)
-        return scan(index, trans), images
-
-    trans = scan(0, tuple(jnp.ones((GROUP, PIX), f32) for _ in range(groups)))
+        images = paint_batch(batch - 1, images)
+        return scan_batch(batch, trans), images
+
+    batches = chunks // BATCH
+    trans = scan_batch(0, tuple(jnp.ones((GROUP, PIX), f32) for _ in range(groups)))
     images = tuple(jnp.zeros((24, PIX), f32) for _ in range(groups))
-    trans, images = lax.fori_loop(1, chunks, forward, (trans, images))
-    images = paint(chunks - 1, images)
+    trans, images = lax.fori_loop(1, batches, forward, (trans, images))
+    images = paint_batch(batches - 1, images)
     for group in range(groups):
         for colour in range(3):
             for tile in range(GROUP):
@@ -520,7 +531,7 @@
     def moment(index):
         for group in range(groups):
             chunk = group * chunks + index
-            first, second = split_two(delta_s[group])
+            first, second = split_two(shade_s[pl.ds(pl.multiple_of(chunk * LANES, LANES), LANES), :])
             found = dot_nt(moments, first.astype(bf16)) + dot_nt(moments, second.astype(bf16))
             sums_s[pl.ds(pl.multiple_of(chunk * 16, 8), 8), :] = found
 
@@ -532,18 +543,27 @@
             for step in reversed(range(STEP)):
                 at = pl.ds(start + step * GROUP, GROUP)
                 ahead = shade_s[at, :] - behind
-                delta_s[group, step * GROUP : (step + 1) * GROUP, :] = weight_s[at, :] * ahead
+                shade_s[at, :] = weight_s[at, :] * ahead
                 behind = behind + alpha_s[at, :] * ahead
             out.append(behind)
         return tuple(out)
 
+    def moment_batch(batch):
+        for one in range(BATCH):
+            moment(batch * BATCH + one)
+
+    def rescan_batch(batch, behinds):
+        for one in reversed(range(BATCH)):
+            behinds = rescan(batch * BATCH + one, behinds)
+        return behinds
+
     def backward(index, behinds):
-        moment(chunks - index)
-        return rescan(chunks - 1 - index, behinds)
-
-    behinds = rescan(chunks - 1, tuple(jnp.zeros((GROUP, PIX), f32) for _ in range(groups)))
-    lax.fori_loop(1, chunks, backward, behinds)
-    moment(0)
+        moment_batch(batches - index)
+        return rescan_batch(batches - 1 - index, behinds)
+
+    behinds = rescan_batch(batches - 1, tuple(jnp.zeros((GROUP, PIX), f32) for _ in range(groups)))
+    lax.fori_loop(1, batches, backward, behinds)
+    moment_batch(0)
 
     slot_s = coef_s
     for block in range(blocks):
@@ -588,7 +608,7 @@
         pick_slots(out_s[...], slots, low_id, high_id, put)
         return 0
 
-    lax.fori_loop(0, layout.count // 2, pick_out, 0, unroll=2)
+    lax.fori_loop(0, layout.count // 2, pick_out, 0, unroll=4)
 
 
 def collect_kernel(layout, camera_frame, angles_ref, gauss_ref, asked_ref, terms_ref, grad_ref, lhs_s, rhs_s, total_s, dense_s, out_s):
@@ -730,7 +750,6 @@
             ((slots, PIX), f32),
             ((slots, PIX), f32),
             ((slots, PIX), f32),
-            ((groups, LANES, PIX), f32),
             ((16 * slot_rows, LANES), f32),
         ],
         1 << 34,

time: 96.8 us -> 87.5 us (0.904)
  Pallas kernels: 56.1 us -> 46.8 us
    pallas_call x1, Pallas kernels: 33.3 us -> 25.6 us  [render(): call(partial(render_kernel, layout), [SMEM, SMEM, VMEM, VMEM, VMEM, VMEM]...]
    pallas_call x1, Pallas kernels: 6.33 us -> 4.65 us  [pick(): call(partial(pick_kernel, layout), [VMEM, VMEM], [((PROJ * layout.count,...]
where the time goes in v4:
time: 87.5 us; the launch traced here: 87.1 us
  Pallas kernels  46.8 us (53%)
  blocking collectives  26.5 us (30%)
  starting transfers between devices  7.3 us (8%)
  waiting for transfers between devices  4.31 us (5%)
  local copies, waits for them, and re-layouts  1.52 us (2%)
    all_to_all x2, blocking collectives, swap_rows(): lax.all_to_all(apart, 'dev', split_axis=0, concat_axis=0, tiled=True)  26.5 us
    pallas_call x1, Pallas kernels, render(): call(partial(render_kernel, layout), [SMEM, SMEM, VMEM, VMEM, VMEM, VMEM]...  25.6 us
    pallas_call x1, Pallas kernels, collect(): call(partial(collect_kernel, layout, camera_frame), [SMEM, VMEM, VMEM, VM...  9.39 us
    all_to_all x1, starting transfers between devices, shards(): asked = lax.all_to_all(want, 'dev', split_axis=0, concat_axis=0, tiled=True)  7.3 us
    pallas_call x1, Pallas kernels, pick(): call(partial(pick_kernel, layout), [VMEM, VMEM], [((PROJ * layout.count,...  4.65 us
    all_to_all x1, waiting for transfers between devices, shards(): asked = lax.all_to_all(want, 'dev', split_axis=0, concat_axis=0, tiled=True)  4.31 us
    pallas_call x1, Pallas kernels, route(): call(partial(route_kernel, devices, per_owner), [ANY, ANY], [(asked, i32)...  4.16 us
    pallas_call x1, Pallas kernels, shade(): call(partial(shade_kernel, camera_frame), [SMEM, VMEM], [((sum(PARTS) * r...  2.92 us
  transfers between devices with their start and end apart: 1, of which 1 were waited for; matrix products, arithmetic and copies ran while one was open for 0% of the time, Pallas kernels for 3%

profile of v4, /device:TPU:0, one launch (start us, length us, event | category | flops | bytes accessed | tf_op | source)
XLA Modules:
  0.0 87.1 jit_solution(4873980778238818693)
XLA Ops:
  0.6 0.0 copy-start.1
  0.6 0.7 copy-done.1
  1.4 0.0 copy-start.2
  1.4 0.8 copy-done.2
  2.1 0.0 copy-start.5
  2.1 4.2 %route.1 = (s32[64,128]{1,0:T(8,128)}, s32[32,256]{1,0:T(8,128)S(1)}, s32[64,128]{1,0:T(8,128)S(1)}) custom-call(s32[16,512]{1,0:T(8,128)S(1)} %copy-done.1, s32[16,512]{1,0:T(8,128)S(1)} %copy-done.2), custom_call_target="tpu_custom_call" | custom-call | flops 1073741824 | bytes 4194304 | tf_op jit(solution)/shard_map/route/pallas_call | solution.py:701
  6.3 7.3 %all-to-all-start = ((s32[32,2,128]{2,1,0:T(2,128)}), s32[32,2,128]{2,1,0:T(2,128)S(1)}, u32[]{:S(2)}, u32[]{:S(2)}) async-start(s32[32,2,128]{2,1,0:T(2,128)} %bitcast), calls=%async_computation | async-start | bytes 65536 | tf_op jit(solution)/shard_map/all_to_all | solution.py:793
  13.6 0.0 copy-done.5
  13.6 2.9 %shade.1.parts_ref = bf16[736,256]{1,0:T(8,128)(2,1)S(1)} custom-call(f32[3]{0:T(128)S(1)} %copy-done.5, f32[59,8192]{1,0:T(8,128)} %gauss_ref.3), custom_call_target="tpu_custom_call" | custom-call | flops 1073741824 | bytes 4194304 | tf_op jit(solution)/shard_map/shade/pallas_call | solution.py:713
  16.6 4.3 %all-to-all-done = s32[32,2,128]{2,1,0:T(2,128)S(1)} async-done(((s32[32,2,128]{2,1,0:T(2,128)}), s32[32,2,128]{2,1,0:T(2,128)S(1)}, u32[]{:S(2)}, u32[]{:S(2)}) %all-to-all-start) | async-done | bytes 32800 | tf_op jit(solution)/shard_map/all_to_all | solution.py:793
  20.9 0.0 copy-start
  20.9 0.0 copy-start.3
  20.9 0.0 copy-start.4
  20.9 4.6 %pick.1 = f32[576,128]{1,0:T(8,128)S(1)} custom-call(bf16[736,256]{1,0:T(8,128)(2,1)S(1)} %shade.1.parts_ref, s32[64,128]{1,0:T(8,128)S(1)} %bitcast.10), custom_call_target="tpu_custom_call" | custom-call | flops 1073741824 | bytes 4194304 | tf_op jit(solution)/shard_map/pick/pallas_call | solution.py:724
  25.5 13.1 %all_to_all.21 = f32[288,2,128]{2,1,0:T(2,128)S(1)} all-to-all(f32[288,2,128]{2,1,0:T(2,128)S(1)} %bitcast.9), channel_id=1, replica_groups=mesh['dev'=32] {'dev'}, dimensions={0} | all-to-all | bytes 589824 | tf_op jit(solution)/shard_map/all_to_all | solution.py:782
  38.7 0.0 copy-done
  38.7 0.0 copy-done.3
  38.7 0.0 copy-done.4
  38.7 25.6 %render.1 = (f32[3,4096]{1,0:T(4,128)}, f32[576,128]{1,0:T(8,128)S(1)}) custom-call(s32[16]{0:T(128)S(1)} %copy-done.3, s32[16]{0:T(128)S(1)} %copy-done.4, f32[576,128]{1,0:T(8,128)S(1)} %bitcast.6, s32[64,128]{1,0:T(8,128)S(1)} %get-tuple-element.8.pos_ref, s32[32,256]{1,0:T(8,128)S(1)} %get-tuple-element.9.back_ref, f32[3,4096]{1,0:T(4,128)S(1)} %copy-done), custom_call_target="tpu_custom_call" | custom-call | flops 17179869184 | bytes 4194304 | tf_op jit(solution)/shard_map/render/pallas_call | solution.py:738
  64.3 13.4 %all_to_all.22 = f32[288,2,128]{2,1,0:T(2,128)S(1)} all-to-all(f32[288,2,128]{2,1,0:T(2,128)S(1)} %bitcast.7), channel_id=1, replica_groups=mesh['dev'=32] {'dev'}, dimensions={0} | all-to-all | bytes 589824 | tf_op jit(solution)/shard_map/all_to_all | solution.py:782
  77.7 9.4 %collect.1 = f32[59,8192]{1,0:T(8,128)} custom-call(f32[3]{0:T(128)S(1)} %copy-done.5, f32[59,8192]{1,0:T(8,128)} %gauss_ref.3, s32[64,128]{1,0:T(8,128)S(1)} %bitcast.11, f32[576,128]{1,0:T(8,128)S(1)} %bitcast.8), custom_call_target="tpu_custom_call" | custom-call | flops 4294967296 | bytes 4194304 | tf_op jit(solution)/shard_map/collect/pallas_call | solution.py:763
Async XLA Ops:
  0.6 0.8 copy-start.1
  1.4 0.8 copy-start.2
  2.1 11.5 %copy-start.5 = (f32[3]{0:T(128)S(1)}, f32[3]{0:T(128)}, u32[]{:S(2)}) copy-start(f32[3]{0:T(128)} %angles_ref.3) | copy-start | bytes 40
  6.3 14.6 %all-to-all-start = ((s32[32,2,128]{2,1,0:T(2,128)}), s32[32,2,128]{2,1,0:T(2,128)S(1)}, u32[]{:S(2)}, u32[]{:S(2)}) async-start(s32[32,2,128]{2,1,0:T(2,128)} %bitcast), calls=%async_computation | async-start | bytes 65536 | tf_op jit(solution)/shard_map/all_to_all | solution.py:793
  20.9 17.8 %copy-start = (f32[3,4096]{1,0:T(4,128)S(1)}, f32[3,4096]{1,0:T(4,128)}, u32[]{:S(2)}) copy-start(f32[3,4096]{1,0:T(4,128)} %cot_ref.1) | copy-start | bytes 147460
  20.9 17.8 %copy-start.3 = (s32[16]{0:T(128)S(1)}, s32[16]{0:T(128)}, u32[]{:S(2)}) copy-start(s32[16]{0:T(128)} %count_ref.1) | copy-start | bytes 196
  20.9 17.8 %copy-start.4 = (s32[16]{0:T(128)S(1)}, s32[16]{0:T(128)}, u32[]{:S(2)}) copy-start(s32[16]{0:T(128)} %order_ref.1) | copy-start | bytes 196

commit v5 on v4

--- a/solution.py
+++ b/solution.py
@@ -16,7 +16,7 @@
 PARTS = (3, 3, 3, 3, 3, 2, 2, 2, 2)
 STEP = LANES // GROUP
 LOG2E = 1.4426950408889634
-BATCH = 4
+BATCH = 8
 VMEM_BYTES = 52 * 1024 * 1024
 
 f32 = jnp.float32
@@ -93,13 +93,13 @@
         put(channel, jnp.sum(jnp.where(mine, value, 0.0), axis=0, keepdims=True))
 
 
-def put_parts(parts_ref, channel, half, value, counts):
-    lows = value.shape[0]
+def put_parts(parts_ref, channel, half, value, counts, lows=None, low=0):
+    lows = lows or value.shape[0]
     first = sum(counts[:channel])
     parts = split_three(value) if counts[channel] == 3 else split_two(value)
     for part, one in enumerate(parts):
-        at = (first + part) * lows
-        parts_ref[at : at + lows, half * LANES : (half + 1) * LANES] = one.astype(bf16)
+        at = (first + part) * lows + low
+        parts_ref[at : at + value.shape[0], half * LANES : (half + 1) * LANES] = one.astype(bf16)
 
 
 def route_kernel(devices, per_owner, own_hbm, loc_hbm, want_ref, back_ref, pos_ref, own_ref, loc_ref, own_s, loc_s, rank_s, sems):
@@ -302,11 +302,13 @@
         for colour in range(3):
             tint_s[pl.ds(8 * colour * rows + row, 8, stride=rows), :] = tints[colour]
         tint_s[pl.ds(24 * rows + row, 3, stride=rows), :] = gauss_ref[56:59, lanes]
-    for half in range(2):
-        at = [pl.ds(index * rows + half, rows // 2, stride=2) for index in range(27)]
+    for part in range(rows // 16):
+        half = part % 2
+        low = part // 2 * 16
+        at = [pl.ds(index * rows + 2 * low + half, 16, stride=2) for index in range(27)]
         columns = [dense_s[one, :] for one in at[:11]]
         for index, value in enumerate(shape_of(columns, rotation, camera_frame)):
-            put_parts(parts_ref, index, half, value, PARTS)
+            put_parts(parts_ref, index, half, value, PARTS, rows // 2, low)
         for colour in range(3):
             total = 0.5
             for inner in range(8):
@@ -314,7 +316,7 @@
             if colour == 2:
                 for inner in range(3):
                     total = total + basis[13 + inner] * tint_s[at[24 + inner], :]
-            put_parts(parts_ref, 6 + colour, half, total, PARTS)
+            put_parts(parts_ref, 6 + colour, half, total, PARTS, rows // 2, low)
 
 
 def pick_kernel(layout, parts_ref, asked_ref, out_ref):
@@ -333,7 +335,7 @@
         pick_slots(parts_ref[...], slots, low_id, high_id, put)
         return 0
 
-    lax.fori_loop(0, layout.count // 2, pick_some, 0, unroll=4)
+    lax.fori_loop(0, layout.count // 2, pick_some, 0, unroll=8)
 
 
 def render_kernel(
@@ -394,7 +396,7 @@
         pick_slots(in_s[...], slots, low_id, high_id, put)
         return 0
 
-    lax.fori_loop(0, slot_rows // 2, pick_in, 0, unroll=4)
+    lax.fori_loop(0, slot_rows // 2, pick_in, 0, unroll=8)
     for block in range(blocks):
         group = block * 8 // chunks
         middle_x, middle_y, live = middles[group]
@@ -608,23 +610,23 @@
         pick_slots(out_s[...], slots, low_id, high_id, put)
         return 0
 
-    lax.fori_loop(0, layout.count // 2, pick_out, 0, unroll=4)
-
-
-def collect_kernel(layout, camera_frame, angles_ref, gauss_ref, asked_ref, terms_ref, grad_ref, lhs_s, rhs_s, total_s, dense_s, out_s):
-    rows = gauss_ref.shape[1] // LANES
-    wide = 2 * LANES
-    lows = gauss_ref.shape[1] // wide
+    lax.fori_loop(0, layout.count // 2, pick_out, 0, unroll=8)
+
+
+def collect_kernel(
+    layout, camera_frame, angles_ref, dense_ref, asked_ref, terms_ref, grad_hbm, lhs_a, lhs_b, rhs_a, rhs_b, total_s, out_s, grad_ref, sems
+):
+    gauss = grad_ref.shape[1]
+    rows = gauss // LANES
+    lows = gauss // WIDE
     low_id = iota((lows, LANES), 0)
-    high_id = iota((wide, LANES), 0)
+    high_id = iota((WIDE, LANES), 0)
     minors = layout.minors()
-    total_s[...] = jnp.zeros(total_s.shape, f32)
-
-    def add(index, _):
-        start = pl.multiple_of(index * 8, 8)
-        asked = asked_ref[pl.ds(start, 8), :]
-        low = asked // wide
-        high = asked % wide
+
+    def build(index, lhs_s, rhs_s):
+        asked = asked_ref[pl.ds(pl.multiple_of(index * 8, 8), 8), :]
+        low = asked // WIDE
+        high = asked % WIDE
         for row in range(8):
             lanes = slice(row * LANES, (row + 1) * LANES)
             mine = low[row : row + 1] == low_id
@@ -634,27 +636,40 @@
                 for part, value in enumerate(split_two(terms_ref[pl.ds(at, 1), :])):
                     first = (part * PROJ + channel) * lows
                     lhs_s[first : first + lows, lanes] = jnp.where(mine, value, 0.0).astype(bf16)
-        total_s[...] += dot_nt(lhs_s[...], rhs_s[...])
+
+    last = layout.count // 8 - 1
+    build(0, lhs_a, rhs_a)
+    total_s[...] = jnp.zeros(total_s.shape, f32)
+
+    def add(index, _):
+        build(2 * index + 1, lhs_b, rhs_b)
+        total_s[...] += dot_nt(lhs_a[...], rhs_a[...])
+        build(jnp.minimum(2 * index + 2, last), lhs_a, rhs_a)
+        total_s[...] += dot_nt(lhs_b[...], rhs_b[...])
         return 0
 
-    lax.fori_loop(0, layout.count // 8, add, 0)
-    spread_columns(gauss_ref, dense_s)
+    lax.fori_loop(0, layout.count // 16, add, 0)
     rotation = view(angles_ref)
     basis = harmonics(*rotation[2])
-    for half in range(2):
+    for part in range(rows // 8):
+        half = part % 2
+        low = part // 2 * 8
         lanes = slice(half * LANES, (half + 1) * LANES)
         sums = [
-            total_s[channel * lows : (channel + 1) * lows, lanes]
-            + total_s[(PROJ + channel) * lows : (PROJ + channel + 1) * lows, lanes]
+            total_s[channel * lows + low : channel * lows + low + 8, lanes]
+            + total_s[(PROJ + channel) * lows + low : (PROJ + channel) * lows + low + 8, lanes]
             for channel in range(PROJ)
         ]
-        columns = tuple(dense_s[pl.ds(index * rows + half, lows, stride=2), :] for index in range(11))
+        columns = tuple(dense_ref[pl.ds(index * rows + 2 * low + half, 8, stride=2), :] for index in range(11))
         _, pullback = jax.vjp(lambda *values: shape_of(values, rotation, camera_frame), *columns)
         grads = pullback(tuple(sums[:6]))
         for index, value in enumerate(tuple(grads) + tuple(sums[6:])):
-            out_s[pl.ds(index * rows + half, lows, stride=2), :] = value
+            out_s[pl.ds(index * rows + 2 * low + half, 8, stride=2), :] = value
     sub = iota((8, LANES), 0)
     patterns = [basis_rows(basis, eighth) for eighth in range(8)]
+    copies = []
+    pieces = sems.shape[0]
+    wide = gauss // pieces
     for row in range(rows):
         lanes = slice(row * LANES, (row + 1) * LANES)
         grad_ref[0:8, lanes] = out_s[pl.ds(row, 8, stride=rows), :]
@@ -672,21 +687,28 @@
                 grad_ref[56:59, lanes] = value[0:3]
             else:
                 grad_ref[8 * eighth : 8 * eighth + 8, lanes] = value
+        if (row + 1) * LANES % wide == 0:
+            piece = len(copies)
+            span = slice(piece * wide, (piece + 1) * wide)
+            copies.append(pltpu.make_async_copy(grad_ref.at[:, span], grad_hbm.at[:, span], sems.at[piece]))
+            copies[-1].start()
+    for copy in copies:
+        copy.wait()
 
 
 VMEM = pl.BlockSpec(memory_space=pltpu.VMEM)
-ANY = pl.BlockSpec(memory_space=pl.ANY)
+HBM = pl.BlockSpec(memory_space=pltpu.HBM)
 SMEM = pl.BlockSpec(memory_space=pltpu.SMEM)
 
 
-def call(kernel, specs, outs, scratch, flops, name):
+def call(kernel, specs, outs, scratch, flops, name, out_spec=VMEM, vmem=VMEM_BYTES):
     return pl.pallas_call(
         kernel,
         in_specs=specs,
-        out_specs=[VMEM] * len(outs),
+        out_specs=[out_spec] * len(outs),
         out_shape=[jax.ShapeDtypeStruct(shape, dtype) for shape, dtype in outs],
         scratch_shapes=[pltpu.VMEM(*one) if isinstance(one, tuple) else one for one in scratch],
-        compiler_params=pltpu.CompilerParams(vmem_limit_bytes=VMEM_BYTES),
+        compiler_params=pltpu.CompilerParams(vmem_limit_bytes=vmem),
         cost_estimate=pl.CostEstimate(flops=flops, bytes_accessed=4 << 20, transcendentals=0),
         name=name,
     )
@@ -700,11 +722,12 @@
     asked = (devices * halves, LANES) if halves else (devices, per_owner)
     return call(
         partial(route_kernel, devices, per_owner),
-        [ANY, ANY],
+        [HBM, HBM],
         [(asked, i32), ((devices, per_owner), i32), ((rows, LANES), i32)],
         [(owners.shape, i32)] * 2 + [((rows, LANES), i32)] * 3 + [pltpu.SemaphoreType.DMA((2,))],
         1 << 30,
         "route",
+        vmem=63 << 20,
     )(owners, locals_)
 
 
@@ -713,11 +736,11 @@
     return call(
         partial(shade_kernel, camera_frame),
         [SMEM, VMEM],
-        [((sum(PARTS) * rows // 2, WIDE), bf16)],
-        [((16 * rows, LANES), f32), ((27 * rows, LANES), f32)],
+        [((sum(PARTS) * rows // 2, WIDE), bf16), ((16 * rows, LANES), f32)],
+        [((27 * rows, LANES), f32)],
         1 << 30,
         "shade",
-    )(view_angles, gaussians)[0]
+    )(view_angles, gaussians)
 
 
 def pick(layout, table, asked):
@@ -757,23 +780,29 @@
     )(list_counts, tile_order, rows, pos, back, cotangent)
 
 
-def collect(layout, camera_frame, view_angles, gaussians, asked, terms):
-    rows = gaussians.shape[1] // LANES
-    lows = gaussians.shape[1] // (2 * LANES)
+def collect(layout, camera_frame, view_angles, shape, dense, asked, terms):
+    rows = shape[1] // LANES
+    lows = shape[1] // WIDE
+    lhs = ((2 * PROJ * lows, 8 * LANES), bf16)
+    rhs = ((WIDE, 8 * LANES), bf16)
     return call(
         partial(collect_kernel, layout, camera_frame),
         [SMEM, VMEM, VMEM, VMEM],
-        [(gaussians.shape, f32)],
+        [(shape, f32)],
         [
-            ((2 * PROJ * lows, 8 * LANES), bf16),
-            ((2 * LANES, 8 * LANES), bf16),
-            ((2 * PROJ * lows, 2 * LANES), f32),
+            lhs,
+            lhs,
+            rhs,
+            rhs,
+            ((2 * PROJ * lows, WIDE), f32),
             ((16 * rows, LANES), f32),
-            ((16 * rows, LANES), f32),
+            (shape, f32),
+            pltpu.SemaphoreType.DMA((8,)),
         ],
         1 << 32,
         "collect",
-    )(view_angles, gaussians, asked, terms)[0]
+        out_spec=HBM,
+    )(view_angles, dense, asked, terms)[0]
 
 
 def swap_rows(layout, devices, rows):
@@ -791,7 +820,7 @@
     layout = Rows(devices, tile_owners.size // devices)
     want, back, pos = route(devices, tile_owners, tile_locals)
     asked = lax.all_to_all(want, "dev", split_axis=0, concat_axis=0, tiled=True)
-    table = shade(camera_frame, view_angles, gaussians)
+    table, dense = shade(camera_frame, view_angles, gaussians)
     if not layout.halves:
         asked = asked.reshape(layout.count, LANES)
     if layout.halves != 2:
@@ -799,7 +828,7 @@
     arrived = swap_rows(layout, devices, pick(layout, table, asked))
     rendered, slot_grads = render(layout, list_counts, tile_order, arrived, pos, back, image_cotangent)
     terms = swap_rows(layout, devices, slot_grads)
-    gradients = collect(layout, camera_frame, view_angles, gaussians, asked, terms)
+    gradients = collect(layout, camera_frame, view_angles, gaussians.shape, dense, asked, terms)
     return (rendered, gradients)
 
 

time: 87.5 us -> 81.4 us (0.930)
  Pallas kernels: 46.8 us -> 42.4 us
  local copies, waits for them, and re-layouts: 1.52 us -> 0.02 us
    pallas_call x1, Pallas kernels: 25.6 us -> 22.5 us  [render(): call(partial(render_kernel, layout), [SMEM, SMEM, VMEM, VMEM, VMEM, VMEM]...]
    unnamed x12, local copies, waits for them, and re-layouts: 1.52 us -> 0.02 us
    pallas_call x1, Pallas kernels: 9.39 us -> 7.97 us  [collect(): call(partial(collect_kernel, layout, camera_frame), [SMEM, VMEM, VMEM, VM...]
  transfers between devices with their start and end apart: 1 -> 1, of which waited for: 1 -> 1; matrix products, arithmetic and copies ran while one was open for 0% -> 0% of each run, Pallas kernels for 3% -> 4%
where the time goes in v5:
time: 81.4 us; the launch traced here: 81.1 us
  Pallas kernels  42.4 us (52%)
  blocking collectives  26.5 us (33%)
  starting transfers between devices  7.3 us (9%)
  waiting for transfers between devices  4.14 us (5%)
    all_to_all x2, blocking collectives, swap_rows(): lax.all_to_all(apart, 'dev', split_axis=0, concat_axis=0, tiled=True)  26.5 us
    pallas_call x1, Pallas kernels, render(): call(partial(render_kernel, layout), [SMEM, SMEM, VMEM, VMEM, VMEM, VMEM]...  22.5 us
    pallas_call x1, Pallas kernels, collect(): call(partial(collect_kernel, layout, camera_frame), [SMEM, VMEM, VMEM, VM...  7.97 us
    all_to_all x1, starting transfers between devices, shards(): asked = lax.all_to_all(want, 'dev', split_axis=0, concat_axis=0, tiled=True)  7.3 us
    pallas_call x1, Pallas kernels, route(): call(partial(route_kernel, devices, per_owner), [HBM, HBM], [(asked, i32)...  4.9 us
    all_to_all x1, waiting for transfers between devices, shards(): asked = lax.all_to_all(want, 'dev', split_axis=0, concat_axis=0, tiled=True)  4.14 us
    pallas_call x1, Pallas kernels, pick(): call(partial(pick_kernel, layout), [VMEM, VMEM], [((PROJ * layout.count,...  3.91 us
    pallas_call x1, Pallas kernels, shade(): call(partial(shade_kernel, camera_frame), [SMEM, VMEM], [((sum(PARTS) * r...  3.09 us
  transfers between devices with their start and end apart: 1, of which 1 were waited for; matrix products, arithmetic and copies ran while one was open for 0% of the time, Pallas kernels for 4%

profile of v5, /device:TPU:0, one launch (start us, length us, event | category | flops | bytes accessed | tf_op | source)
XLA Modules:
  0.0 81.1 jit_solution(640453002043270867)
XLA Ops:
  0.6 0.0 copy-start.3
  0.6 4.9 %route.1 = (s32[64,128]{1,0:T(8,128)}, s32[32,256]{1,0:T(8,128)}, s32[64,128]{1,0:T(8,128)}) custom-call(s32[16,512]{1,0:T(8,128)} %own_hbm.1, s32[16,512]{1,0:T(8,128)} %loc_hbm.1), custom_call_target="tpu_custom_call" | custom-call | flops 1073741824 | bytes 4194304 | tf_op jit(solution)/shard_map/route/pallas_call | solution.py:723
  5.6 7.3 %all-to-all-start = ((s32[32,2,128]{2,1,0:T(2,128)}), s32[32,2,128]{2,1,0:T(2,128)S(1)}, u32[]{:S(2)}, u32[]{:S(2)}) async-start(s32[32,2,128]{2,1,0:T(2,128)} %bitcast.12), calls=%async_computation | async-start | bytes 65536 | tf_op jit(solution)/shard_map/all_to_all | solution.py:822
  12.9 0.0 copy-done.3
  12.9 3.1 %shade.1 = (bf16[736,256]{1,0:T(8,128)(2,1)S(1)}, f32[1024,128]{1,0:T(8,128)S(1)}) custom-call(f32[3]{0:T(128)S(1)} %copy-done.3, f32[59,8192]{1,0:T(8,128)} %gauss_ref.1), custom_call_target="tpu_custom_call" | custom-call | flops 1073741824 | bytes 4194304 | tf_op jit(solution)/shard_map/shade/pallas_call | solution.py:736
  16.0 4.1 %all-to-all-done = s32[32,2,128]{2,1,0:T(2,128)S(1)} async-done(((s32[32,2,128]{2,1,0:T(2,128)}), s32[32,2,128]{2,1,0:T(2,128)S(1)}, u32[]{:S(2)}, u32[]{:S(2)}) %all-to-all-start) | async-done | bytes 32800 | tf_op jit(solution)/shard_map/all_to_all | solution.py:822
  20.1 0.0 copy-start
  20.1 0.0 copy-start.1
  20.1 0.0 copy-start.2
  20.1 0.0 copy-start.4
  20.1 0.0 copy-start.5
  20.1 3.9 %pick.1 = f32[576,128]{1,0:T(8,128)S(1)} custom-call(bf16[736,256]{1,0:T(8,128)(2,1)S(1)} %get-tuple-element.9.parts_ref, s32[64,128]{1,0:T(8,128)S(1)} %bitcast.10), custom_call_target="tpu_custom_call" | custom-call | flops 1073741824 | bytes 4194304 | tf_op jit(solution)/shard_map/pick/pallas_call | solution.py:747
  24.1 13.1 %all_to_all.21 = f32[288,2,128]{2,1,0:T(2,128)S(1)} all-to-all(f32[288,2,128]{2,1,0:T(2,128)S(1)} %bitcast.9), channel_id=1, replica_groups=mesh['dev'=32] {'dev'}, dimensions={0} | all-to-all | bytes 589824 | tf_op jit(solution)/shard_map/all_to_all | solution.py:811
  37.2 0.0 copy-done
  37.2 0.0 copy-done.1
  37.2 0.0 copy-done.2
  37.2 0.0 copy-done.4
  37.2 0.0 copy-done.5
  37.2 22.5 %render.1 = (f32[3,4096]{1,0:T(4,128)}, f32[576,128]{1,0:T(8,128)S(1)}) custom-call(s32[16]{0:T(128)S(1)} %copy-done.1, s32[16]{0:T(128)S(1)} %copy-done.2, f32[576,128]{1,0:T(8,128)S(1)} %bitcast.6, s32[64,128]{1,0:T(8,128)S(1)} %copy-done.5, s32[32,256]{1,0:T(8,128)S(1)} %copy-done.4, f32[3,4096]{1,0:T(4,128)S(1)} %copy-done), custom_call_target="tpu_custom_call" | custom-call | flops 17179869184 | bytes 4194304 | tf_op jit(solution)/shard_map/render/pallas_call | solution.py:761
  59.7 13.4 %all_to_all.22 = f32[288,2,128]{2,1,0:T(2,128)S(1)} all-to-all(f32[288,2,128]{2,1,0:T(2,128)S(1)} %bitcast.7), channel_id=1, replica_groups=mesh['dev'=32] {'dev'}, dimensions={0} | all-to-all | bytes 589824 | tf_op jit(solution)/shard_map/all_to_all | solution.py:811
  73.1 8.0 %collect.1 = f32[59,8192]{1,0:T(8,128)} custom-call(f32[3]{0:T(128)S(1)} %copy-done.3, f32[1024,128]{1,0:T(8,128)S(1)} %get-tuple-element.14.dense_ref, s32[64,128]{1,0:T(8,128)S(1)} %bitcast.11, f32[576,128]{1,0:T(8,128)S(1)} %bitcast.8), custom_call_target="tpu_custom_call" | custom-call | flops 4294967296 | bytes 4194304 | tf_op jit(solution)/shard_map/collect/pallas_call | solution.py:788
Async XLA Ops:
  0.6 12.2 %copy-start.3 = (f32[3]{0:T(128)S(1)}, f32[3]{0:T(128)}, u32[]{:S(2)}) copy-start(f32[3]{0:T(128)} %angles_ref.3) | copy-start | bytes 40
  5.6 14.6 %all-to-all-start = ((s32[32,2,128]{2,1,0:T(2,128)}), s32[32,2,128]{2,1,0:T(2,128)S(1)}, u32[]{:S(2)}, u32[]{:S(2)}) async-start(s32[32,2,128]{2,1,0:T(2,128)} %bitcast.12), calls=%async_computation | async-start | bytes 65536 | tf_op jit(solution)/shard_map/all_to_all | solution.py:822
  20.1 17.1 %copy-start = (f32[3,4096]{1,0:T(4,128)S(1)}, f32[3,4096]{1,0:T(4,128)}, u32[]{:S(2)}) copy-start(f32[3,4096]{1,0:T(4,128)} %cot_ref.1) | copy-start | bytes 147460
  20.1 17.1 %copy-start.1 = (s32[16]{0:T(128)S(1)}, s32[16]{0:T(128)}, u32[]{:S(2)}) copy-start(s32[16]{0:T(128)} %count_ref.1) | copy-start | bytes 196
  20.1 17.1 %copy-start.2 = (s32[16]{0:T(128)S(1)}, s32[16]{0:T(128)}, u32[]{:S(2)}) copy-start(s32[16]{0:T(128)} %order_ref.1) | copy-start | bytes 196
  20.1 17.1 %copy-start.4 = (s32[32,256]{1,0:T(8,128)S(1)}, s32[32,256]{1,0:T(8,128)}, u32[]{:S(2)}) copy-start(s32[32,256]{1,0:T(8,128)} %get-tuple-element.12.back_ref) | copy-start | bytes 98308
  20.1 17.1 %copy-start.5 = (s32[64,128]{1,0:T(8,128)S(1)}, s32[64,128]{1,0:T(8,128)}, u32[]{:S(2)}) copy-start(s32[64,128]{1,0:T(8,128)} %get-tuple-element.11.pos_ref) | copy-start | bytes 98308

commit v6 on v5

--- a/solution.py
+++ b/solution.py
@@ -79,9 +79,16 @@
         return max(self.halves, 1)
 
 
+def narrow(ids):
+    return ids.astype(f32).astype(bf16)
+
+
+def one_hot(ids, every):
+    return jnp.where(narrow(ids) == every, jnp.ones((), bf16), jnp.zeros((), bf16))
+
+
 def pick_slots(parts, slots, low_id, high_id, put):
-    here = jnp.where(slots % WIDE == high_id, 1.0, 0.0).astype(bf16)
-    found = dot(parts, here)
+    found = dot(parts, one_hot(slots % WIDE, high_id))
     mine = slots // WIDE == low_id
     lows = low_id.shape[0]
     first = 0
@@ -140,7 +147,7 @@
     rank_s[...] = rank
 
     owner_id = iota((devices, LANES), 0)
-    rank_id = iota((per_owner, LANES), 0)
+    rank_id = narrow(iota((per_owner, LANES), 0))
     slot_lane = iota((devices, LANES), 1).astype(f32)
 
     def place(index, total):
@@ -166,10 +173,10 @@
                     axis=0,
                 ).astype(bf16)
             )
-            rhs.append(jnp.where(rank_rows[row : row + 1] == rank_id, 1.0, 0.0).astype(bf16))
+            rhs.append(one_hot(rank_rows[row : row + 1], rank_id))
         return total + dot_nt(jnp.concatenate(lhs, axis=1), jnp.concatenate(rhs, axis=1))
 
-    total = lax.fori_loop(0, rows // 8, place, jnp.zeros((4 * devices, per_owner), f32)).astype(i32)
+    total = lax.fori_loop(0, rows // 8, place, jnp.zeros((4 * devices, per_owner), f32), unroll=4).astype(i32)
     want = total[:devices] * LANES + total[devices : 2 * devices]
     halves = per_owner // LANES
     if per_owner % LANES == 0 and halves > 1:
@@ -321,7 +328,7 @@
 
 def pick_kernel(layout, parts_ref, asked_ref, out_ref):
     low_id = iota((parts_ref.shape[0] // sum(PARTS), WIDE), 0)
-    high_id = iota((WIDE, WIDE), 0)
+    high_id = narrow(iota((WIDE, WIDE), 0))
     minors = layout.minors()
 
     def pick_some(index, _):
@@ -335,7 +342,7 @@
         pick_slots(parts_ref[...], slots, low_id, high_id, put)
         return 0
 
-    lax.fori_loop(0, layout.count // 2, pick_some, 0, unroll=8)
+    lax.fori_loop(0, layout.count // 2, pick_some, 0, unroll=16)
 
 
 def render_kernel(
@@ -384,7 +391,7 @@
         for channel in range(PROJ):
             put_parts(in_s, channel, half, layout.half(rows_ref, channel, half), PARTS)
     low_id = iota((slot_rows // 2, WIDE), 0)
-    high_id = iota((WIDE, WIDE), 0)
+    high_id = narrow(iota((WIDE, WIDE), 0))
 
     def pick_in(index, _):
         slots = jnp.concatenate([pos_ref[pl.ds(2 * index + one, 1), :] for one in range(2)], axis=1)
@@ -396,7 +403,7 @@
         pick_slots(in_s[...], slots, low_id, high_id, put)
         return 0
 
-    lax.fori_loop(0, slot_rows // 2, pick_in, 0, unroll=8)
+    lax.fori_loop(0, slot_rows // 2, pick_in, 0, unroll=16)
     for block in range(blocks):
         group = block * 8 // chunks
         middle_x, middle_y, live = middles[group]
@@ -455,6 +462,7 @@
         ).astype(bf16)
 
     own_tile = sub == tile_of
+    own_pair = iota((8, WIDE), 0) == iota((8, WIDE), 1) % GROUP
 
     def evaluate(index, _):
         for group in range(groups):
@@ -464,9 +472,9 @@
             lhs = jnp.concatenate(
                 tints[:3] + [coefs[0:8]] + tints[3:] + [coefs[8:16]] + tints[:3] + [coefs[16:24]], axis=0
             ).astype(bf16)
-            tint_s[chunk] = lhs[0:64]
             both = dot_tn(lhs, rhs_s[group])
             start = pl.multiple_of(chunk * LANES, LANES)
+            tint_s[:, pl.ds(start, LANES)] = lhs[0:64]
             alpha_s[pl.ds(start, LANES), :] = jnp.exp2(both[:, :PIX])
             shade_s[pl.ds(start, LANES), :] = both[:, PIX:]
         return 0
@@ -490,18 +498,20 @@
         out = []
         for group in range(groups):
             chunk = group * chunks + index
-            start = pl.multiple_of(chunk * LANES, LANES)
-            first, second = split_two(weight_s[pl.ds(start, LANES), :])
+            both = pl.ds(pl.multiple_of(chunk * LANES, WIDE), WIDE)
+            first, second = split_two(weight_s[both, :])
             first = first.astype(bf16)
             second = second.astype(bf16)
-            tints = tint_s[chunk]
+            tints = tint_s[:, both]
             by_first = dot(tints, first)
             out.append(images[group] + by_first[0:24] + by_first[32:56] + dot(tints[0:32], second)[0:24])
             by_first = dot_nt(cots[group], first)
             tint_grad = by_first[0:24] + by_first[32:56] + dot_nt(cots[group][0:32], second)[0:24]
             for colour in range(3):
-                own = jnp.where(own_tile, tint_grad[colour * GROUP : (colour + 1) * GROUP], 0.0)
-                sums_s[pl.ds(chunk * 16 + 8 + colour, 1), :] = jnp.sum(own, axis=0, keepdims=True)
+                own = jnp.where(own_pair, tint_grad[colour * GROUP : (colour + 1) * GROUP], 0.0)
+                own = jnp.sum(own, axis=0, keepdims=True)
+                for one in range(2):
+                    sums_s[pl.ds((chunk + one) * 16 + 8 + colour, 1), :] = own[:, one * LANES : (one + 1) * LANES]
         return tuple(out)
 
     def scan_batch(batch, trans):
@@ -510,7 +520,7 @@
         return trans
 
     def paint_batch(batch, images):
-        for one in range(BATCH):
+        for one in range(0, BATCH, 2):
             images = paint(batch * BATCH + one, images)
         return images
 
@@ -533,9 +543,11 @@
     def moment(index):
         for group in range(groups):
             chunk = group * chunks + index
-            first, second = split_two(shade_s[pl.ds(pl.multiple_of(chunk * LANES, LANES), LANES), :])
+            first, second = split_two(shade_s[pl.ds(pl.multiple_of(chunk * LANES, WIDE), WIDE), :])
             found = dot_nt(moments, first.astype(bf16)) + dot_nt(moments, second.astype(bf16))
-            sums_s[pl.ds(pl.multiple_of(chunk * 16, 8), 8), :] = found
+            for one in range(2):
+                start = pl.multiple_of((chunk + one) * 16, 8)
+                sums_s[pl.ds(start, 8), :] = found[:, one * LANES : (one + 1) * LANES]
 
     def rescan(index, behinds):
         out = []
@@ -551,7 +563,7 @@
         return tuple(out)
 
     def moment_batch(batch):
-        for one in range(BATCH):
+        for one in range(0, BATCH, 2):
             moment(batch * BATCH + one)
 
     def rescan_batch(batch, behinds):
@@ -610,7 +622,7 @@
         pick_slots(out_s[...], slots, low_id, high_id, put)
         return 0
 
-    lax.fori_loop(0, layout.count // 2, pick_out, 0, unroll=8)
+    lax.fori_loop(0, layout.count // 2, pick_out, 0, unroll=16)
 
 
 def collect_kernel(
@@ -619,8 +631,8 @@
     gauss = grad_ref.shape[1]
     rows = gauss // LANES
     lows = gauss // WIDE
-    low_id = iota((lows, LANES), 0)
-    high_id = iota((WIDE, LANES), 0)
+    low_id = narrow(iota((lows, LANES), 0))
+    high_id = narrow(iota((WIDE, LANES), 0))
     minors = layout.minors()
 
     def build(index, lhs_s, rhs_s):
@@ -629,13 +641,13 @@
         high = asked % WIDE
         for row in range(8):
             lanes = slice(row * LANES, (row + 1) * LANES)
-            mine = low[row : row + 1] == low_id
-            rhs_s[:, lanes] = jnp.where(high[row : row + 1] == high_id, 1.0, 0.0).astype(bf16)
+            mine = one_hot(low[row : row + 1], low_id)
+            rhs_s[:, lanes] = one_hot(high[row : row + 1], high_id)
             for channel in range(PROJ):
                 at = layout.row(channel, index * (8 // minors) + row // minors, row % minors)
                 for part, value in enumerate(split_two(terms_ref[pl.ds(at, 1), :])):
                     first = (part * PROJ + channel) * lows
-                    lhs_s[first : first + lows, lanes] = jnp.where(mine, value, 0.0).astype(bf16)
+                    lhs_s[first : first + lows, lanes] = mine * value.astype(bf16)
 
     last = layout.count // 8 - 1
     build(0, lhs_a, rhs_a)
@@ -769,7 +781,7 @@
             ((24 * slot_rows, LANES), f32),
             ((24 * groups, PIX), f32),
             ((groups, 96, 2 * PIX), bf16),
-            ((slot_rows, 64, LANES), bf16),
+            ((64, slots), bf16),
             ((slots, PIX), f32),
             ((slots, PIX), f32),
             ((slots, PIX), f32),

time: 81.4 us -> 78.6 us (0.966)
  Pallas kernels: 42.4 us -> 39.4 us
    pallas_call x1, Pallas kernels: 4.9 us -> 3.98 us  [route(): call(partial(route_kernel, devices, per_owner), [HBM, HBM], [(asked, i32)...]
    pallas_call x1, Pallas kernels: 22.5 us -> 21.6 us  [render(): call(partial(render_kernel, layout), [SMEM, SMEM, VMEM, VMEM, VMEM, VMEM]...]
    pallas_call x1, Pallas kernels: 7.97 us -> 7.14 us  [collect(): call(partial(collect_kernel, layout, camera_frame), [SMEM, VMEM, VMEM, VM...]
where the time goes in v6:
time: 78.6 us; the launch traced here: 78.3 us
  Pallas kernels  39.4 us (50%)
  blocking collectives  26.5 us (34%)
  starting transfers between devices  7.3 us (9%)
  waiting for transfers between devices  4.14 us (5%)
  between operations  0.87 us (1%)
    all_to_all x2, blocking collectives, swap_rows(): lax.all_to_all(apart, 'dev', split_axis=0, concat_axis=0, tiled=True)  26.5 us
    pallas_call x1, Pallas kernels, render(): call(partial(render_kernel, layout), [SMEM, SMEM, VMEM, VMEM, VMEM, VMEM]...  21.6 us
    all_to_all x1, starting transfers between devices, shards(): asked = lax.all_to_all(want, 'dev', split_axis=0, concat_axis=0, tiled=True)  7.3 us
    pallas_call x1, Pallas kernels, collect(): call(partial(collect_kernel, layout, camera_frame), [SMEM, VMEM, VMEM, VM...  7.14 us
    all_to_all x1, waiting for transfers between devices, shards(): asked = lax.all_to_all(want, 'dev', split_axis=0, concat_axis=0, tiled=True)  4.14 us
    pallas_call x1, Pallas kernels, route(): call(partial(route_kernel, devices, per_owner), [HBM, HBM], [(asked, i32)...  3.98 us
    pallas_call x1, Pallas kernels, pick(): call(partial(pick_kernel, layout), [VMEM, VMEM], [((PROJ * layout.count,...  3.6 us
    pallas_call x1, Pallas kernels, shade(): call(partial(shade_kernel, camera_frame), [SMEM, VMEM], [((sum(PARTS) * r...  3.09 us
  transfers between devices with their start and end apart: 1, of which 1 were waited for; matrix products, arithmetic and copies ran while one was open for 0% of the time, Pallas kernels for 4%

profile of v6, /device:TPU:0, one launch (start us, length us, event | category | flops | bytes accessed | tf_op | source)
XLA Modules:
  0.0 78.3 jit_solution(6884389931274009458)
XLA Ops:
  0.6 0.0 copy-start.3
  0.6 4.0 %route.1 = (s32[64,128]{1,0:T(8,128)}, s32[32,256]{1,0:T(8,128)}, s32[64,128]{1,0:T(8,128)}) custom-call(s32[16,512]{1,0:T(8,128)} %own_hbm.1, s32[16,512]{1,0:T(8,128)} %loc_hbm.1), custom_call_target="tpu_custom_call" | custom-call | flops 1073741824 | bytes 4194304 | tf_op jit(solution)/shard_map/route/pallas_call | solution.py:735
  4.6 7.3 %all-to-all-start = ((s32[32,2,128]{2,1,0:T(2,128)}), s32[32,2,128]{2,1,0:T(2,128)S(1)}, u32[]{:S(2)}, u32[]{:S(2)}) async-start(s32[32,2,128]{2,1,0:T(2,128)} %bitcast.12), calls=%async_computation | async-start | bytes 65536 | tf_op jit(solution)/shard_map/all_to_all | solution.py:834
  11.9 0.0 copy-done.3
  12.0 3.1 %shade.1 = (bf16[736,256]{1,0:T(8,128)(2,1)S(1)}, f32[1024,128]{1,0:T(8,128)S(1)}) custom-call(f32[3]{0:T(128)S(1)} %copy-done.3, f32[59,8192]{1,0:T(8,128)} %gauss_ref.1), custom_call_target="tpu_custom_call" | custom-call | flops 1073741824 | bytes 4194304 | tf_op jit(solution)/shard_map/shade/pallas_call | solution.py:748
  15.1 4.1 %all-to-all-done = s32[32,2,128]{2,1,0:T(2,128)S(1)} async-done(((s32[32,2,128]{2,1,0:T(2,128)}), s32[32,2,128]{2,1,0:T(2,128)S(1)}, u32[]{:S(2)}, u32[]{:S(2)}) %all-to-all-start) | async-done | bytes 32800 | tf_op jit(solution)/shard_map/all_to_all | solution.py:834
  19.2 0.0 copy-start
  19.2 0.0 copy-start.1
  19.2 0.0 copy-start.2
  19.2 0.0 copy-start.4
  19.2 0.0 copy-start.5
  19.2 3.6 %pick.1 = f32[576,128]{1,0:T(8,128)S(1)} custom-call(bf16[736,256]{1,0:T(8,128)(2,1)S(1)} %get-tuple-element.9.parts_ref, s32[64,128]{1,0:T(8,128)S(1)} %bitcast.10), custom_call_target="tpu_custom_call" | custom-call | flops 1073741824 | bytes 4194304 | tf_op jit(solution)/shard_map/pick/pallas_call | solution.py:759
  22.8 13.1 %all_to_all.21 = f32[288,2,128]{2,1,0:T(2,128)S(1)} all-to-all(f32[288,2,128]{2,1,0:T(2,128)S(1)} %bitcast.9), channel_id=1, replica_groups=mesh['dev'=32] {'dev'}, dimensions={0} | all-to-all | bytes 589824 | tf_op jit(solution)/shard_map/all_to_all | solution.py:823
  35.9 0.0 copy-done
  35.9 0.0 copy-done.1
  35.9 0.0 copy-done.2
  35.9 0.0 copy-done.4
  36.0 0.0 copy-done.5
  36.0 21.6 %render.1 = (f32[3,4096]{1,0:T(4,128)}, f32[576,128]{1,0:T(8,128)S(1)}) custom-call(s32[16]{0:T(128)S(1)} %copy-done.1, s32[16]{0:T(128)S(1)} %copy-done.2, f32[576,128]{1,0:T(8,128)S(1)} %bitcast.6, s32[64,128]{1,0:T(8,128)S(1)} %copy-done.5, s32[32,256]{1,0:T(8,128)S(1)} %copy-done.4, f32[3,4096]{1,0:T(4,128)S(1)} %copy-done), custom_call_target="tpu_custom_call" | custom-call | flops 17179869184 | bytes 4194304 | tf_op jit(solution)/shard_map/render/pallas_call | solution.py:773
  57.6 13.4 %all_to_all.22 = f32[288,2,128]{2,1,0:T(2,128)S(1)} all-to-all(f32[288,2,128]{2,1,0:T(2,128)S(1)} %bitcast.7), channel_id=1, replica_groups=mesh['dev'=32] {'dev'}, dimensions={0} | all-to-all | bytes 589824 | tf_op jit(solution)/shard_map/all_to_all | solution.py:823
  71.0 7.1 %collect.1 = f32[59,8192]{1,0:T(8,128)} custom-call(f32[3]{0:T(128)S(1)} %copy-done.3, f32[1024,128]{1,0:T(8,128)S(1)} %get-tuple-element.14.dense_ref, s32[64,128]{1,0:T(8,128)S(1)} %bitcast.11, f32[576,128]{1,0:T(8,128)S(1)} %bitcast.8), custom_call_target="tpu_custom_call" | custom-call | flops 4294967296 | bytes 4194304 | tf_op jit(solution)/shard_map/collect/pallas_call | solution.py:800
Async XLA Ops:
  0.6 11.3 %copy-start.3 = (f32[3]{0:T(128)S(1)}, f32[3]{0:T(128)}, u32[]{:S(2)}) copy-start(f32[3]{0:T(128)} %angles_ref.3) | copy-start | bytes 40
  4.6 14.6 %all-to-all-start = ((s32[32,2,128]{2,1,0:T(2,128)}), s32[32,2,128]{2,1,0:T(2,128)S(1)}, u32[]{:S(2)}, u32[]{:S(2)}) async-start(s32[32,2,128]{2,1,0:T(2,128)} %bitcast.12), calls=%async_computation | async-start | bytes 65536 | tf_op jit(solution)/shard_map/all_to_all | solution.py:834
  19.2 16.7 %copy-start = (f32[3,4096]{1,0:T(4,128)S(1)}, f32[3,4096]{1,0:T(4,128)}, u32[]{:S(2)}) copy-start(f32[3,4096]{1,0:T(4,128)} %cot_ref.1) | copy-start | bytes 147460
  19.2 16.7 %copy-start.1 = (s32[16]{0:T(128)S(1)}, s32[16]{0:T(128)}, u32[]{:S(2)}) copy-start(s32[16]{0:T(128)} %count_ref.1) | copy-start | bytes 196
  19.2 16.7 %copy-start.2 = (s32[16]{0:T(128)S(1)}, s32[16]{0:T(128)}, u32[]{:S(2)}) copy-start(s32[16]{0:T(128)} %order_ref.1) | copy-start | bytes 196
  19.2 16.8 %copy-start.4 = (s32[32,256]{1,0:T(8,128)S(1)}, s32[32,256]{1,0:T(8,128)}, u32[]{:S(2)}) copy-start(s32[32,256]{1,0:T(8,128)} %get-tuple-element.12.back_ref) | copy-start | bytes 98308
  19.2 16.8 %copy-start.5 = (s32[64,128]{1,0:T(8,128)S(1)}, s32[64,128]{1,0:T(8,128)}, u32[]{:S(2)}) copy-start(s32[64,128]{1,0:T(8,128)} %get-tuple-element.11.pos_ref) | copy-start | bytes 98308

commit v7 on v6

--- a/solution.py
+++ b/solution.py
@@ -16,7 +16,7 @@
 PARTS = (3, 3, 3, 3, 3, 2, 2, 2, 2)
 STEP = LANES // GROUP
 LOG2E = 1.4426950408889634
-BATCH = 8
+AHEAD = 2
 VMEM_BYTES = 52 * 1024 * 1024
 
 f32 = jnp.float32
@@ -176,7 +176,7 @@
             rhs.append(one_hot(rank_rows[row : row + 1], rank_id))
         return total + dot_nt(jnp.concatenate(lhs, axis=1), jnp.concatenate(rhs, axis=1))
 
-    total = lax.fori_loop(0, rows // 8, place, jnp.zeros((4 * devices, per_owner), f32), unroll=4).astype(i32)
+    total = lax.fori_loop(0, rows // 8, place, jnp.zeros((4 * devices, per_owner), f32), unroll=True).astype(i32)
     want = total[:devices] * LANES + total[devices : 2 * devices]
     halves = per_owner // LANES
     if per_owner % LANES == 0 and halves > 1:
@@ -342,7 +342,7 @@
         pick_slots(parts_ref[...], slots, low_id, high_id, put)
         return 0
 
-    lax.fori_loop(0, layout.count // 2, pick_some, 0, unroll=16)
+    lax.fori_loop(0, layout.count // 2, pick_some, 0, unroll=True)
 
 
 def render_kernel(
@@ -403,7 +403,7 @@
         pick_slots(in_s[...], slots, low_id, high_id, put)
         return 0
 
-    lax.fori_loop(0, slot_rows // 2, pick_in, 0, unroll=16)
+    lax.fori_loop(0, slot_rows // 2, pick_in, 0, unroll=True)
     for block in range(blocks):
         group = block * 8 // chunks
         middle_x, middle_y, live = middles[group]
@@ -464,28 +464,25 @@
     own_tile = sub == tile_of
     own_pair = iota((8, WIDE), 0) == iota((8, WIDE), 1) % GROUP
 
-    def evaluate(index, _):
+    def evaluate(index):
         for group in range(groups):
             chunk = group * chunks + index
-            coefs = coef_s[pl.ds(pl.multiple_of(chunk * 24, 8), 24), :]
+            coefs = coef_s[chunk * 24 : (chunk + 1) * 24, :]
             tints = [jnp.where(own_tile, coefs[18 + one : 19 + one], 0.0) for one in range(6)]
             lhs = jnp.concatenate(
                 tints[:3] + [coefs[0:8]] + tints[3:] + [coefs[8:16]] + tints[:3] + [coefs[16:24]], axis=0
             ).astype(bf16)
             both = dot_tn(lhs, rhs_s[group])
-            start = pl.multiple_of(chunk * LANES, LANES)
-            tint_s[:, pl.ds(start, LANES)] = lhs[0:64]
-            alpha_s[pl.ds(start, LANES), :] = jnp.exp2(both[:, :PIX])
-            shade_s[pl.ds(start, LANES), :] = both[:, PIX:]
-        return 0
-
-    lax.fori_loop(0, chunks, evaluate, 0, unroll=BATCH)
+            lanes = slice(chunk * LANES, (chunk + 1) * LANES)
+            tint_s[:, lanes] = lhs[0:64]
+            alpha_s[lanes, :] = jnp.exp2(both[:, :PIX])
+            shade_s[lanes, :] = both[:, PIX:]
 
     def scan(index, trans):
         out = []
         for group in range(groups):
             one = trans[group]
-            start = pl.multiple_of((group * chunks + index) * LANES, LANES)
+            start = (group * chunks + index) * LANES
             for step in range(STEP):
                 alpha = alpha_s[pl.ds(start + step * GROUP, GROUP), :]
                 weight = one * alpha
@@ -498,7 +495,7 @@
         out = []
         for group in range(groups):
             chunk = group * chunks + index
-            both = pl.ds(pl.multiple_of(chunk * LANES, WIDE), WIDE)
+            both = slice(chunk * LANES, chunk * LANES + WIDE)
             first, second = split_two(weight_s[both, :])
             first = first.astype(bf16)
             second = second.astype(bf16)
@@ -511,29 +508,20 @@
                 own = jnp.where(own_pair, tint_grad[colour * GROUP : (colour + 1) * GROUP], 0.0)
                 own = jnp.sum(own, axis=0, keepdims=True)
                 for one in range(2):
-                    sums_s[pl.ds((chunk + one) * 16 + 8 + colour, 1), :] = own[:, one * LANES : (one + 1) * LANES]
+                    sums_s[(chunk + one) * 16 + 8 + colour : (chunk + one) * 16 + 9 + colour, :] = own[:, one * LANES : (one + 1) * LANES]
         return tuple(out)
 
-    def scan_batch(batch, trans):
-        for one in range(BATCH):
-            trans = scan(batch * BATCH + one, trans)
-        return trans
-
-    def paint_batch(batch, images):
-        for one in range(0, BATCH, 2):
-            images = paint(batch * BATCH + one, images)
-        return images
-
-    def forward(batch, state):
-        trans, images = state
-        images = paint_batch(batch - 1, images)
-        return scan_batch(batch, trans), images
-
-    batches = chunks // BATCH
-    trans = scan_batch(0, tuple(jnp.ones((GROUP, PIX), f32) for _ in range(groups)))
+    trans = tuple(jnp.ones((GROUP, PIX), f32) for _ in range(groups))
     images = tuple(jnp.zeros((24, PIX), f32) for _ in range(groups))
-    trans, images = lax.fori_loop(1, batches, forward, (trans, images))
-    images = paint_batch(batches - 1, images)
+    for pair in range(-AHEAD, chunks // 2 + 1):
+        for one in range(2):
+            if pair + AHEAD < chunks // 2:
+                evaluate(2 * (pair + AHEAD) + one)
+        for one in range(2):
+            if 0 <= pair < chunks // 2:
+                trans = scan(2 * pair + one, trans)
+        if pair > 0:
+            images = paint(2 * (pair - 1), images)
     for group in range(groups):
         for colour in range(3):
             for tile in range(GROUP):
@@ -543,17 +531,17 @@
     def moment(index):
         for group in range(groups):
             chunk = group * chunks + index
-            first, second = split_two(shade_s[pl.ds(pl.multiple_of(chunk * LANES, WIDE), WIDE), :])
+            first, second = split_two(shade_s[slice(chunk * LANES, chunk * LANES + WIDE), :])
             found = dot_nt(moments, first.astype(bf16)) + dot_nt(moments, second.astype(bf16))
             for one in range(2):
-                start = pl.multiple_of((chunk + one) * 16, 8)
-                sums_s[pl.ds(start, 8), :] = found[:, one * LANES : (one + 1) * LANES]
+                start = (chunk + one) * 16
+                sums_s[start : start + 8, :] = found[:, one * LANES : (one + 1) * LANES]
 
     def rescan(index, behinds):
         out = []
         for group in range(groups):
             behind = behinds[group]
-            start = pl.multiple_of((group * chunks + index) * LANES, LANES)
+            start = (group * chunks + index) * LANES
             for step in reversed(range(STEP)):
                 at = pl.ds(start + step * GROUP, GROUP)
                 ahead = shade_s[at, :] - behind
@@ -562,22 +550,13 @@
             out.append(behind)
         return tuple(out)
 
-    def moment_batch(batch):
-        for one in range(0, BATCH, 2):
-            moment(batch * BATCH + one)
-
-    def rescan_batch(batch, behinds):
-        for one in reversed(range(BATCH)):
-            behinds = rescan(batch * BATCH + one, behinds)
-        return behinds
-
-    def backward(index, behinds):
-        moment_batch(batches - index)
-        return rescan_batch(batches - 1 - index, behinds)
-
-    behinds = rescan_batch(batches - 1, tuple(jnp.zeros((GROUP, PIX), f32) for _ in range(groups)))
-    lax.fori_loop(1, batches, backward, behinds)
-    moment_batch(0)
+    behinds = tuple(jnp.zeros((GROUP, PIX), f32) for _ in range(groups))
+    for pair in reversed(range(-1, chunks // 2)):
+        for one in reversed(range(2)):
+            if pair >= 0:
+                behinds = rescan(2 * pair + one, behinds)
+        if pair + 1 < chunks // 2:
+            moment(2 * (pair + 1))
 
     slot_s = coef_s
     for block in range(blocks):
@@ -622,11 +601,11 @@
         pick_slots(out_s[...], slots, low_id, high_id, put)
         return 0
 
-    lax.fori_loop(0, layout.count // 2, pick_out, 0, unroll=16)
+    lax.fori_loop(0, layout.count // 2, pick_out, 0, unroll=True)
 
 
 def collect_kernel(
-    layout, camera_frame, angles_ref, dense_ref, asked_ref, terms_ref, grad_hbm, lhs_a, lhs_b, rhs_a, rhs_b, total_s, out_s, grad_ref, sems
+    layout, camera_frame, angles_ref, dense_ref, asked_ref, terms_ref, grad_hbm, lhs_s, rhs_s, total_s, out_s, grad_ref, sems
 ):
     gauss = grad_ref.shape[1]
     rows = gauss // LANES
@@ -635,32 +614,22 @@
     high_id = narrow(iota((WIDE, LANES), 0))
     minors = layout.minors()
 
-    def build(index, lhs_s, rhs_s):
-        asked = asked_ref[pl.ds(pl.multiple_of(index * 8, 8), 8), :]
+    for index in range(layout.count // 8):
+        asked = asked_ref[8 * index : 8 * index + 8, :]
         low = asked // WIDE
         high = asked % WIDE
         for row in range(8):
-            lanes = slice(row * LANES, (row + 1) * LANES)
+            lanes = slice((8 * index + row) * LANES, (8 * index + row + 1) * LANES)
             mine = one_hot(low[row : row + 1], low_id)
             rhs_s[:, lanes] = one_hot(high[row : row + 1], high_id)
             for channel in range(PROJ):
-                at = layout.row(channel, index * (8 // minors) + row // minors, row % minors)
-                for part, value in enumerate(split_two(terms_ref[pl.ds(at, 1), :])):
+                at = layout.row(channel, (8 * index + row) // minors, row % minors)
+                for part, value in enumerate(split_two(terms_ref[at : at + 1, :])):
                     first = (part * PROJ + channel) * lows
                     lhs_s[first : first + lows, lanes] = mine * value.astype(bf16)
-
-    last = layout.count // 8 - 1
-    build(0, lhs_a, rhs_a)
-    total_s[...] = jnp.zeros(total_s.shape, f32)
-
-    def add(index, _):
-        build(2 * index + 1, lhs_b, rhs_b)
-        total_s[...] += dot_nt(lhs_a[...], rhs_a[...])
-        build(jnp.minimum(2 * index + 2, last), lhs_a, rhs_a)
-        total_s[...] += dot_nt(lhs_b[...], rhs_b[...])
-        return 0
-
-    lax.fori_loop(0, layout.count // 16, add, 0)
+        lanes = slice(8 * index * LANES, 8 * (index + 1) * LANES)
+        found = dot_nt(lhs_s[:, lanes], rhs_s[:, lanes])
+        total_s[...] = found if index == 0 else total_s[...] + found
     rotation = view(angles_ref)
     basis = harmonics(*rotation[2])
     for part in range(rows // 8):
@@ -795,17 +764,13 @@
 def collect(layout, camera_frame, view_angles, shape, dense, asked, terms):
     rows = shape[1] // LANES
     lows = shape[1] // WIDE
-    lhs = ((2 * PROJ * lows, 8 * LANES), bf16)
-    rhs = ((WIDE, 8 * LANES), bf16)
     return call(
         partial(collect_kernel, layout, camera_frame),
         [SMEM, VMEM, VMEM, VMEM],
         [(shape, f32)],
         [
-            lhs,
-            lhs,
-            rhs,
-            rhs,
+            ((2 * PROJ * lows, layout.count * LANES), bf16),
+            ((WIDE, layout.count * LANES), bf16),
             ((2 * PROJ * lows, WIDE), f32),
             ((16 * rows, LANES), f32),
             (shape, f32),

time: 78.6 us -> 71.3 us (0.907)
  Pallas kernels: 39.4 us -> 32.1 us
    pallas_call x1, Pallas kernels: 21.6 us -> 14.8 us  [render(): call(partial(render_kernel, layout), [SMEM, SMEM, VMEM, VMEM, VMEM, VMEM]...]
where the time goes in v7:
time: 71.3 us; the launch traced here: 71 us
  Pallas kernels  32.1 us (45%)
  blocking collectives  26.5 us (37%)
  starting transfers between devices  7.3 us (10%)
  waiting for transfers between devices  4.14 us (6%)
  between operations  0.9 us (1%)
    all_to_all x2, blocking collectives, swap_rows(): lax.all_to_all(apart, 'dev', split_axis=0, concat_axis=0, tiled=True)  26.5 us
    pallas_call x1, Pallas kernels, render(): call(partial(render_kernel, layout), [SMEM, SMEM, VMEM, VMEM, VMEM, VMEM]...  14.8 us
    all_to_all x1, starting transfers between devices, shards(): asked = lax.all_to_all(want, 'dev', split_axis=0, concat_axis=0, tiled=True)  7.3 us
    pallas_call x1, Pallas kernels, collect(): call(partial(collect_kernel, layout, camera_frame), [SMEM, VMEM, VMEM, VM...  6.95 us
    all_to_all x1, waiting for transfers between devices, shards(): asked = lax.all_to_all(want, 'dev', split_axis=0, concat_axis=0, tiled=True)  4.14 us
    pallas_call x1, Pallas kernels, route(): call(partial(route_kernel, devices, per_owner), [HBM, HBM], [(asked, i32)...  3.98 us
    pallas_call x1, Pallas kernels, pick(): call(partial(pick_kernel, layout), [VMEM, VMEM], [((PROJ * layout.count,...  3.33 us
    pallas_call x1, Pallas kernels, shade(): call(partial(shade_kernel, camera_frame), [SMEM, VMEM], [((sum(PARTS) * r...  3.09 us
  transfers between devices with their start and end apart: 1, of which 1 were waited for; matrix products, arithmetic and copies ran while one was open for 0% of the time, Pallas kernels for 4%

profile of v7, /device:TPU:0, one launch (start us, length us, event | category | flops | bytes accessed | tf_op | source)
XLA Modules:
  0.0 71.0 jit_solution(9829813439771927685)
XLA Ops:
  0.6 0.0 copy-start.3
  0.6 4.0 %route.1 = (s32[64,128]{1,0:T(8,128)}, s32[32,256]{1,0:T(8,128)}, s32[64,128]{1,0:T(8,128)}) custom-call(s32[16,512]{1,0:T(8,128)} %own_hbm.1, s32[16,512]{1,0:T(8,128)} %loc_hbm.1), custom_call_target="tpu_custom_call" | custom-call | flops 1073741824 | bytes 4194304 | tf_op jit(solution)/shard_map/route/pallas_call | solution.py:704
  4.6 7.3 %all-to-all-start = ((s32[32,2,128]{2,1,0:T(2,128)}), s32[32,2,128]{2,1,0:T(2,128)S(1)}, u32[]{:S(2)}, u32[]{:S(2)}) async-start(s32[32,2,128]{2,1,0:T(2,128)} %bitcast.12), calls=%async_computation | async-start | bytes 65536 | tf_op jit(solution)/shard_map/all_to_all | solution.py:799
  11.9 0.0 copy-done.3
  11.9 3.1 %shade.1 = (bf16[736,256]{1,0:T(8,128)(2,1)S(1)}, f32[1024,128]{1,0:T(8,128)S(1)}) custom-call(f32[3]{0:T(128)S(1)} %copy-done.3, f32[59,8192]{1,0:T(8,128)} %gauss_ref.1), custom_call_target="tpu_custom_call" | custom-call | flops 1073741824 | bytes 4194304 | tf_op jit(solution)/shard_map/shade/pallas_call | solution.py:717
  15.0 4.1 %all-to-all-done = s32[32,2,128]{2,1,0:T(2,128)S(1)} async-done(((s32[32,2,128]{2,1,0:T(2,128)}), s32[32,2,128]{2,1,0:T(2,128)S(1)}, u32[]{:S(2)}, u32[]{:S(2)}) %all-to-all-start) | async-done | bytes 32800 | tf_op jit(solution)/shard_map/all_to_all | solution.py:799
  19.2 0.0 copy-start
  19.2 0.0 copy-start.1
  19.2 0.0 copy-start.2
  19.2 0.0 copy-start.4
  19.2 0.0 copy-start.5
  19.2 3.3 %pick.1 = f32[576,128]{1,0:T(8,128)S(1)} custom-call(bf16[736,256]{1,0:T(8,128)(2,1)S(1)} %get-tuple-element.9.parts_ref, s32[64,128]{1,0:T(8,128)S(1)} %bitcast.10), custom_call_target="tpu_custom_call" | custom-call | flops 1073741824 | bytes 4194304 | tf_op jit(solution)/shard_map/pick/pallas_call | solution.py:728
  22.5 13.1 %all_to_all.21 = f32[288,2,128]{2,1,0:T(2,128)S(1)} all-to-all(f32[288,2,128]{2,1,0:T(2,128)S(1)} %bitcast.9), channel_id=1, replica_groups=mesh['dev'=32] {'dev'}, dimensions={0} | all-to-all | bytes 589824 | tf_op jit(solution)/shard_map/all_to_all | solution.py:788
  35.7 0.0 copy-done
  35.7 0.0 copy-done.1
  35.7 0.0 copy-done.2
  35.7 0.0 copy-done.4
  35.7 0.0 copy-done.5
  35.7 14.8 %render.1 = (f32[3,4096]{1,0:T(4,128)}, f32[576,128]{1,0:T(8,128)S(1)}) custom-call(s32[16]{0:T(128)S(1)} %copy-done.1, s32[16]{0:T(128)S(1)} %copy-done.2, f32[576,128]{1,0:T(8,128)S(1)} %bitcast.6, s32[64,128]{1,0:T(8,128)S(1)} %copy-done.5, s32[32,256]{1,0:T(8,128)S(1)} %copy-done.4, f32[3,4096]{1,0:T(4,128)S(1)} %copy-done), custom_call_target="tpu_custom_call" | custom-call | flops 17179869184 | bytes 4194304 | tf_op jit(solution)/shard_map/render/pallas_call | solution.py:742
  50.5 13.4 %all_to_all.22 = f32[288,2,128]{2,1,0:T(2,128)S(1)} all-to-all(f32[288,2,128]{2,1,0:T(2,128)S(1)} %bitcast.7), channel_id=1, replica_groups=mesh['dev'=32] {'dev'}, dimensions={0} | all-to-all | bytes 589824 | tf_op jit(solution)/shard_map/all_to_all | solution.py:788
  63.9 6.9 %collect.1 = f32[59,8192]{1,0:T(8,128)} custom-call(f32[3]{0:T(128)S(1)} %copy-done.3, f32[1024,128]{1,0:T(8,128)S(1)} %get-tuple-element.14.dense_ref, s32[64,128]{1,0:T(8,128)S(1)} %bitcast.11, f32[576,128]{1,0:T(8,128)S(1)} %bitcast.8), custom_call_target="tpu_custom_call" | custom-call | flops 4294967296 | bytes 4194304 | tf_op jit(solution)/shard_map/collect/pallas_call | solution.py:767
Async XLA Ops:
  0.6 11.3 %copy-start.3 = (f32[3]{0:T(128)S(1)}, f32[3]{0:T(128)}, u32[]{:S(2)}) copy-start(f32[3]{0:T(128)} %angles_ref.3) | copy-start | bytes 40
  4.6 14.6 %all-to-all-start = ((s32[32,2,128]{2,1,0:T(2,128)}), s32[32,2,128]{2,1,0:T(2,128)S(1)}, u32[]{:S(2)}, u32[]{:S(2)}) async-start(s32[32,2,128]{2,1,0:T(2,128)} %bitcast.12), calls=%async_computation | async-start | bytes 65536 | tf_op jit(solution)/shard_map/all_to_all | solution.py:799
  19.2 16.5 %copy-start = (f32[3,4096]{1,0:T(4,128)S(1)}, f32[3,4096]{1,0:T(4,128)}, u32[]{:S(2)}) copy-start(f32[3,4096]{1,0:T(4,128)} %cot_ref.1) | copy-start | bytes 147460
  19.2 16.5 %copy-start.1 = (s32[16]{0:T(128)S(1)}, s32[16]{0:T(128)}, u32[]{:S(2)}) copy-start(s32[16]{0:T(128)} %count_ref.1) | copy-start | bytes 196
  19.2 16.5 %copy-start.2 = (s32[16]{0:T(128)S(1)}, s32[16]{0:T(128)}, u32[]{:S(2)}) copy-start(s32[16]{0:T(128)} %order_ref.1) | copy-start | bytes 196
  19.2 16.5 %copy-start.4 = (s32[32,256]{1,0:T(8,128)S(1)}, s32[32,256]{1,0:T(8,128)}, u32[]{:S(2)}) copy-start(s32[32,256]{1,0:T(8,128)} %get-tuple-element.12.back_ref) | copy-start | bytes 98308
  19.2 16.5 %copy-start.5 = (s32[64,128]{1,0:T(8,128)S(1)}, s32[64,128]{1,0:T(8,128)}, u32[]{:S(2)}) copy-start(s32[64,128]{1,0:T(8,128)} %get-tuple-element.11.pos_ref) | copy-start | bytes 98308

commit v8 on v7

--- a/solution.py
+++ b/solution.py
@@ -67,13 +67,11 @@
             return channel * self.count + major
         return major * (PROJ * halves) + channel * halves + minor
 
-    def half(self, ref, channel, half):
-        halves = self.halves
-        if halves == 0:
-            return ref[pl.ds(channel * self.count + half, self.count // 2, stride=2), :]
-        return jnp.concatenate(
-            [ref[pl.ds(self.row(channel, one // halves, one % halves), 1), :] for one in range(half, self.count, 2)], axis=0
-        ) if halves != 2 else ref[pl.ds(channel * 2 + half, self.count // 2, stride=2 * PROJ), :]
+    def half(self, channel, half):
+        if self.halves == 0:
+            return pl.ds(channel * self.count + half, self.count // 2, stride=2)
+        assert self.halves <= 2
+        return pl.ds(self.row(channel, half // self.halves, half % self.halves), self.count // 2, stride=2 * PROJ)
 
     def minors(self):
         return max(self.halves, 1)
@@ -87,12 +85,23 @@
     return jnp.where(narrow(ids) == every, jnp.ones((), bf16), jnp.zeros((), bf16))
 
 
-def pick_slots(parts, slots, low_id, high_id, put):
-    found = dot(parts, one_hot(slots % WIDE, high_id))
+def put_terms(lhs_s, channel, lanes, row, mine):
+    lows = mine.shape[0]
+    row = jnp.broadcast_to(row, (16, LANES))
+    first = row.astype(bf16)
+    second = (row - first.astype(f32)).astype(bf16)
+    for part, value in enumerate((first, second)):
+        for low in range(0, lows, 16):
+            start = (part * PROJ + channel) * lows + low
+            lhs_s[start : start + 16, lanes] = mine[low : low + 16] * value
+
+
+def pick_slots(parts, hot, slots, low_id, put):
+    found = dot(parts, hot)
     mine = slots // WIDE == low_id
     lows = low_id.shape[0]
     first = 0
-    for channel, count in enumerate(PARTS if parts.shape[0] == sum(PARTS) * lows else (2,) * PROJ):
+    for channel, count in enumerate(PARTS):
         value = found[first * lows : (first + 1) * lows]
         for part in range(1, count):
             value = value + found[(first + part) * lows : (first + part + 1) * lows]
@@ -109,27 +118,17 @@
         parts_ref[at : at + value.shape[0], half * LANES : (half + 1) * LANES] = one.astype(bf16)
 
 
-def route_kernel(devices, per_owner, own_hbm, loc_hbm, want_ref, back_ref, pos_ref, own_ref, loc_ref, own_s, loc_s, rank_s, sems):
+def route_kernel(devices, per_owner, own_hbm, loc_hbm, want_ref, pos_ref, own_ref, loc_ref, sems):
     copies = [pltpu.make_async_copy(own_hbm, own_ref, sems.at[0]), pltpu.make_async_copy(loc_hbm, loc_ref, sems.at[1])]
     for copy in copies:
         copy.start()
     for copy in copies:
         copy.wait()
-    rows = own_s.shape[0]
+    tiles = own_ref.shape[0]
     blocks = own_ref.shape[1] // LANES
-    lane = iota((8, LANES), 1)
-    from_slot = iota((8, LANES), 0) * STEP + lane // GROUP
-    tile_of = lane % GROUP
-    for group in range(own_ref.shape[0] // GROUP):
-        for block in range(blocks):
-            for source, target in ((own_ref, own_s), (loc_ref, loc_s)):
-                part = source[group * GROUP : (group + 1) * GROUP, block * LANES : (block + 1) * LANES]
-                out = jnp.zeros((8, LANES), i32)
-                for tile in range(GROUP):
-                    out = jnp.where(tile_of == tile, lane_pick(part[tile : tile + 1], from_slot), out)
-                start = (group * blocks + block) * 8
-                target[start : start + 8, :] = out
-    owner = own_s[...]
+    rows = tiles * blocks
+    owner = jnp.concatenate([own_ref[:, block * LANES : (block + 1) * LANES] for block in range(blocks)], axis=0)
+    local = jnp.concatenate([loc_ref[:, block * LANES : (block + 1) * LANES] for block in range(blocks)], axis=0)
     left = (iota((LANES, 2 * LANES), 0) < iota((LANES, 2 * LANES), 1)) | (iota((LANES, 2 * LANES), 1) >= LANES)
     above = iota((rows, rows), 1) < iota((rows, rows), 0)
     hits = jnp.concatenate([jnp.where(owner == one, 1.0, 0.0).astype(bf16) for one in range(devices)], axis=0)
@@ -143,48 +142,45 @@
         here = sums[one * rows : (one + 1) * rows, :LANES] + base[:, one * LANES : (one + 1) * LANES]
         rank = jnp.where(owner == one, here, rank)
     rank = rank.astype(i32)
-    pos_ref[...] = owner * per_owner + rank
-    rank_s[...] = rank
+    place = owner * per_owner + rank
 
     owner_id = iota((devices, LANES), 0)
     rank_id = narrow(iota((per_owner, LANES), 0))
-    slot_lane = iota((devices, LANES), 1).astype(f32)
-
-    def place(index, total):
-        start = pl.multiple_of(index * 8, 8)
-        own_rows = own_s[pl.ds(start, 8), :]
-        loc_rows = loc_s[pl.ds(start, 8), :]
-        rank_rows = rank_s[pl.ds(start, 8), :]
-        high_rows = (loc_rows // LANES).astype(f32)
-        low_rows = (loc_rows % LANES).astype(f32)
+    high = (local // LANES).astype(f32)
+    low = (local % LANES).astype(f32)
+    total = jnp.zeros((2 * devices, per_owner), f32)
+    for start in range(0, rows, 8):
         lhs = []
         rhs = []
-        for row in range(8):
-            mine = own_rows[row : row + 1] == owner_id
-            number = (start + row).astype(f32)
+        for row in range(start, start + 8):
+            mine = owner[row : row + 1] == owner_id
             lhs.append(
                 jnp.concatenate(
-                    [
-                        jnp.where(mine, high_rows[row : row + 1], 0.0),
-                        jnp.where(mine, low_rows[row : row + 1], 0.0),
-                        jnp.where(mine, number, 0.0),
-                        jnp.where(mine, slot_lane, 0.0),
-                    ],
-                    axis=0,
+                    [jnp.where(mine, high[row : row + 1], 0.0), jnp.where(mine, low[row : row + 1], 0.0)], axis=0
                 ).astype(bf16)
             )
-            rhs.append(one_hot(rank_rows[row : row + 1], rank_id))
-        return total + dot_nt(jnp.concatenate(lhs, axis=1), jnp.concatenate(rhs, axis=1))
-
-    total = lax.fori_loop(0, rows // 8, place, jnp.zeros((4 * devices, per_owner), f32), unroll=True).astype(i32)
-    want = total[:devices] * LANES + total[devices : 2 * devices]
+            rhs.append(one_hot(rank[row : row + 1], rank_id))
+        total = total + dot_nt(jnp.concatenate(lhs, axis=1), jnp.concatenate(rhs, axis=1))
+    total = total.astype(i32)
+    want = total[:devices] * LANES + total[devices:]
     halves = per_owner // LANES
     if per_owner % LANES == 0 and halves > 1:
         for half in range(halves):
             want_ref[pl.ds(half, devices, stride=halves), :] = want[:, half * LANES : (half + 1) * LANES]
     else:
         want_ref[...] = want
-    back_ref[...] = total[2 * devices : 3 * devices] * LANES + total[3 * devices :]
+
+    lane = iota((8, LANES), 1)
+    from_slot = iota((8, LANES), 0) * STEP + lane // GROUP
+    tile_of = lane % GROUP
+    for group in range(tiles // GROUP):
+        for block in range(blocks):
+            part = place[block * tiles + group * GROUP : block * tiles + (group + 1) * GROUP]
+            out = jnp.zeros((8, LANES), i32)
+            for tile in range(GROUP):
+                out = jnp.where(tile_of == tile, lane_pick(part[tile : tile + 1], from_slot), out)
+            start = (group * blocks + block) * 8
+            pos_ref[start : start + 8, :] = out
 
 
 def view(angles_ref):
@@ -331,18 +327,15 @@
     high_id = narrow(iota((WIDE, WIDE), 0))
     minors = layout.minors()
 
-    def pick_some(index, _):
-        slots = jnp.concatenate([asked_ref[pl.ds(2 * index + one, 1), :] for one in range(2)], axis=1)
+    for index in range(layout.count // 2):
+        slots = jnp.concatenate([asked_ref[2 * index + one : 2 * index + one + 1, :] for one in range(2)], axis=1)
 
         def put(channel, value):
             for one in range(2):
                 at = layout.row(channel, (2 * index + one) // minors, (2 * index + one) % minors)
-                out_ref[pl.ds(at, 1), :] = value[:, one * LANES : (one + 1) * LANES]
-
-        pick_slots(parts_ref[...], slots, low_id, high_id, put)
-        return 0
-
-    lax.fori_loop(0, layout.count // 2, pick_some, 0, unroll=True)
+                out_ref[at : at + 1, :] = value[:, one * LANES : (one + 1) * LANES]
+
+        pick_slots(parts_ref[...], one_hot(slots % WIDE, high_id), slots, low_id, put)
 
 
 def render_kernel(
@@ -351,12 +344,13 @@
     order_ref,
     rows_ref,
     pos_ref,
-    back_ref,
     cot_ref,
     image_ref,
     out_ref,
     in_s,
-    out_s,
+    hot_s,
+    lhs_s,
+    total_s,
     raw_s,
     coef_s,
     cot_s,
@@ -389,22 +383,23 @@
 
     for half in range(2):
         for channel in range(PROJ):
-            put_parts(in_s, channel, half, layout.half(rows_ref, channel, half), PARTS)
+            put_parts(in_s, channel, half, rows_ref[layout.half(channel, half), :], PARTS)
     low_id = iota((slot_rows // 2, WIDE), 0)
     high_id = narrow(iota((WIDE, WIDE), 0))
 
-    def pick_in(index, _):
-        slots = jnp.concatenate([pos_ref[pl.ds(2 * index + one, 1), :] for one in range(2)], axis=1)
+    def pick_in(row):
+        slots = jnp.concatenate([pos_ref[row + one : row + one + 1, :] for one in range(2)], axis=1)
+        hot = one_hot(slots % WIDE, high_id)
+        hot_s[:, row * LANES : (row + 2) * LANES] = hot
 
         def put(channel, value):
             for one in range(2):
-                raw_s[pl.ds(channel * slot_rows + 2 * index + one, 1), :] = value[:, one * LANES : (one + 1) * LANES]
-
-        pick_slots(in_s[...], slots, low_id, high_id, put)
-        return 0
-
-    lax.fori_loop(0, slot_rows // 2, pick_in, 0, unroll=True)
-    for block in range(blocks):
+                at = channel * slot_rows + row + one
+                raw_s[at : at + 1, :] = value[:, one * LANES : (one + 1) * LANES]
+
+        pick_slots(in_s[...], hot, slots, low_id, put)
+
+    def quadratics(block):
         group = block * 8 // chunks
         middle_x, middle_y, live = middles[group]
         found = [
@@ -513,7 +508,19 @@
 
     trans = tuple(jnp.ones((GROUP, PIX), f32) for _ in range(groups))
     images = tuple(jnp.zeros((24, PIX), f32) for _ in range(groups))
+    per_group = chunks // 8
+    for block in range(0, blocks, per_group):
+        for row in range(0, 8, 2):
+            pick_in(8 * block + row)
+        quadratics(block)
     for pair in range(-AHEAD, chunks // 2 + 1):
+        step = pair + AHEAD + 4
+        if 4 <= step < chunks // 2:
+            for group in range(groups):
+                block = group * per_group + step // 4
+                pick_in(8 * block + step % 4 * 2)
+                if step % 4 == 3:
+                    quadratics(block)
         for one in range(2):
             if pair + AHEAD < chunks // 2:
                 evaluate(2 * (pair + AHEAD) + one)
@@ -550,18 +557,11 @@
             out.append(behind)
         return tuple(out)
 
-    behinds = tuple(jnp.zeros((GROUP, PIX), f32) for _ in range(groups))
-    for pair in reversed(range(-1, chunks // 2)):
-        for one in reversed(range(2)):
-            if pair >= 0:
-                behinds = rescan(2 * pair + one, behinds)
-        if pair + 1 < chunks // 2:
-            moment(2 * (pair + 1))
-
-    slot_s = coef_s
-    for block in range(blocks):
+    slot_s = raw_s
+    owner_id = narrow(iota((slot_rows // 2, LANES), 0))
+
+    def send(block):
         middle_x, middle_y, _ = middles[block * 8 // chunks]
-        at = slice(8 * block, 8 * block + 8)
         raw = [raw_s[channel * slot_rows + 8 * block : channel * slot_rows + 8 * block + 8, :] for channel in range(6)]
         (sum_xx, sum_xy, sum_yy, sum_x, sum_y, sum_one) = [
             sums_s[pl.ds(8 * block * 16 + index, 8, stride=16), :] for index in range(6)
@@ -581,27 +581,33 @@
         for channel, value in enumerate(grads):
             slot_s[channel * slot_rows + 8 * block : channel * slot_rows + 8 * block + 8, :] = value
 
-    for half in range(2):
-        for channel in range(PROJ):
-            value = slot_s[pl.ds(channel * slot_rows + half, slot_rows // 2, stride=2), :]
-            put_parts(out_s, channel, half, value, (2,) * PROJ)
-    minors = layout.minors()
-
-    def pick_out(index, _):
-        if layout.halves == 2:
-            slots = back_ref[pl.ds(index, 1), :]
-        else:
-            slots = jnp.concatenate([back_ref[pl.ds(2 * index + one, 1), :] for one in range(2)], axis=1)
-
-        def put(channel, value):
-            for one in range(2):
-                at = layout.row(channel, (2 * index + one) // minors, (2 * index + one) % minors)
-                out_ref[pl.ds(at, 1), :] = value[:, one * LANES : (one + 1) * LANES]
-
-        pick_slots(out_s[...], slots, low_id, high_id, put)
-        return 0
-
-    lax.fori_loop(0, layout.count // 2, pick_out, 0, unroll=True)
+        for row in range(8 * block, 8 * block + 8):
+            lanes = slice(row * LANES, (row + 1) * LANES)
+            mine = one_hot(pos_ref[row : row + 1, :] // WIDE, owner_id)
+            for channel in range(PROJ):
+                at = channel * slot_rows + row
+                put_terms(lhs_s, channel, lanes, slot_s[at : at + 1, :], mine)
+        lanes = slice(8 * block * LANES, 8 * (block + 1) * LANES)
+        found = dot_nt(lhs_s[:, lanes], hot_s[:, lanes])
+        total_s[...] = found if block == per_group - 1 else total_s[...] + found
+
+    behinds = tuple(jnp.zeros((GROUP, PIX), f32) for _ in range(groups))
+    for pair in reversed(range(-1, chunks // 2)):
+        for one in reversed(range(2)):
+            if pair >= 0:
+                behinds = rescan(2 * pair + one, behinds)
+        if pair + 1 < chunks // 2:
+            moment(2 * (pair + 1))
+            if (pair + 1) % 4 == 0:
+                for group in range(groups):
+                    send(group * per_group + (pair + 1) // 4)
+
+    lows = slot_rows // 2
+    for channel in range(PROJ):
+        value = total_s[channel * lows : (channel + 1) * lows, :]
+        value = value + total_s[(PROJ + channel) * lows : (PROJ + channel + 1) * lows, :]
+        for half in range(2):
+            out_ref[layout.half(channel, half), :] = value[:, half * LANES : (half + 1) * LANES]
 
 
 def collect_kernel(
@@ -624,9 +630,7 @@
             rhs_s[:, lanes] = one_hot(high[row : row + 1], high_id)
             for channel in range(PROJ):
                 at = layout.row(channel, (8 * index + row) // minors, row % minors)
-                for part, value in enumerate(split_two(terms_ref[at : at + 1, :])):
-                    first = (part * PROJ + channel) * lows
-                    lhs_s[first : first + lows, lanes] = mine * value.astype(bf16)
+                put_terms(lhs_s, channel, lanes, terms_ref[at : at + 1, :], mine)
         lanes = slice(8 * index * LANES, 8 * (index + 1) * LANES)
         found = dot_nt(lhs_s[:, lanes], rhs_s[:, lanes])
         total_s[...] = found if index == 0 else total_s[...] + found
@@ -704,8 +708,8 @@
     return call(
         partial(route_kernel, devices, per_owner),
         [HBM, HBM],
-        [(asked, i32), ((devices, per_owner), i32), ((rows, LANES), i32)],
-        [(owners.shape, i32)] * 2 + [((rows, LANES), i32)] * 3 + [pltpu.SemaphoreType.DMA((2,))],
+        [(asked, i32), ((rows, LANES), i32)],
+        [(owners.shape, i32)] * 2 + [pltpu.SemaphoreType.DMA((2,))],
         1 << 30,
         "route",
         vmem=63 << 20,
@@ -735,17 +739,19 @@
     )(table, asked)[0]
 
 
-def render(layout, list_counts, tile_order, rows, pos, back, cotangent):
+def render(layout, list_counts, tile_order, rows, pos, cotangent):
     slot_rows = pos.shape[0]
     groups = tile_order.shape[0] // GROUP
     slots = slot_rows * LANES
     return call(
         partial(render_kernel, layout),
-        [SMEM, SMEM, VMEM, VMEM, VMEM, VMEM],
+        [SMEM, SMEM, VMEM, VMEM, VMEM],
         [(cotangent.shape, f32), ((PROJ * layout.count, LANES), f32)],
         [
             ((sum(PARTS) * slot_rows // 2, WIDE), bf16),
-            ((2 * PROJ * slot_rows // 2, WIDE), bf16),
+            ((WIDE, slots), bf16),
+            ((PROJ * slot_rows, slots), bf16),
+            ((PROJ * slot_rows, WIDE), f32),
             ((PROJ * slot_rows, LANES), f32),
             ((24 * slot_rows, LANES), f32),
             ((24 * groups, PIX), f32),
@@ -758,7 +764,7 @@
         ],
         1 << 34,
         "render",
-    )(list_counts, tile_order, rows, pos, back, cotangent)
+    )(list_counts, tile_order, rows, pos, cotangent)
 
 
 def collect(layout, camera_frame, view_angles, shape, dense, asked, terms):
@@ -795,15 +801,13 @@
     tiles_y = devices * tile_order.shape[0] // TX
     camera_frame = (4.0 * TX, 4.0 * tiles_y, 8.0 * TX, 8.0 * tiles_y)
     layout = Rows(devices, tile_owners.size // devices)
-    want, back, pos = route(devices, tile_owners, tile_locals)
+    want, pos = route(devices, tile_owners, tile_locals)
     asked = lax.all_to_all(want, "dev", split_axis=0, concat_axis=0, tiled=True)
     table, dense = shade(camera_frame, view_angles, gaussians)
     if not layout.halves:
         asked = asked.reshape(layout.count, LANES)
-    if layout.halves != 2:
-        back = back.reshape(layout.count, LANES)
     arrived = swap_rows(layout, devices, pick(layout, table, asked))
-    rendered, slot_grads = render(layout, list_counts, tile_order, arrived, pos, back, image_cotangent)
+    rendered, slot_grads = render(layout, list_counts, tile_order, arrived, pos, image_cotangent)
     terms = swap_rows(layout, devices, slot_grads)
     gradients = collect(layout, camera_frame, view_angles, gaussians.shape, dense, asked, terms)
     return (rendered, gradients)

time: 71.3 us -> 72 us (level)
    pallas_call x1, Pallas kernels: 14.8 us -> 16.5 us  [render(): call(partial(render_kernel, layout), [SMEM, SMEM, VMEM, VMEM, VMEM], [(co...]
    pallas_call x1, Pallas kernels: 6.95 us -> 6.05 us  [collect(): call(partial(collect_kernel, layout, camera_frame), [SMEM, VMEM, VMEM, VM...]
where the time goes in v8:
time: 72 us; the launch traced here: 71.7 us
  Pallas kernels  32.8 us (46%)
  blocking collectives  26.5 us (37%)
  starting transfers between devices  7.3 us (10%)
  waiting for transfers between devices  4.14 us (6%)
  between operations  0.88 us (1%)
    all_to_all x2, blocking collectives, swap_rows(): lax.all_to_all(apart, 'dev', split_axis=0, concat_axis=0, tiled=True)  26.5 us
    pallas_call x1, Pallas kernels, render(): call(partial(render_kernel, layout), [SMEM, SMEM, VMEM, VMEM, VMEM], [(co...  16.5 us
    all_to_all x1, starting transfers between devices, shards(): asked = lax.all_to_all(want, 'dev', split_axis=0, concat_axis=0, tiled=True)  7.3 us
    pallas_call x1, Pallas kernels, collect(): call(partial(collect_kernel, layout, camera_frame), [SMEM, VMEM, VMEM, VM...  6.05 us
    all_to_all x1, waiting for transfers between devices, shards(): asked = lax.all_to_all(want, 'dev', split_axis=0, concat_axis=0, tiled=True)  4.14 us
    pallas_call x1, Pallas kernels, route(): call(partial(route_kernel, devices, per_owner), [HBM, HBM], [(asked, i32)...  3.82 us
    pallas_call x1, Pallas kernels, pick(): call(partial(pick_kernel, layout), [VMEM, VMEM], [((PROJ * layout.count,...  3.33 us
    pallas_call x1, Pallas kernels, shade(): call(partial(shade_kernel, camera_frame), [SMEM, VMEM], [((sum(PARTS) * r...  3.09 us
  transfers between devices with their start and end apart: 1, of which 1 were waited for; matrix products, arithmetic and copies ran while one was open for 0% of the time, Pallas kernels for 4%

profile of v8, /device:TPU:0, one launch (start us, length us, event | category | flops | bytes accessed | tf_op | source)
XLA Modules:
  0.0 71.7 jit_solution(459019859214174498)
XLA Ops:
  0.6 0.0 copy-start.3
  0.6 3.8 %route.1 = (s32[64,128]{1,0:T(8,128)}, s32[64,128]{1,0:T(8,128)}) custom-call(s32[16,512]{1,0:T(8,128)} %own_hbm.1, s32[16,512]{1,0:T(8,128)} %loc_hbm.1), custom_call_target="tpu_custom_call" | custom-call | flops 1073741824 | bytes 4194304 | tf_op jit(solution)/shard_map/route/pallas_call | solution.py:708
  4.5 7.3 %all-to-all-start = ((s32[32,2,128]{2,1,0:T(2,128)}), s32[32,2,128]{2,1,0:T(2,128)S(1)}, u32[]{:S(2)}, u32[]{:S(2)}) async-start(s32[32,2,128]{2,1,0:T(2,128)} %bitcast.12), calls=%async_computation | async-start | bytes 65536 | tf_op jit(solution)/shard_map/all_to_all | solution.py:805
  11.8 0.0 copy-done.3
  11.8 3.1 %shade.1 = (bf16[736,256]{1,0:T(8,128)(2,1)S(1)}, f32[1024,128]{1,0:T(8,128)S(1)}) custom-call(f32[3]{0:T(128)S(1)} %copy-done.3, f32[59,8192]{1,0:T(8,128)} %gauss_ref.1), custom_call_target="tpu_custom_call" | custom-call | flops 1073741824 | bytes 4194304 | tf_op jit(solution)/shard_map/shade/pallas_call | solution.py:721
  14.9 4.1 %all-to-all-done = s32[32,2,128]{2,1,0:T(2,128)S(1)} async-done(((s32[32,2,128]{2,1,0:T(2,128)}), s32[32,2,128]{2,1,0:T(2,128)S(1)}, u32[]{:S(2)}, u32[]{:S(2)}) %all-to-all-start) | async-done | bytes 32800 | tf_op jit(solution)/shard_map/all_to_all | solution.py:805
  19.0 0.0 copy-start
  19.0 0.0 copy-start.1
  19.0 0.0 copy-start.2
  19.0 0.0 copy-start.4
  19.0 3.3 %pick.1 = f32[576,128]{1,0:T(8,128)S(1)} custom-call(bf16[736,256]{1,0:T(8,128)(2,1)S(1)} %get-tuple-element.8.parts_ref, s32[64,128]{1,0:T(8,128)S(1)} %bitcast.10), custom_call_target="tpu_custom_call" | custom-call | flops 1073741824 | bytes 4194304 | tf_op jit(solution)/shard_map/pick/pallas_call | solution.py:732
  22.4 13.1 %all_to_all.21 = f32[288,2,128]{2,1,0:T(2,128)S(1)} all-to-all(f32[288,2,128]{2,1,0:T(2,128)S(1)} %bitcast.9), channel_id=1, replica_groups=mesh['dev'=32] {'dev'}, dimensions={0} | all-to-all | bytes 589824 | tf_op jit(solution)/shard_map/all_to_all | solution.py:794
  35.5 0.0 copy-done
  35.5 0.0 copy-done.1
  35.5 0.0 copy-done.2
  35.5 0.0 copy-done.4
  35.5 16.5 %render.1 = (f32[3,4096]{1,0:T(4,128)}, f32[576,128]{1,0:T(8,128)S(1)}) custom-call(s32[16]{0:T(128)S(1)} %copy-done.1, s32[16]{0:T(128)S(1)} %copy-done.2, f32[576,128]{1,0:T(8,128)S(1)} %bitcast.6, s32[64,128]{1,0:T(8,128)S(1)} %copy-done.4, f32[3,4096]{1,0:T(4,128)S(1)} %copy-done), custom_call_target="tpu_custom_call" | custom-call | flops 17179869184 | bytes 4194304 | tf_op jit(solution)/shard_map/render/pallas_call | solution.py:746
  52.1 13.4 %all_to_all.22 = f32[288,2,128]{2,1,0:T(2,128)S(1)} all-to-all(f32[288,2,128]{2,1,0:T(2,128)S(1)} %bitcast.7), channel_id=1, replica_groups=mesh['dev'=32] {'dev'}, dimensions={0} | all-to-all | bytes 589824 | tf_op jit(solution)/shard_map/all_to_all | solution.py:794
  65.5 6.0 %collect.1 = f32[59,8192]{1,0:T(8,128)} custom-call(f32[3]{0:T(128)S(1)} %copy-done.3, f32[1024,128]{1,0:T(8,128)S(1)} %get-tuple-element.12.dense_ref, s32[64,128]{1,0:T(8,128)S(1)} %bitcast.11, f32[576,128]{1,0:T(8,128)S(1)} %bitcast.8), custom_call_target="tpu_custom_call" | custom-call | flops 4294967296 | bytes 4194304 | tf_op jit(solution)/shard_map/collect/pallas_call | solution.py:773
Async XLA Ops:
  0.6 11.1 %copy-start.3 = (f32[3]{0:T(128)S(1)}, f32[3]{0:T(128)}, u32[]{:S(2)}) copy-start(f32[3]{0:T(128)} %angles_ref.3) | copy-start | bytes 40
  4.5 14.6 %all-to-all-start = ((s32[32,2,128]{2,1,0:T(2,128)}), s32[32,2,128]{2,1,0:T(2,128)S(1)}, u32[]{:S(2)}, u32[]{:S(2)}) async-start(s32[32,2,128]{2,1,0:T(2,128)} %bitcast.12), calls=%async_computation | async-start | bytes 65536 | tf_op jit(solution)/shard_map/all_to_all | solution.py:805
  19.0 16.5 %copy-start = (f32[3,4096]{1,0:T(4,128)S(1)}, f32[3,4096]{1,0:T(4,128)}, u32[]{:S(2)}) copy-start(f32[3,4096]{1,0:T(4,128)} %cot_ref.1) | copy-start | bytes 147460
  19.0 16.5 %copy-start.1 = (s32[16]{0:T(128)S(1)}, s32[16]{0:T(128)}, u32[]{:S(2)}) copy-start(s32[16]{0:T(128)} %count_ref.1) | copy-start | bytes 196
  19.0 16.5 %copy-start.2 = (s32[16]{0:T(128)S(1)}, s32[16]{0:T(128)}, u32[]{:S(2)}) copy-start(s32[16]{0:T(128)} %order_ref.1) | copy-start | bytes 196
  19.0 16.5 %copy-start.4 = (s32[64,128]{1,0:T(8,128)S(1)}, s32[64,128]{1,0:T(8,128)}, u32[]{:S(2)}) copy-start(s32[64,128]{1,0:T(8,128)} %get-tuple-element.10.pos_ref) | copy-start | bytes 98308

commit v9 on v7

--- a/solution.py
+++ b/solution.py
@@ -16,6 +16,7 @@
 PARTS = (3, 3, 3, 3, 3, 2, 2, 2, 2)
 STEP = LANES // GROUP
 LOG2E = 1.4426950408889634
+PLANE = 8
 AHEAD = 2
 VMEM_BYTES = 52 * 1024 * 1024
 
@@ -85,6 +86,17 @@
 
 def one_hot(ids, every):
     return jnp.where(narrow(ids) == every, jnp.ones((), bf16), jnp.zeros((), bf16))
+
+
+def put_terms(lhs_s, channel, lanes, row, mine):
+    lows = mine.shape[0]
+    row = jnp.broadcast_to(row, (16, LANES))
+    first = row.astype(bf16)
+    second = (row - first.astype(f32)).astype(bf16)
+    for part, value in enumerate((first, second)):
+        for low in range(0, lows, 16):
+            start = (part * PROJ + channel) * lows + low
+            lhs_s[start : start + 16, lanes] = mine[low : low + 16] * value
 
 
 def pick_slots(parts, slots, low_id, high_id, put):
@@ -176,12 +188,15 @@
             rhs.append(one_hot(rank_rows[row : row + 1], rank_id))
         return total + dot_nt(jnp.concatenate(lhs, axis=1), jnp.concatenate(rhs, axis=1))
 
-    total = lax.fori_loop(0, rows // 8, place, jnp.zeros((4 * devices, per_owner), f32), unroll=True).astype(i32)
+    total = lax.fori_loop(0, rows // 8, place, jnp.zeros((4 * devices, per_owner), f32), unroll=devices <= 32).astype(i32)
     want = total[:devices] * LANES + total[devices : 2 * devices]
     halves = per_owner // LANES
     if per_owner % LANES == 0 and halves > 1:
-        for half in range(halves):
-            want_ref[pl.ds(half, devices, stride=halves), :] = want[:, half * LANES : (half + 1) * LANES]
+        planes = devices // PLANE
+        for plane in range(planes):
+            for half in range(halves):
+                rows_of = pl.ds(plane * halves + half, PLANE, stride=planes * halves)
+                want_ref[rows_of, :] = want[plane * PLANE : (plane + 1) * PLANE, half * LANES : (half + 1) * LANES]
     else:
         want_ref[...] = want
     back_ref[...] = total[2 * devices : 3 * devices] * LANES + total[3 * devices :]
@@ -624,9 +639,7 @@
             rhs_s[:, lanes] = one_hot(high[row : row + 1], high_id)
             for channel in range(PROJ):
                 at = layout.row(channel, (8 * index + row) // minors, row % minors)
-                for part, value in enumerate(split_two(terms_ref[at : at + 1, :])):
-                    first = (part * PROJ + channel) * lows
-                    lhs_s[first : first + lows, lanes] = mine * value.astype(bf16)
+                put_terms(lhs_s, channel, lanes, terms_ref[at : at + 1, :], mine)
         lanes = slice(8 * index * LANES, 8 * (index + 1) * LANES)
         found = dot_nt(lhs_s[:, lanes], rhs_s[:, lanes])
         total_s[...] = found if index == 0 else total_s[...] + found
@@ -782,6 +795,17 @@
     )(view_angles, dense, asked, terms)[0]
 
 
+def swap_requests(layout, devices, want):
+    if layout.halves < 2:
+        return lax.all_to_all(want, "dev", split_axis=0, concat_axis=0, tiled=True)
+    planes = devices // PLANE
+    in_plane = [[plane * PLANE + one for one in range(PLANE)] for plane in range(planes)]
+    across = [[plane * PLANE + one for plane in range(planes)] for one in range(PLANE)]
+    near = lax.all_to_all(want, "dev", split_axis=0, concat_axis=0, axis_index_groups=in_plane, tiled=True)
+    near = near.reshape(PLANE, planes, layout.halves, LANES).transpose(1, 0, 2, 3).reshape(want.shape)
+    return lax.all_to_all(near, "dev", split_axis=0, concat_axis=0, axis_index_groups=across, tiled=True)
+
+
 def swap_rows(layout, devices, rows):
     if layout.halves:
         apart = rows.reshape(devices * PROJ, layout.halves, LANES)
@@ -796,7 +820,7 @@
     camera_frame = (4.0 * TX, 4.0 * tiles_y, 8.0 * TX, 8.0 * tiles_y)
     layout = Rows(devices, tile_owners.size // devices)
     want, back, pos = route(devices, tile_owners, tile_locals)
-    asked = lax.all_to_all(want, "dev", split_axis=0, concat_axis=0, tiled=True)
+    asked = swap_requests(layout, devices, want)
     table, dense = shade(camera_frame, view_angles, gaussians)
     if not layout.halves:
         asked = asked.reshape(layout.count, LANES)

time: 71.3 us -> 77.1 us (1.081)
  blocking collectives: 26.5 us -> 36.5 us
  starting transfers between devices: 7.3 us -> 4.87 us
  waiting for transfers between devices: 4.14 us -> 2.56 us
  Pallas kernels: 32.1 us -> 31.2 us
    all_to_all x0 -> x1, blocking collectives: none -> 10 us  [swap_requests(): lax.all_to_all(want, 'dev', split_axis=0, concat_axis=0, axis_index_group...]
    all_to_all x1, starting transfers between devices: 7.3 us -> 4.87 us  [swap_requests(): lax.all_to_all(near, 'dev', split_axis=0, concat_axis=0, axis_index_group...]
    all_to_all x1, waiting for transfers between devices: 4.14 us -> 2.56 us  [swap_requests(): lax.all_to_all(near, 'dev', split_axis=0, concat_axis=0, axis_index_group...]
    pallas_call x1, Pallas kernels: 6.95 us -> 6.05 us  [collect(): call(partial(collect_kernel, layout, camera_frame), [SMEM, VMEM, VMEM, VM...]
where the time goes in v9:
time: 77.1 us; the launch traced here: 76.7 us
  blocking collectives  36.5 us (47%)
  Pallas kernels  31.2 us (40%)
  starting transfers between devices  4.87 us (6%)
  waiting for transfers between devices  2.56 us (3%)
  between operations  0.89 us (1%)
    all_to_all x2, blocking collectives, swap_rows(): lax.all_to_all(apart, 'dev', split_axis=0, concat_axis=0, tiled=True)  26.5 us
    pallas_call x1, Pallas kernels, render(): call(partial(render_kernel, layout), [SMEM, SMEM, VMEM, VMEM, VMEM, VMEM]...  14.8 us
    all_to_all x1, blocking collectives, swap_requests(): lax.all_to_all(want, 'dev', split_axis=0, concat_axis=0, axis_index_group...  10 us
    pallas_call x1, Pallas kernels, collect(): call(partial(collect_kernel, layout, camera_frame), [SMEM, VMEM, VMEM, VM...  6.05 us
    all_to_all x1, starting transfers between devices, swap_requests(): lax.all_to_all(near, 'dev', split_axis=0, concat_axis=0, axis_index_group...  4.87 us
    pallas_call x1, Pallas kernels, route(): call(partial(route_kernel, devices, per_owner), [HBM, HBM], [(asked, i32)...  3.98 us
    pallas_call x1, Pallas kernels, pick(): call(partial(pick_kernel, layout), [VMEM, VMEM], [((PROJ * layout.count,...  3.32 us
    pallas_call x1, Pallas kernels, shade(): call(partial(shade_kernel, camera_frame), [SMEM, VMEM], [((sum(PARTS) * r...  3.09 us
  transfers between devices with their start and end apart: 1, of which 1 were waited for; matrix products, arithmetic and copies ran while one was open for 0% of the time, Pallas kernels for 4%

profile of v9, /device:TPU:0, one launch (start us, length us, event | category | flops | bytes accessed | tf_op | source)
XLA Modules:
  0.0 76.7 jit_solution(17491540387974930331)
XLA Ops:
  0.6 0.0 copy-start.3
  0.6 4.0 %route.1 = (s32[64,128]{1,0:T(8,128)}, s32[32,256]{1,0:T(8,128)}, s32[64,128]{1,0:T(8,128)}) custom-call(s32[16,512]{1,0:T(8,128)} %own_hbm.1, s32[16,512]{1,0:T(8,128)} %loc_hbm.1), custom_call_target="tpu_custom_call" | custom-call | flops 1073741824 | bytes 4194304 | tf_op jit(solution)/shard_map/route/pallas_call | solution.py:717
  4.6 10.0 %all_to_all.30 = s32[8,8,128]{2,1,0:T(8,128)S(1)} all-to-all(s32[8,8,128]{2,1,0:T(8,128)} %bitcast.17), channel_id=1, replica_groups={{0,1,2,3,4,5,6,7},{8,9,10,11,12,13,14,15},{16,17,18,19,20,21,22,23},{24..., dimensions={0} | all-to-all | bytes 65536 | tf_op jit(solution)/shard_map/all_to_all | solution.py:804
  14.6 0.6 copy.9
  15.3 4.9 %all-to-all-start.1 = ((s32[4,16,128]{2,1,0:T(8,128)}), s32[4,16,128]{2,1,0:T(8,128)S(1)}, u32[]{:S(2)}, u32[]{:S(2)}) async-start(s32[4,16,128]{2,1,0:T(8,128)} %bitcast.3), calls=%async_computation.1 | async-start | bytes 65536 | tf_op jit(solution)/shard_map/all_to_all | solution.py:806
  20.1 0.0 copy-done.3
  20.1 3.1 %shade.1 = (bf16[736,256]{1,0:T(8,128)(2,1)S(1)}, f32[1024,128]{1,0:T(8,128)S(1)}) custom-call(f32[3]{0:T(128)S(1)} %copy-done.3, f32[59,8192]{1,0:T(8,128)} %gauss_ref.1), custom_call_target="tpu_custom_call" | custom-call | flops 1073741824 | bytes 4194304 | tf_op jit(solution)/shard_map/shade/pallas_call | solution.py:730
  23.2 2.6 %all-to-all-done.1 = s32[4,16,128]{2,1,0:T(8,128)S(1)} async-done(((s32[4,16,128]{2,1,0:T(8,128)}), s32[4,16,128]{2,1,0:T(8,128)S(1)}, u32[]{:S(2)}, u32[]{:S(2)}) %all-to-all-start.1) | async-done | bytes 32800 | tf_op jit(solution)/shard_map/all_to_all | solution.py:806
  25.8 0.0 copy-start
  25.8 0.0 copy-start.1
  25.8 0.0 copy-start.2
  25.8 0.0 copy-start.4
  25.8 0.0 copy-start.5
  25.8 3.3 %pick.1 = f32[576,128]{1,0:T(8,128)S(1)} custom-call(bf16[736,256]{1,0:T(8,128)(2,1)S(1)} %get-tuple-element.9.parts_ref, s32[64,128]{1,0:T(8,128)S(1)} %bitcast.14), custom_call_target="tpu_custom_call" | custom-call | flops 1073741824 | bytes 4194304 | tf_op jit(solution)/shard_map/pick/pallas_call | solution.py:741
  29.1 13.1 %all_to_all.31 = f32[288,2,128]{2,1,0:T(2,128)S(1)} all-to-all(f32[288,2,128]{2,1,0:T(2,128)S(1)} %bitcast.13), channel_id=1, replica_groups=mesh['dev'=32] {'dev'}, dimensions={0} | all-to-all | bytes 589824 | tf_op jit(solution)/shard_map/all_to_all | solution.py:812
  42.3 0.0 copy-done
  42.3 0.0 copy-done.1
  42.3 0.0 copy-done.2
  42.3 0.0 copy-done.4
  42.3 0.0 copy-done.5
  42.3 14.8 %render.1 = (f32[3,4096]{1,0:T(4,128)}, f32[576,128]{1,0:T(8,128)S(1)}) custom-call(s32[16]{0:T(128)S(1)} %copy-done.1, s32[16]{0:T(128)S(1)} %copy-done.2, f32[576,128]{1,0:T(8,128)S(1)} %bitcast.10, s32[64,128]{1,0:T(8,128)S(1)} %copy-done.5, s32[32,256]{1,0:T(8,128)S(1)} %copy-done.4, f32[3,4096]{1,0:T(4,128)S(1)} %copy-done), custom_call_target="tpu_custom_call" | custom-call | flops 17179869184 | bytes 4194304 | tf_op jit(solution)/shard_map/render/pallas_call | solution.py:755
  57.1 13.4 %all_to_all.32 = f32[288,2,128]{2,1,0:T(2,128)S(1)} all-to-all(f32[288,2,128]{2,1,0:T(2,128)S(1)} %bitcast.11), channel_id=1, replica_groups=mesh['dev'=32] {'dev'}, dimensions={0} | all-to-all | bytes 589824 | tf_op jit(solution)/shard_map/all_to_all | solution.py:812
  70.5 6.0 %collect.1 = f32[59,8192]{1,0:T(8,128)} custom-call(f32[3]{0:T(128)S(1)} %copy-done.3, f32[1024,128]{1,0:T(8,128)S(1)} %get-tuple-element.14.dense_ref, s32[64,128]{1,0:T(8,128)S(1)} %bitcast.15, f32[576,128]{1,0:T(8,128)S(1)} %bitcast.12), custom_call_target="tpu_custom_call" | custom-call | flops 4294967296 | bytes 4194304 | tf_op jit(solution)/shard_map/collect/pallas_call | solution.py:780
Async XLA Ops:
  0.6 19.5 %copy-start.3 = (f32[3]{0:T(128)S(1)}, f32[3]{0:T(128)}, u32[]{:S(2)}) copy-start(f32[3]{0:T(128)} %angles_ref.3) | copy-start | bytes 40
  15.3 10.5 %all-to-all-start.1 = ((s32[4,16,128]{2,1,0:T(8,128)}), s32[4,16,128]{2,1,0:T(8,128)S(1)}, u32[]{:S(2)}, u32[]{:S(2)}) async-start(s32[4,16,128]{2,1,0:T(8,128)} %bitcast.3), calls=%async_computation.1 | async-start | bytes 65536 | tf_op jit(solution)/shard_map/all_to_all | solution.py:806
  25.8 16.5 %copy-start = (f32[3,4096]{1,0:T(4,128)S(1)}, f32[3,4096]{1,0:T(4,128)}, u32[]{:S(2)}) copy-start(f32[3,4096]{1,0:T(4,128)} %cot_ref.1) | copy-start | bytes 147460
  25.8 16.5 %copy-start.1 = (s32[16]{0:T(128)S(1)}, s32[16]{0:T(128)}, u32[]{:S(2)}) copy-start(s32[16]{0:T(128)} %count_ref.1) | copy-start | bytes 196
  25.8 16.5 %copy-start.2 = (s32[16]{0:T(128)S(1)}, s32[16]{0:T(128)}, u32[]{:S(2)}) copy-start(s32[16]{0:T(128)} %order_ref.1) | copy-start | bytes 196
  25.8 16.5 %copy-start.4 = (s32[32,256]{1,0:T(8,128)S(1)}, s32[32,256]{1,0:T(8,128)}, u32[]{:S(2)}) copy-start(s32[32,256]{1,0:T(8,128)} %get-tuple-element.12.back_ref) | copy-start | bytes 98308
  25.8 16.5 %copy-start.5 = (s32[64,128]{1,0:T(8,128)S(1)}, s32[64,128]{1,0:T(8,128)}, u32[]{:S(2)}) copy-start(s32[64,128]{1,0:T(8,128)} %get-tuple-element.11.pos_ref) | copy-start | bytes 98308

commit v10 on v7

--- a/solution.py
+++ b/solution.py
@@ -87,8 +87,19 @@
     return jnp.where(narrow(ids) == every, jnp.ones((), bf16), jnp.zeros((), bf16))
 
 
-def pick_slots(parts, slots, low_id, high_id, put):
-    found = dot(parts, one_hot(slots % WIDE, high_id))
+def put_terms(lhs_s, channel, lanes, row, mine):
+    lows = mine.shape[0]
+    row = jnp.broadcast_to(row, (16, LANES))
+    first = row.astype(bf16)
+    second = (row - first.astype(f32)).astype(bf16)
+    for part, value in enumerate((first, second)):
+        for low in range(0, lows, 16):
+            start = (part * PROJ + channel) * lows + low
+            lhs_s[start : start + 16, lanes] = mine[low : low + 16] * value
+
+
+def pick_slots(parts, hot, slots, low_id, put):
+    found = dot(parts, hot)
     mine = slots // WIDE == low_id
     lows = low_id.shape[0]
     first = 0
@@ -176,7 +187,7 @@
             rhs.append(one_hot(rank_rows[row : row + 1], rank_id))
         return total + dot_nt(jnp.concatenate(lhs, axis=1), jnp.concatenate(rhs, axis=1))
 
-    total = lax.fori_loop(0, rows // 8, place, jnp.zeros((4 * devices, per_owner), f32), unroll=True).astype(i32)
+    total = lax.fori_loop(0, rows // 8, place, jnp.zeros((4 * devices, per_owner), f32), unroll=devices <= 32).astype(i32)
     want = total[:devices] * LANES + total[devices : 2 * devices]
     halves = per_owner // LANES
     if per_owner % LANES == 0 and halves > 1:
@@ -331,18 +342,15 @@
     high_id = narrow(iota((WIDE, WIDE), 0))
     minors = layout.minors()
 
-    def pick_some(index, _):
-        slots = jnp.concatenate([asked_ref[pl.ds(2 * index + one, 1), :] for one in range(2)], axis=1)
+    for index in range(layout.count // 2):
+        slots = jnp.concatenate([asked_ref[2 * index + one : 2 * index + one + 1, :] for one in range(2)], axis=1)
 
         def put(channel, value):
             for one in range(2):
                 at = layout.row(channel, (2 * index + one) // minors, (2 * index + one) % minors)
-                out_ref[pl.ds(at, 1), :] = value[:, one * LANES : (one + 1) * LANES]
-
-        pick_slots(parts_ref[...], slots, low_id, high_id, put)
-        return 0
-
-    lax.fori_loop(0, layout.count // 2, pick_some, 0, unroll=True)
+                out_ref[at : at + 1, :] = value[:, one * LANES : (one + 1) * LANES]
+
+        pick_slots(parts_ref[...], one_hot(slots % WIDE, high_id), slots, low_id, put)
 
 
 def render_kernel(
@@ -353,8 +361,10 @@
     pos_ref,
     back_ref,
     cot_ref,
+    image_hbm,
+    out_ref,
     image_ref,
-    out_ref,
+    image_sem,
     in_s,
     out_s,
     raw_s,
@@ -393,18 +403,17 @@
     low_id = iota((slot_rows // 2, WIDE), 0)
     high_id = narrow(iota((WIDE, WIDE), 0))
 
-    def pick_in(index, _):
-        slots = jnp.concatenate([pos_ref[pl.ds(2 * index + one, 1), :] for one in range(2)], axis=1)
+    def pick_in(row):
+        slots = jnp.concatenate([pos_ref[row + one : row + one + 1, :] for one in range(2)], axis=1)
 
         def put(channel, value):
             for one in range(2):
-                raw_s[pl.ds(channel * slot_rows + 2 * index + one, 1), :] = value[:, one * LANES : (one + 1) * LANES]
-
-        pick_slots(in_s[...], slots, low_id, high_id, put)
-        return 0
-
-    lax.fori_loop(0, slot_rows // 2, pick_in, 0, unroll=True)
-    for block in range(blocks):
+                at = channel * slot_rows + row + one
+                raw_s[at : at + 1, :] = value[:, one * LANES : (one + 1) * LANES]
+
+        pick_slots(in_s[...], one_hot(slots % WIDE, high_id), slots, low_id, put)
+
+    def quadratics(block):
         group = block * 8 // chunks
         middle_x, middle_y, live = middles[group]
         found = [
@@ -513,7 +522,19 @@
 
     trans = tuple(jnp.ones((GROUP, PIX), f32) for _ in range(groups))
     images = tuple(jnp.zeros((24, PIX), f32) for _ in range(groups))
+    per_group = chunks // 8
+    for block in range(0, blocks, per_group):
+        for row in range(0, 8, 2):
+            pick_in(8 * block + row)
+        quadratics(block)
     for pair in range(-AHEAD, chunks // 2 + 1):
+        step = pair + AHEAD + 4
+        if 4 <= step < chunks // 2:
+            for group in range(groups):
+                block = group * per_group + step // 4
+                pick_in(8 * block + step % 4 * 2)
+                if step % 4 == 3:
+                    quadratics(block)
         for one in range(2):
             if pair + AHEAD < chunks // 2:
                 evaluate(2 * (pair + AHEAD) + one)
@@ -527,6 +548,8 @@
             for tile in range(GROUP):
                 at = (group * GROUP + tile) * PIX
                 image_ref[colour, at : at + PIX] = images[group][colour * GROUP + tile]
+    image_copy = pltpu.make_async_copy(image_ref, image_hbm, image_sem)
+    image_copy.start()
 
     def moment(index):
         for group in range(groups):
@@ -598,10 +621,11 @@
                 at = layout.row(channel, (2 * index + one) // minors, (2 * index + one) % minors)
                 out_ref[pl.ds(at, 1), :] = value[:, one * LANES : (one + 1) * LANES]
 
-        pick_slots(out_s[...], slots, low_id, high_id, put)
+        pick_slots(out_s[...], one_hot(slots % WIDE, high_id), slots, low_id, put)
         return 0
 
     lax.fori_loop(0, layout.count // 2, pick_out, 0, unroll=True)
+    image_copy.wait()
 
 
 def collect_kernel(
@@ -624,12 +648,11 @@
             rhs_s[:, lanes] = one_hot(high[row : row + 1], high_id)
             for channel in range(PROJ):
                 at = layout.row(channel, (8 * index + row) // minors, row % minors)
-                for part, value in enumerate(split_two(terms_ref[at : at + 1, :])):
-                    first = (part * PROJ + channel) * lows
-                    lhs_s[first : first + lows, lanes] = mine * value.astype(bf16)
-        lanes = slice(8 * index * LANES, 8 * (index + 1) * LANES)
-        found = dot_nt(lhs_s[:, lanes], rhs_s[:, lanes])
-        total_s[...] = found if index == 0 else total_s[...] + found
+                put_terms(lhs_s, channel, lanes, terms_ref[at : at + 1, :], mine)
+        if index % 2 == 1:
+            lanes = slice(8 * (index - 1) * LANES, 8 * (index + 1) * LANES)
+            found = dot_nt(lhs_s[:, lanes], rhs_s[:, lanes])
+            total_s[...] = found if index == 1 else total_s[...] + found
     rotation = view(angles_ref)
     basis = harmonics(*rotation[2])
     for part in range(rows // 8):
@@ -686,7 +709,7 @@
     return pl.pallas_call(
         kernel,
         in_specs=specs,
-        out_specs=[out_spec] * len(outs),
+        out_specs=list(out_spec) if isinstance(out_spec, tuple) else [out_spec] * len(outs),
         out_shape=[jax.ShapeDtypeStruct(shape, dtype) for shape, dtype in outs],
         scratch_shapes=[pltpu.VMEM(*one) if isinstance(one, tuple) else one for one in scratch],
         compiler_params=pltpu.CompilerParams(vmem_limit_bytes=vmem),
@@ -744,6 +767,8 @@
         [SMEM, SMEM, VMEM, VMEM, VMEM, VMEM],
         [(cotangent.shape, f32), ((PROJ * layout.count, LANES), f32)],
         [
+            (cotangent.shape, f32),
+            pltpu.SemaphoreType.DMA,
             ((sum(PARTS) * slot_rows // 2, WIDE), bf16),
             ((2 * PROJ * slot_rows // 2, WIDE), bf16),
             ((PROJ * slot_rows, LANES), f32),
@@ -758,6 +783,7 @@
         ],
         1 << 34,
         "render",
+        out_spec=(HBM, VMEM),
     )(list_counts, tile_order, rows, pos, back, cotangent)
 
 

time: 71.3 us -> 70.7 us (level)
    pallas_call x1, Pallas kernels: 6.95 us -> 6.05 us  [collect(): call(partial(collect_kernel, layout, camera_frame), [SMEM, VMEM, VMEM, VM...]
where the time goes in v10:
time: 70.7 us; the launch traced here: 70.4 us
  Pallas kernels  31.5 us (45%)
  blocking collectives  26.5 us (37%)
  starting transfers between devices  7.3 us (10%)
  waiting for transfers between devices  4.14 us (6%)
  between operations  0.9 us (1%)
    all_to_all x2, blocking collectives, swap_rows(): lax.all_to_all(apart, 'dev', split_axis=0, concat_axis=0, tiled=True)  26.5 us
    pallas_call x1, Pallas kernels, render(): call(partial(render_kernel, layout), [SMEM, SMEM, VMEM, VMEM, VMEM, VMEM]...  15.1 us
    all_to_all x1, starting transfers between devices, shards(): asked = lax.all_to_all(want, 'dev', split_axis=0, concat_axis=0, tiled=True)  7.3 us
    pallas_call x1, Pallas kernels, collect(): call(partial(collect_kernel, layout, camera_frame), [SMEM, VMEM, VMEM, VM...  6.05 us
    all_to_all x1, waiting for transfers between devices, shards(): asked = lax.all_to_all(want, 'dev', split_axis=0, concat_axis=0, tiled=True)  4.14 us
    pallas_call x1, Pallas kernels, route(): call(partial(route_kernel, devices, per_owner), [HBM, HBM], [(asked, i32)...  3.98 us
    pallas_call x1, Pallas kernels, pick(): call(partial(pick_kernel, layout), [VMEM, VMEM], [((PROJ * layout.count,...  3.33 us
    pallas_call x1, Pallas kernels, shade(): call(partial(shade_kernel, camera_frame), [SMEM, VMEM], [((sum(PARTS) * r...  3.09 us
  transfers between devices with their start and end apart: 1, of which 1 were waited for; matrix products, arithmetic and copies ran while one was open for 0% of the time, Pallas kernels for 4%

profile of v10, /device:TPU:0, one launch (start us, length us, event | category | flops | bytes accessed | tf_op | source)
XLA Modules:
  0.0 70.4 jit_solution(16694104421875409483)
XLA Ops:
  0.6 0.0 copy-start.3
  0.6 4.0 %route.1 = (s32[64,128]{1,0:T(8,128)}, s32[32,256]{1,0:T(8,128)}, s32[64,128]{1,0:T(8,128)}) custom-call(s32[16,512]{1,0:T(8,128)} %own_hbm.1, s32[16,512]{1,0:T(8,128)} %loc_hbm.1), custom_call_target="tpu_custom_call" | custom-call | flops 1073741824 | bytes 4194304 | tf_op jit(solution)/shard_map/route/pallas_call | solution.py:727
  4.6 7.3 %all-to-all-start = ((s32[32,2,128]{2,1,0:T(2,128)}), s32[32,2,128]{2,1,0:T(2,128)S(1)}, u32[]{:S(2)}, u32[]{:S(2)}) async-start(s32[32,2,128]{2,1,0:T(2,128)} %bitcast.12), calls=%async_computation | async-start | bytes 65536 | tf_op jit(solution)/shard_map/all_to_all | solution.py:825
  11.9 0.0 copy-done.3
  11.9 3.1 %shade.1 = (bf16[736,256]{1,0:T(8,128)(2,1)S(1)}, f32[1024,128]{1,0:T(8,128)S(1)}) custom-call(f32[3]{0:T(128)S(1)} %copy-done.3, f32[59,8192]{1,0:T(8,128)} %gauss_ref.1), custom_call_target="tpu_custom_call" | custom-call | flops 1073741824 | bytes 4194304 | tf_op jit(solution)/shard_map/shade/pallas_call | solution.py:740
  15.0 4.1 %all-to-all-done = s32[32,2,128]{2,1,0:T(2,128)S(1)} async-done(((s32[32,2,128]{2,1,0:T(2,128)}), s32[32,2,128]{2,1,0:T(2,128)S(1)}, u32[]{:S(2)}, u32[]{:S(2)}) %all-to-all-start) | async-done | bytes 32800 | tf_op jit(solution)/shard_map/all_to_all | solution.py:825
  19.2 0.0 copy-start
  19.2 0.0 copy-start.1
  19.2 0.0 copy-start.2
  19.2 0.0 copy-start.4
  19.2 0.0 copy-start.5
  19.2 3.3 %pick.1 = f32[576,128]{1,0:T(8,128)S(1)} custom-call(bf16[736,256]{1,0:T(8,128)(2,1)S(1)} %get-tuple-element.9.parts_ref, s32[64,128]{1,0:T(8,128)S(1)} %bitcast.10), custom_call_target="tpu_custom_call" | custom-call | flops 1073741824 | bytes 4194304 | tf_op jit(solution)/shard_map/pick/pallas_call | solution.py:751
  22.5 13.1 %all_to_all.21 = f32[288,2,128]{2,1,0:T(2,128)S(1)} all-to-all(f32[288,2,128]{2,1,0:T(2,128)S(1)} %bitcast.9), channel_id=1, replica_groups=mesh['dev'=32] {'dev'}, dimensions={0} | all-to-all | bytes 589824 | tf_op jit(solution)/shard_map/all_to_all | solution.py:814
  35.7 0.0 copy-done
  35.7 0.0 copy-done.1
  35.7 0.0 copy-done.2
  35.7 0.0 copy-done.4
  35.7 0.0 copy-done.5
  35.7 15.1 %render.1 = (f32[3,4096]{1,0:T(4,128)}, f32[576,128]{1,0:T(8,128)S(1)}) custom-call(s32[16]{0:T(128)S(1)} %copy-done.1, s32[16]{0:T(128)S(1)} %copy-done.2, f32[576,128]{1,0:T(8,128)S(1)} %bitcast.6, s32[64,128]{1,0:T(8,128)S(1)} %copy-done.5, s32[32,256]{1,0:T(8,128)S(1)} %copy-done.4, f32[3,4096]{1,0:T(4,128)S(1)} %copy-done), custom_call_target="tpu_custom_call" | custom-call | flops 17179869184 | bytes 4194304 | tf_op jit(solution)/shard_map/render/pallas_call | solution.py:765
  50.8 13.4 %all_to_all.22 = f32[288,2,128]{2,1,0:T(2,128)S(1)} all-to-all(f32[288,2,128]{2,1,0:T(2,128)S(1)} %bitcast.7), channel_id=1, replica_groups=mesh['dev'=32] {'dev'}, dimensions={0} | all-to-all | bytes 589824 | tf_op jit(solution)/shard_map/all_to_all | solution.py:814
  64.2 6.0 %collect.1 = f32[59,8192]{1,0:T(8,128)} custom-call(f32[3]{0:T(128)S(1)} %copy-done.3, f32[1024,128]{1,0:T(8,128)S(1)} %get-tuple-element.14.dense_ref, s32[64,128]{1,0:T(8,128)S(1)} %bitcast.11, f32[576,128]{1,0:T(8,128)S(1)} %bitcast.8), custom_call_target="tpu_custom_call" | custom-call | flops 4294967296 | bytes 4194304 | tf_op jit(solution)/shard_map/collect/pallas_call | solution.py:793
Async XLA Ops:
  0.6 11.3 %copy-start.3 = (f32[3]{0:T(128)S(1)}, f32[3]{0:T(128)}, u32[]{:S(2)}) copy-start(f32[3]{0:T(128)} %angles_ref.3) | copy-start | bytes 40
  4.6 14.6 %all-to-all-start = ((s32[32,2,128]{2,1,0:T(2,128)}), s32[32,2,128]{2,1,0:T(2,128)S(1)}, u32[]{:S(2)}, u32[]{:S(2)}) async-start(s32[32,2,128]{2,1,0:T(2,128)} %bitcast.12), calls=%async_computation | async-start | bytes 65536 | tf_op jit(solution)/shard_map/all_to_all | solution.py:825
  19.2 16.5 %copy-start = (f32[3,4096]{1,0:T(4,128)S(1)}, f32[3,4096]{1,0:T(4,128)}, u32[]{:S(2)}) copy-start(f32[3,4096]{1,0:T(4,128)} %cot_ref.1) | copy-start | bytes 147460
  19.2 16.5 %copy-start.1 = (s32[16]{0:T(128)S(1)}, s32[16]{0:T(128)}, u32[]{:S(2)}) copy-start(s32[16]{0:T(128)} %count_ref.1) | copy-start | bytes 196
  19.2 16.5 %copy-start.2 = (s32[16]{0:T(128)S(1)}, s32[16]{0:T(128)}, u32[]{:S(2)}) copy-start(s32[16]{0:T(128)} %order_ref.1) | copy-start | bytes 196
  19.2 16.5 %copy-start.4 = (s32[32,256]{1,0:T(8,128)S(1)}, s32[32,256]{1,0:T(8,128)}, u32[]{:S(2)}) copy-start(s32[32,256]{1,0:T(8,128)} %get-tuple-element.12.back_ref) | copy-start | bytes 98308
  19.2 16.5 %copy-start.5 = (s32[64,128]{1,0:T(8,128)S(1)}, s32[64,128]{1,0:T(8,128)}, u32[]{:S(2)}) copy-start(s32[64,128]{1,0:T(8,128)} %get-tuple-element.11.pos_ref) | copy-start | bytes 98308

commit v11 on v10

--- a/solution.py
+++ b/solution.py
@@ -120,26 +120,17 @@
         parts_ref[at : at + value.shape[0], half * LANES : (half + 1) * LANES] = one.astype(bf16)
 
 
-def route_kernel(devices, per_owner, own_hbm, loc_hbm, want_ref, back_ref, pos_ref, own_ref, loc_ref, own_s, loc_s, rank_s, sems):
+def route_kernel(devices, per_owner, own_hbm, loc_hbm, want_ref, place_ref, own_ref, loc_ref, own_s, loc_s, rank_s, sems):
     copies = [pltpu.make_async_copy(own_hbm, own_ref, sems.at[0]), pltpu.make_async_copy(loc_hbm, loc_ref, sems.at[1])]
     for copy in copies:
         copy.start()
     for copy in copies:
         copy.wait()
+    tiles = own_ref.shape[0]
     rows = own_s.shape[0]
-    blocks = own_ref.shape[1] // LANES
-    lane = iota((8, LANES), 1)
-    from_slot = iota((8, LANES), 0) * STEP + lane // GROUP
-    tile_of = lane % GROUP
-    for group in range(own_ref.shape[0] // GROUP):
-        for block in range(blocks):
-            for source, target in ((own_ref, own_s), (loc_ref, loc_s)):
-                part = source[group * GROUP : (group + 1) * GROUP, block * LANES : (block + 1) * LANES]
-                out = jnp.zeros((8, LANES), i32)
-                for tile in range(GROUP):
-                    out = jnp.where(tile_of == tile, lane_pick(part[tile : tile + 1], from_slot), out)
-                start = (group * blocks + block) * 8
-                target[start : start + 8, :] = out
+    for block in range(rows // tiles):
+        own_s[block * tiles : (block + 1) * tiles, :] = own_ref[:, block * LANES : (block + 1) * LANES]
+        loc_s[block * tiles : (block + 1) * tiles, :] = loc_ref[:, block * LANES : (block + 1) * LANES]
     owner = own_s[...]
     left = (iota((LANES, 2 * LANES), 0) < iota((LANES, 2 * LANES), 1)) | (iota((LANES, 2 * LANES), 1) >= LANES)
     above = iota((rows, rows), 1) < iota((rows, rows), 0)
@@ -154,12 +145,11 @@
         here = sums[one * rows : (one + 1) * rows, :LANES] + base[:, one * LANES : (one + 1) * LANES]
         rank = jnp.where(owner == one, here, rank)
     rank = rank.astype(i32)
-    pos_ref[...] = owner * per_owner + rank
+    place_ref[...] = owner * per_owner + rank
     rank_s[...] = rank
 
     owner_id = iota((devices, LANES), 0)
     rank_id = narrow(iota((per_owner, LANES), 0))
-    slot_lane = iota((devices, LANES), 1).astype(f32)
 
     def place(index, total):
         start = pl.multiple_of(index * 8, 8)
@@ -172,14 +162,11 @@
         rhs = []
         for row in range(8):
             mine = own_rows[row : row + 1] == owner_id
-            number = (start + row).astype(f32)
             lhs.append(
                 jnp.concatenate(
                     [
                         jnp.where(mine, high_rows[row : row + 1], 0.0),
                         jnp.where(mine, low_rows[row : row + 1], 0.0),
-                        jnp.where(mine, number, 0.0),
-                        jnp.where(mine, slot_lane, 0.0),
                     ],
                     axis=0,
                 ).astype(bf16)
@@ -187,15 +174,55 @@
             rhs.append(one_hot(rank_rows[row : row + 1], rank_id))
         return total + dot_nt(jnp.concatenate(lhs, axis=1), jnp.concatenate(rhs, axis=1))
 
-    total = lax.fori_loop(0, rows // 8, place, jnp.zeros((4 * devices, per_owner), f32), unroll=devices <= 32).astype(i32)
-    want = total[:devices] * LANES + total[devices : 2 * devices]
+    total = lax.fori_loop(0, rows // 8, place, jnp.zeros((2 * devices, per_owner), f32), unroll=devices <= 32).astype(i32)
+    want = total[:devices] * LANES + total[devices:]
     halves = per_owner // LANES
     if per_owner % LANES == 0 and halves > 1:
         for half in range(halves):
             want_ref[pl.ds(half, devices, stride=halves), :] = want[:, half * LANES : (half + 1) * LANES]
     else:
         want_ref[...] = want
-    back_ref[...] = total[2 * devices : 3 * devices] * LANES + total[3 * devices :]
+
+
+def order_kernel(tiles, place_ref, pos_ref, back_ref):
+    rows = place_ref.shape[0]
+    blocks = rows // tiles
+    chunks = rows * GROUP // tiles
+    lane = iota((8, LANES), 1)
+    from_slot = iota((8, LANES), 0) * STEP + lane // GROUP
+    tile_of = lane % GROUP
+    for group in range(tiles // GROUP):
+        for block in range(blocks):
+            start = block * tiles + group * GROUP
+            part = place_ref[start : start + GROUP, :]
+            out = jnp.zeros((8, LANES), i32)
+            for tile in range(GROUP):
+                out = jnp.where(tile_of == tile, lane_pick(part[tile : tile + 1], from_slot), out)
+            start = group * chunks + block * 8
+            pos_ref[start : start + 8, :] = out
+    lows = back_ref.shape[0]
+    low_id = iota((lows, LANES), 0)
+    high_id = narrow(iota((WIDE, LANES), 0))
+    lane = iota((lows, LANES), 1)
+    total = jnp.zeros((2 * lows, WIDE), f32)
+    for start in range(0, rows, 8):
+        lhs = []
+        rhs = []
+        for row in range(start, start + 8):
+            place = place_ref[row : row + 1, :]
+            mine = place // WIDE == low_id
+            tile = row % tiles
+            number = tile // GROUP * chunks + row // tiles * 8 + lane // STEP
+            within = lane % STEP * GROUP + tile % GROUP
+            lhs.append(
+                jnp.concatenate(
+                    [jnp.where(mine, number.astype(f32), 0.0), jnp.where(mine, within.astype(f32), 0.0)], axis=0
+                ).astype(bf16)
+            )
+            rhs.append(one_hot(place % WIDE, high_id))
+        total = total + dot_nt(jnp.concatenate(lhs, axis=1), jnp.concatenate(rhs, axis=1))
+    total = total.astype(i32)
+    back_ref[...] = total[:lows] * LANES + total[lows:]
 
 
 def view(angles_ref):
@@ -441,6 +468,11 @@
             for part, value in enumerate(split_two(found[6 + colour])):
                 coef_s[pl.ds(8 * block * 24 + 18 + 3 * part + colour, 8, stride=24), :] = value
 
+    for row in range(0, slot_rows, 2):
+        pick_in(row)
+    for block in range(blocks):
+        quadratics(block)
+
     pixel = iota((24, PIX), 1)
     row = iota((24, PIX), 0)
     pix_x = (pixel % 16).astype(f32) - 7.5
@@ -522,19 +554,7 @@
 
     trans = tuple(jnp.ones((GROUP, PIX), f32) for _ in range(groups))
     images = tuple(jnp.zeros((24, PIX), f32) for _ in range(groups))
-    per_group = chunks // 8
-    for block in range(0, blocks, per_group):
-        for row in range(0, 8, 2):
-            pick_in(8 * block + row)
-        quadratics(block)
     for pair in range(-AHEAD, chunks // 2 + 1):
-        step = pair + AHEAD + 4
-        if 4 <= step < chunks // 2:
-            for group in range(groups):
-                block = group * per_group + step // 4
-                pick_in(8 * block + step % 4 * 2)
-                if step % 4 == 3:
-                    quadratics(block)
         for one in range(2):
             if pair + AHEAD < chunks // 2:
                 evaluate(2 * (pair + AHEAD) + one)
@@ -611,10 +631,7 @@
     minors = layout.minors()
 
     def pick_out(index, _):
-        if layout.halves == 2:
-            slots = back_ref[pl.ds(index, 1), :]
-        else:
-            slots = jnp.concatenate([back_ref[pl.ds(2 * index + one, 1), :] for one in range(2)], axis=1)
+        slots = back_ref[pl.ds(index, 1), :]
 
         def put(channel, value):
             for one in range(2):
@@ -628,33 +645,53 @@
     image_copy.wait()
 
 
+def ready_kernel(camera_frame, angles_ref, dense_ref, asked_ref, hot_ref, mine_ref, slope_ref):
+    rows = dense_ref.shape[0] // 16
+    low_id = narrow(iota((mine_ref.shape[0], LANES), 0))
+    high_id = narrow(iota((WIDE, LANES), 0))
+    for row in range(asked_ref.shape[0]):
+        lanes = slice(row * LANES, (row + 1) * LANES)
+        asked = asked_ref[row : row + 1, :]
+        mine_ref[:, lanes] = one_hot(asked // WIDE, low_id)
+        hot_ref[:, lanes] = one_hot(asked % WIDE, high_id)
+    rotation = view(angles_ref)
+    for start in range(0, rows, 8):
+        columns = [dense_ref[index * rows + start : index * rows + start + 8, :] for index in range(11)]
+
+        def conics(*values):
+            return shape_of(columns[0:3] + list(values) + columns[10:11], rotation, camera_frame)[2:5]
+
+        _, pullback = jax.vjp(conics, *columns[3:10])
+        for one in range(3):
+            unit = tuple(jnp.full((8, LANES), 1.0 if one == other else 0.0, f32) for other in range(3))
+            for index, slope in enumerate(pullback(unit)):
+                at = (7 * one + index) * rows + start
+                slope_ref[at : at + 8, :] = slope
+        _, pullback = jax.vjp(lambda value: 1.0 / (1.0 + jnp.exp(-value)), columns[10])
+        slope_ref[21 * rows + start : 21 * rows + start + 8, :] = pullback(jnp.ones((8, LANES), f32))[0]
+
+
 def collect_kernel(
-    layout, camera_frame, angles_ref, dense_ref, asked_ref, terms_ref, grad_hbm, lhs_s, rhs_s, total_s, out_s, grad_ref, sems
+    layout, camera_frame, angles_ref, hot_ref, mine_ref, slope_ref, terms_ref, grad_hbm, lhs_s, total_s, out_s, grad_ref, sems
 ):
     gauss = grad_ref.shape[1]
     rows = gauss // LANES
     lows = gauss // WIDE
-    low_id = narrow(iota((lows, LANES), 0))
-    high_id = narrow(iota((WIDE, LANES), 0))
     minors = layout.minors()
-
     for index in range(layout.count // 8):
-        asked = asked_ref[8 * index : 8 * index + 8, :]
-        low = asked // WIDE
-        high = asked % WIDE
-        for row in range(8):
-            lanes = slice((8 * index + row) * LANES, (8 * index + row + 1) * LANES)
-            mine = one_hot(low[row : row + 1], low_id)
-            rhs_s[:, lanes] = one_hot(high[row : row + 1], high_id)
+        for row in range(8 * index, 8 * index + 8):
+            lanes = slice(row * LANES, (row + 1) * LANES)
+            mine = mine_ref[:, lanes]
             for channel in range(PROJ):
-                at = layout.row(channel, (8 * index + row) // minors, row % minors)
+                at = layout.row(channel, row // minors, row % minors)
                 put_terms(lhs_s, channel, lanes, terms_ref[at : at + 1, :], mine)
         if index % 2 == 1:
             lanes = slice(8 * (index - 1) * LANES, 8 * (index + 1) * LANES)
-            found = dot_nt(lhs_s[:, lanes], rhs_s[:, lanes])
+            found = dot_nt(lhs_s[:, lanes], hot_ref[:, lanes])
             total_s[...] = found if index == 1 else total_s[...] + found
     rotation = view(angles_ref)
     basis = harmonics(*rotation[2])
+    focal_x, focal_y, _, _ = camera_frame
     for part in range(rows // 8):
         half = part % 2
         low = part // 2 * 8
@@ -664,10 +701,11 @@
             + total_s[(PROJ + channel) * lows + low : (PROJ + channel) * lows + low + 8, lanes]
             for channel in range(PROJ)
         ]
-        columns = tuple(dense_ref[pl.ds(index * rows + 2 * low + half, 8, stride=2), :] for index in range(11))
-        _, pullback = jax.vjp(lambda *values: shape_of(values, rotation, camera_frame), *columns)
-        grads = pullback(tuple(sums[:6]))
-        for index, value in enumerate(tuple(grads) + tuple(sums[6:])):
+        slope = [slope_ref[pl.ds(index * rows + 2 * low + half, 8, stride=2), :] for index in range(22)]
+        grads = [focal_x * rotation[0][k] * sums[0] + focal_y * rotation[1][k] * sums[1] for k in range(3)]
+        grads += [slope[k] * sums[2] + slope[7 + k] * sums[3] + slope[14 + k] * sums[4] for k in range(7)]
+        grads += [slope[21] * sums[5]]
+        for index, value in enumerate(grads + sums[6:]):
             out_s[pl.ds(index * rows + 2 * low + half, 8, stride=2), :] = value
     sub = iota((8, LANES), 0)
     patterns = [basis_rows(basis, eighth) for eighth in range(8)]
@@ -727,12 +765,24 @@
     return call(
         partial(route_kernel, devices, per_owner),
         [HBM, HBM],
-        [(asked, i32), ((devices, per_owner), i32), ((rows, LANES), i32)],
+        [(asked, i32), ((rows, LANES), i32)],
         [(owners.shape, i32)] * 2 + [((rows, LANES), i32)] * 3 + [pltpu.SemaphoreType.DMA((2,))],
         1 << 30,
         "route",
         vmem=63 << 20,
     )(owners, locals_)
+
+
+def order(tiles, place):
+    rows = place.shape[0]
+    return call(
+        partial(order_kernel, tiles),
+        [VMEM],
+        [((rows, LANES), i32), ((rows // 2, WIDE), i32)],
+        [],
+        1 << 30,
+        "order",
+    )(place)
 
 
 def shade(camera_frame, view_angles, gaussians):
@@ -787,16 +837,29 @@
     )(list_counts, tile_order, rows, pos, back, cotangent)
 
 
-def collect(layout, camera_frame, view_angles, shape, dense, asked, terms):
+def ready(camera_frame, view_angles, dense, asked):
+    rows = dense.shape[0] // 16
+    slots = asked.size
+    return call(
+        partial(ready_kernel, camera_frame),
+        [SMEM, VMEM, VMEM],
+        [((WIDE, slots), bf16), ((rows // 2, slots), bf16), ((22 * rows, LANES), f32)],
+        [],
+        1 << 30,
+        "ready",
+        vmem=24 << 20,
+    )(view_angles, dense, asked)
+
+
+def collect(layout, camera_frame, view_angles, shape, prepared, terms):
     rows = shape[1] // LANES
     lows = shape[1] // WIDE
     return call(
         partial(collect_kernel, layout, camera_frame),
-        [SMEM, VMEM, VMEM, VMEM],
+        [SMEM, VMEM, VMEM, VMEM, VMEM],
         [(shape, f32)],
         [
             ((2 * PROJ * lows, layout.count * LANES), bf16),
-            ((WIDE, layout.count * LANES), bf16),
             ((2 * PROJ * lows, WIDE), f32),
             ((16 * rows, LANES), f32),
             (shape, f32),
@@ -805,7 +868,8 @@
         1 << 32,
         "collect",
         out_spec=HBM,
-    )(view_angles, dense, asked, terms)[0]
+        vmem=32 << 20,
+    )(view_angles, *prepared, terms)[0]
 
 
 def swap_rows(layout, devices, rows):
@@ -821,17 +885,19 @@
     tiles_y = devices * tile_order.shape[0] // TX
     camera_frame = (4.0 * TX, 4.0 * tiles_y, 8.0 * TX, 8.0 * tiles_y)
     layout = Rows(devices, tile_owners.size // devices)
-    want, back, pos = route(devices, tile_owners, tile_locals)
+    want, place = route(devices, tile_owners, tile_locals)
     asked = lax.all_to_all(want, "dev", split_axis=0, concat_axis=0, tiled=True)
     table, dense = shade(camera_frame, view_angles, gaussians)
     if not layout.halves:
         asked = asked.reshape(layout.count, LANES)
-    if layout.halves != 2:
-        back = back.reshape(layout.count, LANES)
-    arrived = swap_rows(layout, devices, pick(layout, table, asked))
+    picked, place = lax.optimization_barrier((pick(layout, table, asked), place))
+    arrived = swap_rows(layout, devices, picked)
+    pos, back = order(tile_owners.shape[0], place)
     rendered, slot_grads = render(layout, list_counts, tile_order, arrived, pos, back, image_cotangent)
+    slot_grads, asked = lax.optimization_barrier((slot_grads, asked))
     terms = swap_rows(layout, devices, slot_grads)
-    gradients = collect(layout, camera_frame, view_angles, gaussians.shape, dense, asked, terms)
+    prepared = ready(camera_frame, view_angles, dense, asked)
+    gradients = collect(layout, camera_frame, view_angles, gaussians.shape, prepared, terms)
     return (rendered, gradients)
 
 

time: 70.7 us -> 75 us (1.061)
  blocking collectives: 26.5 us -> 0 us
  waiting for transfers between devices: 4.14 us -> 20.5 us
  starting transfers between devices: 7.3 us -> 12.7 us
  Pallas kernels: 31.5 us -> 36.3 us
  local copies, waits for them, and re-layouts: 0.02 us -> 4.17 us
    all_to_all x2 -> x0, blocking collectives: 26.5 us -> none  [swap_rows(): lax.all_to_all(apart, 'dev', split_axis=0, concat_axis=0, tiled=True)]
    all_to_all x0 -> x2, waiting for transfers between devices: none -> 16.3 us  [swap_rows(): lax.all_to_all(apart, 'dev', split_axis=0, concat_axis=0, tiled=True)]
    all_to_all x0 -> x2, starting transfers between devices: none -> 5.37 us  [swap_rows(): lax.all_to_all(apart, 'dev', split_axis=0, concat_axis=0, tiled=True)]
    pallas_call x0 -> x2, Pallas kernels: none -> 4.27 us  [the longest x1 2.86 us: ready(): call(partial(ready_kernel, camera_frame), [SMEM, VMEM, VMEM], [((WIDE, sl...]
    unnamed x12 -> x14, local copies, waits for them, and re-layouts: 0.02 us -> 4.17 us
    pallas_call x1, Pallas kernels: 6.05 us -> 5.13 us  [collect(): call(partial(collect_kernel, layout, camera_frame), [SMEM, VMEM, VMEM, VM...]
    pallas_call x1, Pallas kernels: 15.1 us -> 16 us  [render(): call(partial(render_kernel, layout), [SMEM, SMEM, VMEM, VMEM, VMEM, VMEM]...]
  transfers between devices with their start and end apart: 1 -> 3, of which waited for: 1 -> 3; matrix products, arithmetic and copies ran while one was open for 0% -> 0% of each run, Pallas kernels for 4% -> 10%
where the time goes in v11:
time: 75 us; the launch traced here: 74.6 us
  Pallas kernels  36.3 us (48%)
  waiting for transfers between devices  20.5 us (27%)
  starting transfers between devices  12.7 us (17%)
  local copies, waits for them, and re-layouts  4.17 us (6%)
  between operations  0.93 us (1%)
    all_to_all x2, waiting for transfers between devices, swap_rows(): lax.all_to_all(apart, 'dev', split_axis=0, concat_axis=0, tiled=True)  16.3 us
    pallas_call x1, Pallas kernels, render(): call(partial(render_kernel, layout), [SMEM, SMEM, VMEM, VMEM, VMEM, VMEM]...  16 us
    all_to_all x1, starting transfers between devices, shards(): asked = lax.all_to_all(want, 'dev', split_axis=0, concat_axis=0, tiled=True)  7.3 us
    all_to_all x2, starting transfers between devices, swap_rows(): lax.all_to_all(apart, 'dev', split_axis=0, concat_axis=0, tiled=True)  5.37 us
    pallas_call x1, Pallas kernels, collect(): call(partial(collect_kernel, layout, camera_frame), [SMEM, VMEM, VMEM, VM...  5.13 us
    unnamed x14, local copies, waits for them, and re-layouts  4.17 us
    all_to_all x1, waiting for transfers between devices, shards(): asked = lax.all_to_all(want, 'dev', split_axis=0, concat_axis=0, tiled=True)  4.14 us
    pallas_call x1, Pallas kernels, pick(): call(partial(pick_kernel, layout), [VMEM, VMEM], [((PROJ * layout.count,...  4.07 us
  transfers between devices with their start and end apart: 3, of which 3 were waited for; matrix products, arithmetic and copies ran while one was open for 0% of the time, Pallas kernels for 10%

profile of v11, /device:TPU:0, one launch (start us, length us, event | category | flops | bytes accessed | tf_op | source)
XLA Modules:
  0.0 74.6 jit_solution(10383912675092144390)
XLA Ops:
  0.6 0.0 copy-start.3
  0.6 3.8 %route.1 = (s32[64,128]{1,0:T(8,128)}, s32[64,128]{1,0:T(8,128)}) custom-call(s32[16,512]{1,0:T(8,128)} %own_hbm.1, s32[16,512]{1,0:T(8,128)} %loc_hbm.1), custom_call_target="tpu_custom_call" | custom-call | flops 1073741824 | bytes 4194304 | tf_op jit(solution)/shard_map/route/pallas_call | solution.py:765
  4.5 7.3 %all-to-all-start = ((s32[32,2,128]{2,1,0:T(2,128)}), s32[32,2,128]{2,1,0:T(2,128)S(1)}, u32[]{:S(2)}, u32[]{:S(2)}) async-start(s32[32,2,128]{2,1,0:T(2,128)} %bitcast.10), calls=%async_computation | async-start | bytes 65536 | tf_op jit(solution)/shard_map/all_to_all | solution.py:889
  11.8 0.0 copy-done.3
  11.8 3.1 %shade.1 = (bf16[736,256]{1,0:T(8,128)(2,1)S(1)}, f32[1024,128]{1,0:T(8,128)S(1)}) custom-call(f32[3]{0:T(128)S(1)} %copy-done.3, f32[59,8192]{1,0:T(8,128)} %gauss_ref.1), custom_call_target="tpu_custom_call" | custom-call | flops 1073741824 | bytes 4194304 | tf_op jit(solution)/shard_map/shade/pallas_call | solution.py:790
  14.9 4.1 %all-to-all-done = s32[32,2,128]{2,1,0:T(2,128)S(1)} async-done(((s32[32,2,128]{2,1,0:T(2,128)}), s32[32,2,128]{2,1,0:T(2,128)S(1)}, u32[]{:S(2)}, u32[]{:S(2)}) %all-to-all-start) | async-done | bytes 32800 | tf_op jit(solution)/shard_map/all_to_all | solution.py:889
  19.0 0.0 copy-start.6
  19.0 4.1 %pick.1 = f32[576,128]{1,0:T(8,128)} custom-call(bf16[736,256]{1,0:T(8,128)(2,1)S(1)} %get-tuple-element.17.parts_ref, s32[64,128]{1,0:T(8,128)S(1)} %bitcast.8), custom_call_target="tpu_custom_call" | custom-call | flops 1073741824 | bytes 4194304 | tf_op jit(solution)/shard_map/pick/pallas_call | solution.py:801
  23.1 2.8 %all-to-all-start.1 = ((f32[288,2,128]{2,1,0:T(2,128)}), f32[288,2,128]{2,1,0:T(2,128)S(1)}, u32[]{:S(2)}, u32[]{:S(2)}) async-start(f32[288,2,128]{2,1,0:T(2,128)} %bitcast.2), calls=%async_computation.1 | async-start | bytes 589824 | tf_op jit(solution)/shard_map/all_to_all | solution.py:878
  25.9 0.0 copy-done.6
  25.9 0.0 copy-start
  25.9 0.0 copy-start.1
  25.9 0.0 copy-start.2
  25.9 1.4 %order.1 = (s32[64,128]{1,0:T(8,128)S(1)}, s32[32,256]{1,0:T(8,128)S(1)}) custom-call(s32[64,128]{1,0:T(8,128)S(1)} %copy-done.6), custom_call_target="tpu_custom_call" | custom-call | flops 1073741824 | bytes 4194304 | tf_op jit(solution)/shard_map/order/pallas_call | solution.py:778
  27.3 9.8 %all-to-all-done.1 = f32[288,2,128]{2,1,0:T(2,128)S(1)} async-done(((f32[288,2,128]{2,1,0:T(2,128)}), f32[288,2,128]{2,1,0:T(2,128)S(1)}, u32[]{:S(2)}, u32[]{:S(2)}) %all-to-all-start.1) | async-done | bytes 294944 | tf_op jit(solution)/shard_map/all_to_all | solution.py:878
  37.1 0.0 copy-done
  37.1 0.0 copy-done.1
  37.1 0.0 copy-done.2
  37.1 16.0 %render.1 = (f32[3,4096]{1,0:T(4,128)}, f32[576,128]{1,0:T(8,128)}) custom-call(s32[16]{0:T(128)S(1)} %copy-done.1, s32[16]{0:T(128)S(1)} %copy-done.2, f32[576,128]{1,0:T(8,128)S(1)} %bitcast.7, s32[64,128]{1,0:T(8,128)S(1)} %get-tuple-element.22.pos_ref, s32[32,256]{1,0:T(8,128)S(1)} %get-tuple-element.23.back_ref, f32[3,4096]{1,0:T(4,128)S(1)} %copy-done), custom_call_target="tpu_custom_call" | custom-call | flops 17179869184 | bytes 4194304 | tf_op jit(solution)/shard_map/render/pallas_call | solution.py:815
  53.1 2.6 %all-to-all-start.2 = ((f32[288,2,128]{2,1,0:T(2,128)}), f32[288,2,128]{2,1,0:T(2,128)S(1)}, u32[]{:S(2)}, u32[]{:S(2)}) async-start(f32[288,2,128]{2,1,0:T(2,128)} %bitcast.4), calls=%async_computation.2 | async-start | bytes 589824 | tf_op jit(solution)/shard_map/all_to_all | solution.py:878
  55.7 2.9 %ready.1 = (bf16[256,8192]{1,0:T(8,128)(2,1)S(1)}, bf16[32,8192]{1,0:T(8,128)(2,1)S(1)}, f32[1408,128]{1,0:T(8,128)S(1)}) custom-call(f32[3]{0:T(128)S(1)} %copy-done.3, f32[1024,128]{1,0:T(8,128)S(1)} %get-tuple-element.25.dense_ref, s32[64,128]{1,0:T(8,128)S(1)} %bitcast.9), custom_call_target="tpu_custom_call" | custom-call | flops 1073741824 | bytes 4194304 | tf_op jit(solution)/shard_map/ready/pallas_call | solution.py:843
  58.6 0.0 copy-start.4
  58.6 2.0 %copy-done.4 = bf16[256,8192]{1,0:T(8,128)(2,1)} copy-done((bf16[256,8192]{1,0:T(8,128)(2,1)}, bf16[256,8192]{1,0:T(8,128)(2,1)S(1)}, u32[]{:S(2)}) %copy-start.4) | copy-done | bytes 4194328
  60.5 6.6 %all-to-all-done.2 = f32[288,2,128]{2,1,0:T(2,128)S(1)} async-done(((f32[288,2,128]{2,1,0:T(2,128)}), f32[288,2,128]{2,1,0:T(2,128)S(1)}, u32[]{:S(2)}, u32[]{:S(2)}) %all-to-all-start.2) | async-done | bytes 294944 | tf_op jit(solution)/shard_map/all_to_all | solution.py:878
  67.1 0.0 copy-start.5
  67.1 2.2 %copy-done.5 = bf16[256,8192]{1,0:T(8,128)(2,1)S(1)} copy-done((bf16[256,8192]{1,0:T(8,128)(2,1)S(1)}, bf16[256,8192]{1,0:T(8,128)(2,1)}, u32[]{:S(2)}) %copy-start.5) | copy-done | bytes 4194328
  69.3 5.1 %collect.1 = f32[59,8192]{1,0:T(8,128)} custom-call(f32[3]{0:T(128)S(1)} %copy-done.3, bf16[256,8192]{1,0:T(8,128)(2,1)S(1)} %copy-done.5, bf16[32,8192]{1,0:T(8,128)(2,1)S(1)} %get-tuple-element.29.mine_ref, f32[1408,128]{1,0:T(8,128)S(1)} %get-tuple-element.30.slope_ref, f32[576,128]{1,0:T(8,128)S(1)} %bitcast.6), custom_call_target="tpu_custom_call" | custom-call | flops 4294967296 | bytes 4194304 | tf_op jit(solution)/shard_map/collect/pallas_call | solution.py:857
Async XLA Ops:
  0.6 11.1 %copy-start.3 = (f32[3]{0:T(128)S(1)}, f32[3]{0:T(128)}, u32[]{:S(2)}) copy-start(f32[3]{0:T(128)} %angles_ref.5) | copy-start | bytes 40
  4.5 14.6 %all-to-all-start = ((s32[32,2,128]{2,1,0:T(2,128)}), s32[32,2,128]{2,1,0:T(2,128)S(1)}, u32[]{:S(2)}, u32[]{:S(2)}) async-start(s32[32,2,128]{2,1,0:T(2,128)} %bitcast.10), calls=%async_computation | async-start | bytes 65536 | tf_op jit(solution)/shard_map/all_to_all | solution.py:889
  19.0 6.8 %copy-start.6 = (s32[64,128]{1,0:T(8,128)S(1)}, s32[64,128]{1,0:T(8,128)}, u32[]{:S(2)}) copy-start(s32[64,128]{1,0:T(8,128)} %get-tuple-element.21.place_ref) | copy-start | bytes 98308
  23.1 14.0 %all-to-all-start.1 = ((f32[288,2,128]{2,1,0:T(2,128)}), f32[288,2,128]{2,1,0:T(2,128)S(1)}, u32[]{:S(2)}, u32[]{:S(2)}) async-start(f32[288,2,128]{2,1,0:T(2,128)} %bitcast.2), calls=%async_computation.1 | async-start | bytes 589824 | tf_op jit(solution)/shard_map/all_to_all | solution.py:878
  25.9 11.2 %copy-start = (f32[3,4096]{1,0:T(4,128)S(1)}, f32[3,4096]{1,0:T(4,128)}, u32[]{:S(2)}) copy-start(f32[3,4096]{1,0:T(4,128)} %cot_ref.1) | copy-start | bytes 147460
  25.9 11.2 %copy-start.1 = (s32[16]{0:T(128)S(1)}, s32[16]{0:T(128)}, u32[]{:S(2)}) copy-start(s32[16]{0:T(128)} %count_ref.1) | copy-start | bytes 196
  25.9 11.2 %copy-start.2 = (s32[16]{0:T(128)S(1)}, s32[16]{0:T(128)}, u32[]{:S(2)}) copy-start(s32[16]{0:T(128)} %order_ref.1) | copy-start | bytes 196
  53.1 14.0 %all-to-all-start.2 = ((f32[288,2,128]{2,1,0:T(2,128)}), f32[288,2,128]{2,1,0:T(2,128)S(1)}, u32[]{:S(2)}, u32[]{:S(2)}) async-start(f32[288,2,128]{2,1,0:T(2,128)} %bitcast.4), calls=%async_computation.2 | async-start | bytes 589824 | tf_op jit(solution)/shard_map/all_to_all | solution.py:878
  58.6 2.0 %copy-start.4 = (bf16[256,8192]{1,0:T(8,128)(2,1)}, bf16[256,8192]{1,0:T(8,128)(2,1)S(1)}, u32[]{:S(2)}) copy-start(bf16[256,8192]{1,0:T(8,128)(2,1)S(1)} %get-tuple-element.28.hot_ref) | copy-start | bytes 12582916
  67.1 2.2 %copy-start.5 = (bf16[256,8192]{1,0:T(8,128)(2,1)S(1)}, bf16[256,8192]{1,0:T(8,128)(2,1)}, u32[]{:S(2)}) copy-start(bf16[256,8192]{1,0:T(8,128)(2,1)} %copy-done.4) | copy-start | bytes 12582916

commit v12 on v7

--- a/solution.py
+++ b/solution.py
@@ -85,6 +85,17 @@
 
 def one_hot(ids, every):
     return jnp.where(narrow(ids) == every, jnp.ones((), bf16), jnp.zeros((), bf16))
+
+
+def put_terms(lhs_s, channel, lanes, row, mine):
+    lows = mine.shape[0]
+    row = jnp.broadcast_to(row, (16, LANES))
+    first = row.astype(bf16)
+    second = (row - first.astype(f32)).astype(bf16)
+    for part, value in enumerate((first, second)):
+        for low in range(0, lows, 16):
+            start = (part * PROJ + channel) * lows + low
+            lhs_s[start : start + 16, lanes] = mine[low : low + 16] * value
 
 
 def pick_slots(parts, slots, low_id, high_id, put):
@@ -176,7 +187,7 @@
             rhs.append(one_hot(rank_rows[row : row + 1], rank_id))
         return total + dot_nt(jnp.concatenate(lhs, axis=1), jnp.concatenate(rhs, axis=1))
 
-    total = lax.fori_loop(0, rows // 8, place, jnp.zeros((4 * devices, per_owner), f32), unroll=True).astype(i32)
+    total = lax.fori_loop(0, rows // 8, place, jnp.zeros((4 * devices, per_owner), f32), unroll=devices <= 32).astype(i32)
     want = total[:devices] * LANES + total[devices : 2 * devices]
     halves = per_owner // LANES
     if per_owner % LANES == 0 and halves > 1:
@@ -624,9 +635,7 @@
             rhs_s[:, lanes] = one_hot(high[row : row + 1], high_id)
             for channel in range(PROJ):
                 at = layout.row(channel, (8 * index + row) // minors, row % minors)
-                for part, value in enumerate(split_two(terms_ref[at : at + 1, :])):
-                    first = (part * PROJ + channel) * lows
-                    lhs_s[first : first + lows, lanes] = mine * value.astype(bf16)
+                put_terms(lhs_s, channel, lanes, terms_ref[at : at + 1, :], mine)
         lanes = slice(8 * index * LANES, 8 * (index + 1) * LANES)
         found = dot_nt(lhs_s[:, lanes], rhs_s[:, lanes])
         total_s[...] = found if index == 0 else total_s[...] + found

time: 71.3 us -> 70.4 us (0.987)
  Pallas kernels: 32.1 us -> 31.2 us
    pallas_call x1, Pallas kernels: 6.95 us -> 6.05 us  [collect(): call(partial(collect_kernel, layout, camera_frame), [SMEM, VMEM, VMEM, VM...]
where the time goes in v12:
time: 70.4 us; the launch traced here: 70.1 us
  Pallas kernels  31.2 us (44%)
  blocking collectives  26.5 us (38%)
  starting transfers between devices  7.3 us (10%)
  waiting for transfers between devices  4.14 us (6%)
  between operations  0.9 us (1%)
    all_to_all x2, blocking collectives, swap_rows(): lax.all_to_all(apart, 'dev', split_axis=0, concat_axis=0, tiled=True)  26.5 us
    pallas_call x1, Pallas kernels, render(): call(partial(render_kernel, layout), [SMEM, SMEM, VMEM, VMEM, VMEM, VMEM]...  14.8 us
    all_to_all x1, starting transfers between devices, shards(): asked = lax.all_to_all(want, 'dev', split_axis=0, concat_axis=0, tiled=True)  7.3 us
    pallas_call x1, Pallas kernels, collect(): call(partial(collect_kernel, layout, camera_frame), [SMEM, VMEM, VMEM, VM...  6.05 us
    all_to_all x1, waiting for transfers between devices, shards(): asked = lax.all_to_all(want, 'dev', split_axis=0, concat_axis=0, tiled=True)  4.14 us
    pallas_call x1, Pallas kernels, route(): call(partial(route_kernel, devices, per_owner), [HBM, HBM], [(asked, i32)...  3.98 us
    pallas_call x1, Pallas kernels, pick(): call(partial(pick_kernel, layout), [VMEM, VMEM], [((PROJ * layout.count,...  3.33 us
    pallas_call x1, Pallas kernels, shade(): call(partial(shade_kernel, camera_frame), [SMEM, VMEM], [((sum(PARTS) * r...  3.09 us
  transfers between devices with their start and end apart: 1, of which 1 were waited for; matrix products, arithmetic and copies ran while one was open for 0% of the time, Pallas kernels for 4%

profile of v12, /device:TPU:0, one launch (start us, length us, event | category | flops | bytes accessed | tf_op | source)
XLA Modules:
  0.0 70.1 jit_solution(2637259522713406084)
XLA Ops:
  0.6 0.0 copy-start.3
  0.6 4.0 %route.1 = (s32[64,128]{1,0:T(8,128)}, s32[32,256]{1,0:T(8,128)}, s32[64,128]{1,0:T(8,128)}) custom-call(s32[16,512]{1,0:T(8,128)} %own_hbm.1, s32[16,512]{1,0:T(8,128)} %loc_hbm.1), custom_call_target="tpu_custom_call" | custom-call | flops 1073741824 | bytes 4194304 | tf_op jit(solution)/shard_map/route/pallas_call | solution.py:713
  4.6 7.3 %all-to-all-start = ((s32[32,2,128]{2,1,0:T(2,128)}), s32[32,2,128]{2,1,0:T(2,128)S(1)}, u32[]{:S(2)}, u32[]{:S(2)}) async-start(s32[32,2,128]{2,1,0:T(2,128)} %bitcast.12), calls=%async_computation | async-start | bytes 65536 | tf_op jit(solution)/shard_map/all_to_all | solution.py:808
  11.9 0.0 copy-done.3
  11.9 3.1 %shade.1 = (bf16[736,256]{1,0:T(8,128)(2,1)S(1)}, f32[1024,128]{1,0:T(8,128)S(1)}) custom-call(f32[3]{0:T(128)S(1)} %copy-done.3, f32[59,8192]{1,0:T(8,128)} %gauss_ref.1), custom_call_target="tpu_custom_call" | custom-call | flops 1073741824 | bytes 4194304 | tf_op jit(solution)/shard_map/shade/pallas_call | solution.py:726
  15.0 4.1 %all-to-all-done = s32[32,2,128]{2,1,0:T(2,128)S(1)} async-done(((s32[32,2,128]{2,1,0:T(2,128)}), s32[32,2,128]{2,1,0:T(2,128)S(1)}, u32[]{:S(2)}, u32[]{:S(2)}) %all-to-all-start) | async-done | bytes 32800 | tf_op jit(solution)/shard_map/all_to_all | solution.py:808
  19.2 0.0 copy-start
  19.2 0.0 copy-start.1
  19.2 0.0 copy-start.2
  19.2 0.0 copy-start.4
  19.2 0.0 copy-start.5
  19.2 3.3 %pick.1 = f32[576,128]{1,0:T(8,128)S(1)} custom-call(bf16[736,256]{1,0:T(8,128)(2,1)S(1)} %get-tuple-element.9.parts_ref, s32[64,128]{1,0:T(8,128)S(1)} %bitcast.10), custom_call_target="tpu_custom_call" | custom-call | flops 1073741824 | bytes 4194304 | tf_op jit(solution)/shard_map/pick/pallas_call | solution.py:737
  22.5 13.1 %all_to_all.21 = f32[288,2,128]{2,1,0:T(2,128)S(1)} all-to-all(f32[288,2,128]{2,1,0:T(2,128)S(1)} %bitcast.9), channel_id=1, replica_groups=mesh['dev'=32] {'dev'}, dimensions={0} | all-to-all | bytes 589824 | tf_op jit(solution)/shard_map/all_to_all | solution.py:797
  35.7 0.0 copy-done
  35.7 0.0 copy-done.1
  35.7 0.0 copy-done.2
  35.7 0.0 copy-done.4
  35.7 0.0 copy-done.5
  35.7 14.8 %render.1 = (f32[3,4096]{1,0:T(4,128)}, f32[576,128]{1,0:T(8,128)S(1)}) custom-call(s32[16]{0:T(128)S(1)} %copy-done.1, s32[16]{0:T(128)S(1)} %copy-done.2, f32[576,128]{1,0:T(8,128)S(1)} %bitcast.6, s32[64,128]{1,0:T(8,128)S(1)} %copy-done.5, s32[32,256]{1,0:T(8,128)S(1)} %copy-done.4, f32[3,4096]{1,0:T(4,128)S(1)} %copy-done), custom_call_target="tpu_custom_call" | custom-call | flops 17179869184 | bytes 4194304 | tf_op jit(solution)/shard_map/render/pallas_call | solution.py:751
  50.5 13.4 %all_to_all.22 = f32[288,2,128]{2,1,0:T(2,128)S(1)} all-to-all(f32[288,2,128]{2,1,0:T(2,128)S(1)} %bitcast.7), channel_id=1, replica_groups=mesh['dev'=32] {'dev'}, dimensions={0} | all-to-all | bytes 589824 | tf_op jit(solution)/shard_map/all_to_all | solution.py:797
  63.9 6.0 %collect.1 = f32[59,8192]{1,0:T(8,128)} custom-call(f32[3]{0:T(128)S(1)} %copy-done.3, f32[1024,128]{1,0:T(8,128)S(1)} %get-tuple-element.14.dense_ref, s32[64,128]{1,0:T(8,128)S(1)} %bitcast.11, f32[576,128]{1,0:T(8,128)S(1)} %bitcast.8), custom_call_target="tpu_custom_call" | custom-call | flops 4294967296 | bytes 4194304 | tf_op jit(solution)/shard_map/collect/pallas_call | solution.py:776
Async XLA Ops:
  0.6 11.3 %copy-start.3 = (f32[3]{0:T(128)S(1)}, f32[3]{0:T(128)}, u32[]{:S(2)}) copy-start(f32[3]{0:T(128)} %angles_ref.3) | copy-start | bytes 40
  4.6 14.6 %all-to-all-start = ((s32[32,2,128]{2,1,0:T(2,128)}), s32[32,2,128]{2,1,0:T(2,128)S(1)}, u32[]{:S(2)}, u32[]{:S(2)}) async-start(s32[32,2,128]{2,1,0:T(2,128)} %bitcast.12), calls=%async_computation | async-start | bytes 65536 | tf_op jit(solution)/shard_map/all_to_all | solution.py:808
  19.2 16.5 %copy-start = (f32[3,4096]{1,0:T(4,128)S(1)}, f32[3,4096]{1,0:T(4,128)}, u32[]{:S(2)}) copy-start(f32[3,4096]{1,0:T(4,128)} %cot_ref.1) | copy-start | bytes 147460
  19.2 16.5 %copy-start.1 = (s32[16]{0:T(128)S(1)}, s32[16]{0:T(128)}, u32[]{:S(2)}) copy-start(s32[16]{0:T(128)} %count_ref.1) | copy-start | bytes 196
  19.2 16.5 %copy-start.2 = (s32[16]{0:T(128)S(1)}, s32[16]{0:T(128)}, u32[]{:S(2)}) copy-start(s32[16]{0:T(128)} %order_ref.1) | copy-start | bytes 196
  19.2 16.5 %copy-start.4 = (s32[32,256]{1,0:T(8,128)S(1)}, s32[32,256]{1,0:T(8,128)}, u32[]{:S(2)}) copy-start(s32[32,256]{1,0:T(8,128)} %get-tuple-element.12.back_ref) | copy-start | bytes 98308
  19.2 16.5 %copy-start.5 = (s32[64,128]{1,0:T(8,128)S(1)}, s32[64,128]{1,0:T(8,128)}, u32[]{:S(2)}) copy-start(s32[64,128]{1,0:T(8,128)} %get-tuple-element.11.pos_ref) | copy-start | bytes 98308
